TPU v7x, 32 devices: a whole 2x2x4 slice. The times are simulated.
32 devices in a mesh: clip: 4 (over y, x), sp: 8 (over z, core).
Axes of the slice: x: 2, y: 2, z: 4, core: 2. Of those that a mesh axis runs over, the one named last changes fastest.
Arguments:
- tokens: bfloat16 [4, 16, 2048, 384], P('clip', None, 'sp'), may hold values from -6 to 6
- conditioning: bfloat16 [4, 384], P('clip'), may hold values from -6 to 6
- timesteps: int32 [4], P('clip'), may hold values from 0 to 999, as said below
- out_grad: bfloat16 [4, 16, 2048, 384], P('clip', None, 'sp'), may hold values from -6 to 6
- ada_weight: bfloat16 [384, 3456], replicated, may hold values from -0.4375 to 0.4375
- ada_bias: float32 [3456], replicated, may hold values from -3 to 3
- spatial_proj: bfloat16 [384, 1152], replicated, may hold values from -0.3125 to 0.3125
- spatial_bias: float32 [768], replicated, may hold values from -3 to 3
- spatial_out: bfloat16 [384, 384], replicated, may hold values from -6 to 6
- spatial_out_bias: float32 [384], replicated, may hold values from -2 to 2
- temporal_proj: bfloat16 [384, 1152], replicated, may hold values from -0.3125 to 0.3125
- temporal_bias: float32 [768], replicated, may hold values from -3 to 3
- temporal_out: bfloat16 [384, 384], replicated, may hold values from -0.75 to 0.75
- temporal_out_bias: float32 [384], replicated, may hold values from -2 to 2
- hidden_in: bfloat16 [384, 1536], replicated, may hold values from -0.3125 to 0.3125
- hidden_in_bias: float32 [1536], replicated, may hold values from -3 to 3
- hidden_out: bfloat16 [1536, 384], replicated, may hold values from -0.15625 to 0.15625
- hidden_out_bias: float32 [384], replicated, may hold values from -2 to 2
Outputs:
- block_out: bfloat16 [4, 16, 2048, 384], P('clip', None, 'sp')
- input_grad: bfloat16 [4, 16, 2048, 384], P('clip', None, 'sp')
- grad_ada_weight: float32 [384, 3456], replicated
- grad_ada_bias: float32 [3456], replicated
- grad_spatial_proj: float32 [384, 1152], replicated
- grad_spatial_bias: float32 [768], replicated
- grad_spatial_out: float32 [384, 384], replicated
- grad_spatial_out_bias: float32 [384], replicated
- grad_temporal_proj: float32 [384, 1152], replicated
- grad_temporal_bias: float32 [768], replicated
- grad_temporal_out: float32 [384, 384], replicated
- grad_temporal_out_bias: float32 [384], replicated
- grad_hidden_in: float32 [384, 1536], replicated
- grad_hidden_in_bias: float32 [1536], replicated
- grad_hidden_out: float32 [1536, 384], replicated
- grad_hidden_out_bias: float32 [384], replicated
Inputs may be any that keep to these rules, and one draw needn't show every extreme that they name: One diffusion timestep a clip; later timesteps are more common, and some clip has the last one, 999.
All inputs are finite; a program needn't handle non-finite values.
Results may differ from a plain program's by a relative error of at most 0.025.
The roundings to bfloat16 on the way count: a program that leaves them out, or rounds other values in their place, can miss the bound.
Values may be sent and summed in bfloat16 or wider, within the bound.
A program may use at most 1.125 GiB of HBM per device.

v0:
```python
from functools import partial
import math

import jax
import jax.numpy as jnp
from jax import lax
from jax.sharding import PartitionSpec as P

HEADS = 6
HEAD_DIM = 64
FRAME_BLOCK = 8
TSTEPS = 1000


def modulate(field, shift, scale):
    centred = field - jnp.mean(field, axis=-1, keepdims=True)
    normed = centred * lax.rsqrt(jnp.mean(centred * centred, axis=-1, keepdims=True) + 1e-06)
    return normed * (1.0 + scale) + shift


def loss_weights(timesteps):
    phase = (timesteps.astype(jnp.float32) / TSTEPS + 0.008) / 1.008 * (0.5 * math.pi)
    slope = jnp.tan(phase)
    return jnp.minimum(1.0, 5.0 * slope * slope)


def split_heads(array):
    return array.reshape(array.shape[:-1] + (HEADS, HEAD_DIM))


def join_heads(array):
    return array.reshape(array.shape[:-2] + (HEADS * HEAD_DIM,))


def attend(queries, keys, values):
    scores = jnp.einsum(
        "csqhe,cskhe->cshqk", queries, keys, preferred_element_type=jnp.float32
    ) * HEAD_DIM ** (-0.5)
    row_max = jnp.max(scores, axis=-1, keepdims=True)
    exponent = jnp.exp(scores - row_max)
    total = jnp.sum(exponent, axis=-1, keepdims=True)
    soft_weights = (exponent / total).astype(jnp.bfloat16)
    mixed = jnp.einsum(
        "cshqk,cskhe->csqhe", soft_weights, values, preferred_element_type=jnp.float32
    )
    return (mixed, row_max[..., 0] + jnp.log(total[..., 0]))


def probabilities(queries, keys, values, grads, log_total):
    scores = jnp.einsum(
        "csqhe,cskhe->cshqk", queries, keys, preferred_element_type=jnp.float32
    ) * HEAD_DIM ** (-0.5)
    soft_weights = jnp.exp(scores - log_total[..., None])
    grad_weights = jnp.einsum(
        "csqhe,cskhe->cshqk", grads, values, preferred_element_type=jnp.float32
    )
    return (soft_weights, grad_weights)


def query_pass(queries, keys, values, grads, log_total):
    soft_weights, grad_weights = probabilities(queries, keys, values, grads, log_total)
    delta = jnp.sum(soft_weights * grad_weights, axis=-1)
    grad_scores = (soft_weights * (grad_weights - delta[..., None]) * HEAD_DIM ** (-0.5)).astype(
        jnp.bfloat16
    )
    grad_queries = jnp.einsum(
        "cshqk,cskhe->csqhe", grad_scores, keys, preferred_element_type=jnp.float32
    )
    return (grad_queries, delta)


def key_pass(queries, keys, values, grads, log_total, delta):
    soft_weights, grad_weights = probabilities(queries, keys, values, grads, log_total)
    grad_scores = (soft_weights * (grad_weights - delta[..., None]) * HEAD_DIM ** (-0.5)).astype(
        jnp.bfloat16
    )
    grad_keys = jnp.einsum(
        "cshqk,csqhe->cskhe", grad_scores, queries, preferred_element_type=jnp.float32
    )
    grad_values = jnp.einsum(
        "cshqk,csqhe->cskhe",
        soft_weights.astype(jnp.bfloat16),
        grads,
        preferred_element_type=jnp.float32,
    )
    return jnp.concatenate([join_heads(grad_keys), join_heads(grad_values)], axis=-1)


def column_sums(array):
    return jnp.sum(array.astype(jnp.float32), axis=(0, 1, 2))


def body(
    tokens,
    conditioning,
    timesteps,
    out_grad,
    ada_weight,
    ada_bias,
    spatial_proj,
    spatial_bias,
    spatial_out,
    spatial_out_bias,
    temporal_proj,
    temporal_bias,
    temporal_out,
    temporal_out_bias,
    hidden_in,
    hidden_in_bias,
    hidden_out,
    hidden_out_bias,
):
    clips, frames, stripe, width = tokens.shape
    blocks = frames // FRAME_BLOCK
    scale_factor = HEAD_DIM ** (-0.5)
    field = tokens.astype(jnp.float32)
    cond_act = jax.nn.silu(conditioning.astype(jnp.float32)).astype(jnp.bfloat16)
    modes = jnp.dot(cond_act, ada_weight, preferred_element_type=jnp.float32) + ada_bias
    modes = modes.reshape(clips, 9, 1, 1, width)
    hidden_one, back_one = jax.vjp(modulate, field, modes[:, 0], modes[:, 1])
    hidden_one = hidden_one.astype(jnp.bfloat16)
    query_mix = jnp.einsum(
        "cfpd,de->cfpe", hidden_one, spatial_proj[:, :width], preferred_element_type=jnp.float32
    )
    queries = (query_mix + spatial_bias[:width]).astype(jnp.bfloat16)
    keyval_mix = jnp.einsum(
        "cfpd,de->cfpe", hidden_one, spatial_proj[:, width:], preferred_element_type=jnp.float32
    )
    keyval_bias = jnp.concatenate([jnp.zeros((width,), jnp.float32), spatial_bias[width:]])
    keyvals = (keyval_mix + keyval_bias).astype(jnp.bfloat16)
    query_heads = split_heads(queries)
    mixed_parts = []
    log_parts = []
    for index in range(blocks):
        first = index * FRAME_BLOCK
        whole = lax.all_gather(keyvals[:, first : first + FRAME_BLOCK], "sp", axis=2, tiled=True)
        mixed_part, log_part = attend(
            query_heads[:, first : first + FRAME_BLOCK],
            split_heads(whole[..., :width]),
            split_heads(whole[..., width:]),
        )
        mixed_parts.append(join_heads(mixed_part))
        log_parts.append(log_part)
    attn_one = jnp.concatenate(mixed_parts, axis=1).astype(jnp.bfloat16)
    spatial_log = jnp.concatenate(log_parts, axis=1)
    branch_one = (
        jnp.einsum("cfpd,de->cfpe", attn_one, spatial_out, preferred_element_type=jnp.float32)
        + spatial_out_bias
    )
    field_one = field + modes[:, 2] * branch_one
    hidden_two, back_two = jax.vjp(modulate, field_one, modes[:, 3], modes[:, 4])
    hidden_two = hidden_two.astype(jnp.bfloat16)
    time_mix = jnp.einsum(
        "cfpd,de->cfpe", hidden_two, temporal_proj, preferred_element_type=jnp.float32
    )
    time_queries = split_heads((time_mix[..., :width] + temporal_bias[:width]).astype(jnp.bfloat16))
    time_keys = split_heads(time_mix[..., width : 2 * width].astype(jnp.bfloat16))
    time_values = split_heads(
        (time_mix[..., 2 * width :] + temporal_bias[width:]).astype(jnp.bfloat16)
    )
    time_scores = (
        jnp.einsum(
            "cfphe,cgphe->cphfg", time_queries, time_keys, preferred_element_type=jnp.float32
        )
        * scale_factor
    )
    time_max = jnp.max(time_scores, axis=-1, keepdims=True)
    time_exponent = jnp.exp(time_scores - time_max)
    time_weights = time_exponent / jnp.sum(time_exponent, axis=-1, keepdims=True)
    time_rounded = time_weights.astype(jnp.bfloat16)
    attn_two = join_heads(
        jnp.einsum(
            "cphfg,cgphe->cfphe", time_rounded, time_values, preferred_element_type=jnp.float32
        )
    ).astype(jnp.bfloat16)
    branch_two = (
        jnp.einsum("cfpd,de->cfpe", attn_two, temporal_out, preferred_element_type=jnp.float32)
        + temporal_out_bias
    )
    field_two = field_one + modes[:, 5] * branch_two
    hidden_three, back_three = jax.vjp(modulate, field_two, modes[:, 6], modes[:, 7])
    hidden_three = hidden_three.astype(jnp.bfloat16)
    inner = (
        jnp.einsum("cfpd,dk->cfpk", hidden_three, hidden_in, preferred_element_type=jnp.float32)
        + hidden_in_bias
    )
    active, gelu_back = jax.vjp(partial(jax.nn.gelu, approximate=True), inner)
    active = active.astype(jnp.bfloat16)
    branch_three = (
        jnp.einsum("cfpk,kd->cfpd", active, hidden_out, preferred_element_type=jnp.float32)
        + hidden_out_bias
    )
    block_out = (field_two + modes[:, 8] * branch_three).astype(jnp.bfloat16)
    weights = loss_weights(timesteps)
    grad_field = out_grad.astype(jnp.float32) * weights[:, None, None, None]
    grad_gate_three = jnp.sum(grad_field * branch_three, axis=(1, 2))
    grad_branch = (modes[:, 8] * grad_field).astype(jnp.bfloat16)
    grad_hidden_out = jnp.einsum(
        "cfpk,cfpd->kd", active, grad_branch, preferred_element_type=jnp.float32
    )
    grad_hidden_out_bias = column_sums(grad_branch)
    grad_active = jnp.einsum(
        "cfpd,kd->cfpk", grad_branch, hidden_out, preferred_element_type=jnp.float32
    )
    grad_inner = gelu_back(grad_active)[0].astype(jnp.bfloat16)
    grad_hidden_in = jnp.einsum(
        "cfpd,cfpk->dk", hidden_three, grad_inner, preferred_element_type=jnp.float32
    )
    grad_hidden_in_bias = column_sums(grad_inner)
    grad_hidden = jnp.einsum(
        "cfpk,dk->cfpd", grad_inner, hidden_in, preferred_element_type=jnp.float32
    )
    grad_input, grad_shift_three, grad_scale_three = back_three(grad_hidden)
    grad_field = grad_field + grad_input
    grad_gate_two = jnp.sum(grad_field * branch_two, axis=(1, 2))
    grad_branch = (modes[:, 5] * grad_field).astype(jnp.bfloat16)
    grad_temporal_out = jnp.einsum(
        "cfpd,cfpe->de", attn_two, grad_branch, preferred_element_type=jnp.float32
    )
    grad_temporal_out_bias = column_sums(grad_branch)
    grad_attn = split_heads(
        jnp.einsum(
            "cfpe,de->cfpd", grad_branch, temporal_out, preferred_element_type=jnp.float32
        ).astype(jnp.bfloat16)
    )
    grad_weights = jnp.einsum(
        "cfphe,cgphe->cphfg", grad_attn, time_values, preferred_element_type=jnp.float32
    )
    delta = jnp.sum(time_weights * grad_weights, axis=-1, keepdims=True)
    grad_scores = (time_weights * (grad_weights - delta) * scale_factor).astype(jnp.bfloat16)
    grad_time_queries = jnp.einsum(
        "cphfg,cgphe->cfphe", grad_scores, time_keys, preferred_element_type=jnp.float32
    )
    grad_time_keys = jnp.einsum(
        "cphfg,cfphe->cgphe", grad_scores, time_queries, preferred_element_type=jnp.float32
    )
    grad_time_values = jnp.einsum(
        "cphfg,cfphe->cgphe", time_rounded, grad_attn, preferred_element_type=jnp.float32
    )
    grad_time_mix = jnp.concatenate(
        [join_heads(grad_time_queries), join_heads(grad_time_keys), join_heads(grad_time_values)],
        axis=-1,
    ).astype(jnp.bfloat16)
    grad_temporal_proj = jnp.einsum(
        "cfpd,cfpe->de", hidden_two, grad_time_mix, preferred_element_type=jnp.float32
    )
    grad_temporal_bias = jnp.concatenate(
        [column_sums(grad_time_mix[..., :width]), column_sums(grad_time_mix[..., 2 * width :])]
    )
    grad_hidden = jnp.einsum(
        "cfpe,de->cfpd", grad_time_mix, temporal_proj, preferred_element_type=jnp.float32
    )
    grad_input, grad_shift_two, grad_scale_two = back_two(grad_hidden)
    grad_field = grad_field + grad_input
    grad_gate_one = jnp.sum(grad_field * branch_one, axis=(1, 2))
    grad_branch = (modes[:, 2] * grad_field).astype(jnp.bfloat16)
    grad_spatial_out = jnp.einsum(
        "cfpd,cfpe->de", attn_one, grad_branch, preferred_element_type=jnp.float32
    )
    grad_spatial_out_bias = column_sums(grad_branch)
    grad_attn = jnp.einsum(
        "cfpe,de->cfpd", grad_branch, spatial_out, preferred_element_type=jnp.float32
    ).astype(jnp.bfloat16)
    query_parts = []
    key_parts = []
    for index in range(blocks):
        first = index * FRAME_BLOCK
        whole = lax.all_gather(keyvals[:, first : first + FRAME_BLOCK], "sp", axis=2, tiled=True)
        piece = query_heads[:, first : first + FRAME_BLOCK]
        grad_piece = split_heads(grad_attn[:, first : first + FRAME_BLOCK])
        log_piece = spatial_log[:, first : first + FRAME_BLOCK]
        grad_query_part, delta = query_pass(
            piece,
            split_heads(whole[..., :width]),
            split_heads(whole[..., width:]),
            grad_piece,
            log_piece,
        )
        term = key_pass(
            piece,
            split_heads(whole[..., :width]),
            split_heads(whole[..., width:]),
            grad_piece,
            log_piece,
            delta,
        )
        owned = lax.psum_scatter(
            jnp.transpose(term, (2, 0, 1, 3)).astype(jnp.bfloat16),
            "sp",
            scatter_dimension=0,
            tiled=True,
        ).astype(jnp.float32)
        query_parts.append(join_heads(grad_query_part))
        key_parts.append(jnp.transpose(owned, (1, 2, 0, 3)))
    grad_queries = jnp.concatenate(query_parts, axis=1)
    grad_keyvals = jnp.concatenate(key_parts, axis=1)
    grad_queries = grad_queries.astype(jnp.bfloat16)
    grad_keyvals = grad_keyvals.astype(jnp.bfloat16)
    grad_spatial_proj = jnp.concatenate(
        [
            jnp.einsum(
                "cfpd,cfpe->de", hidden_one, grad_queries, preferred_element_type=jnp.float32
            ),
            jnp.einsum(
                "cfpd,cfpe->de", hidden_one, grad_keyvals, preferred_element_type=jnp.float32
            ),
        ],
        axis=1,
    )
    grad_spatial_bias = jnp.concatenate(
        [column_sums(grad_queries), column_sums(grad_keyvals[..., width:])]
    )
    grad_hidden = jnp.einsum(
        "cfpe,de->cfpd", grad_queries, spatial_proj[:, :width], preferred_element_type=jnp.float32
    )
    grad_hidden = grad_hidden + jnp.einsum(
        "cfpe,de->cfpd", grad_keyvals, spatial_proj[:, width:], preferred_element_type=jnp.float32
    )
    grad_input, grad_shift_one, grad_scale_one = back_one(grad_hidden)
    input_grad = (grad_field + grad_input).astype(jnp.bfloat16)
    grad_modes = jnp.stack(
        [
            grad_shift_one.reshape(clips, width),
            grad_scale_one.reshape(clips, width),
            grad_gate_one,
            grad_shift_two.reshape(clips, width),
            grad_scale_two.reshape(clips, width),
            grad_gate_two,
            grad_shift_three.reshape(clips, width),
            grad_scale_three.reshape(clips, width),
            grad_gate_three,
        ],
        axis=1,
    ).reshape(clips, 9 * width)
    grad_ada_weight = jnp.dot(
        cond_act.astype(jnp.float32).T, grad_modes, precision=lax.Precision.HIGHEST
    )
    grad_ada_bias = jnp.sum(grad_modes, axis=0)
    summed = lax.psum(
        (
            grad_ada_weight,
            grad_ada_bias,
            grad_spatial_proj,
            grad_spatial_bias,
            grad_spatial_out,
            grad_spatial_out_bias,
            grad_temporal_proj,
            grad_temporal_bias,
            grad_temporal_out,
            grad_temporal_out_bias,
            grad_hidden_in,
            grad_hidden_in_bias,
            grad_hidden_out,
            grad_hidden_out_bias,
        ),
        ("clip", "sp"),
    )
    return (
        block_out,
        input_grad,
        summed[0],
        summed[1],
        summed[2],
        summed[3],
        summed[4],
        summed[5],
        summed[6],
        summed[7],
        summed[8],
        summed[9],
        summed[10],
        summed[11],
        summed[12],
        summed[13],
    )


def solution(mesh):
    return jax.shard_map(
        body,
        mesh=mesh,
        in_specs=(
            P("clip", None, "sp", None),
            P("clip", None),
            P("clip"),
            P("clip", None, "sp", None),
            P(),
            P(),
            P(),
            P(),
            P(),
            P(),
            P(),
            P(),
            P(),
            P(),
            P(),
            P(),
            P(),
            P(),
        ),
        out_specs=(
            P("clip", None, "sp", None),
            P("clip", None, "sp", None),
            P(),
            P(),
            P(),
            P(),
            P(),
            P(),
            P(),
            P(),
            P(),
            P(),
            P(),
            P(),
            P(),
            P(),
        ),
        check_vma=False,
    )
```

profile of v0, /device:TPU:0, one launch (start us, length us, event | category | flops | bytes accessed | tf_op | source)
XLA Modules:
  0.0 2278.4 jit_solution(9129803636439604786)
XLA Ops:
  38.0 210.0 %all-gather.3.cloned.1.call-done = bf16[1,8,2048,768]{3,2,1,0:T(8,128)(2,1)} async-done(((bf16[1,8,256,768]{3,2,1,0:T(8,128)(2,1)}), bf16[1,8,2048,768]{3,2,1,0:T(8,128)(2,1)}) %all-gather.3.cloned.1.call-update) | async-done | bytes 25165840 | tf_op jit(solution)/shard_map/all_gather | solution.py:136
  248.1 20.1 fusion.209
  268.2 16.7 copy.76
  284.9 183.4 %all-gather.5.cloned.1.call-done = bf16[1,8,2048,768]{3,2,1,0:T(8,128)(2,1)} async-done(((bf16[1,8,256,768]{3,2,1,0:T(8,128)(2,1)}), bf16[1,8,2048,768]{3,2,1,0:T(8,128)(2,1)}) %all-gather.5.cloned.1.call-update) | async-done | bytes 25165840 | tf_op jit(solution)/shard_map/all_gather | solution.py:136
  468.3 17.3 fusion.210
  517.8 16.7 copy.74
  534.5 39.1 %multiply_reduce_fusion.2 = (f32[8,6,256]{2,1,0:T(8,128)S(1)}, f32[8,6,256,2048]{3,2,1,0:T(8,128)}) fusion(bf16[8,2048,6,64]{1,3,2,0:T(8,128)(2,1)} %bitcast.313, bf16[1,16,256,6,64]{2,4,3,1,0:T(8,128)(2,1)} %bitcast.325), kind=kOutput, calls=%fused_computation.18 | convolution fusion | flops 3271544832 | bytes 114868224 | tf_op jit(solution)/shard_map/csqhe,cskhe->cshqk/dot_general | solution.py:36
  573.6 31.1 %fusion.7 = f32[8,6,256]{2,1,0:T(8,128)S(1)} fusion(f32[8,6,256,2048]{3,2,1,0:T(8,128)} %get-tuple-element.80, f32[8,6,256]{2,1,0:T(8,128)S(1)} %get-tuple-element.79), kind=kLoop, calls=%fused_computation.17 | loop fusion | flops 75485184 | bytes 100761600 | tf_op jit(solution)/shard_map/reduce_sum | solution.py:41
  604.7 37.8 %fusion.126 = bf16[8,6,64,256]{3,2,1,0:T(8,128)(2,1)S(1)} fusion(bf16[8,2048,6,64]{1,3,2,0:T(8,128)(2,1)} %bitcast.315, f32[8,6,256,2048]{3,2,1,0:T(8,128)} %get-tuple-element.80, f32[8,6,256]{2,1,0:T(8,128)S(1)} %fusion.7, f32[8,6,256]{2,1,0:T(8,128)S(1)} %get-tuple-element.79), kind=kOutput, calls=%fused_computation.160 | convolution fusion | flops 3322675200 | bytes 114917376 | tf_op jit(solution)/shard_map/cshqk,cskhe->csqhe/dot_general | solution.py:43
  644.2 39.3 %multiply_reduce_fusion.3 = (f32[8,6,256]{2,1,0:T(8,128)S(1)}, f32[8,6,256,2048]{3,2,1,0:T(8,128)}) fusion(bf16[8,2048,6,64]{1,3,2,0:T(8,128)(2,1)} %bitcast.311, bf16[1,16,256,6,64]{2,4,3,1,0:T(8,128)(2,1)} %bitcast.326), kind=kOutput, calls=%fused_computation.19 | convolution fusion | flops 3271544832 | bytes 114868224 | tf_op jit(solution)/shard_map/csqhe,cskhe->cshqk/dot_general | solution.py:36
  683.5 31.1 %fusion.6 = f32[8,6,256]{2,1,0:T(8,128)S(1)} fusion(f32[8,6,256,2048]{3,2,1,0:T(8,128)} %get-tuple-element.82, f32[8,6,256]{2,1,0:T(8,128)S(1)} %get-tuple-element.81), kind=kLoop, calls=%fused_computation.16 | loop fusion | flops 75485184 | bytes 100761600 | tf_op jit(solution)/shard_map/reduce_sum | solution.py:41
  715.2 39.3 %fusion.127 = bf16[8,6,64,256]{3,2,1,0:T(8,128)(2,1)} fusion(bf16[8,2048,6,64]{1,3,2,0:T(8,128)(2,1)} %bitcast.317, f32[8,6,256,2048]{3,2,1,0:T(8,128)} %get-tuple-element.82, f32[8,6,256]{2,1,0:T(8,128)S(1)} %fusion.6, f32[8,6,256]{2,1,0:T(8,128)S(1)} %get-tuple-element.81), kind=kOutput, calls=%fused_computation.161 | convolution fusion | flops 3322675200 | bytes 114917376 | tf_op jit(solution)/shard_map/cshqk,cskhe->csqhe/dot_general | solution.py:43
  876.4 16.8 multiply_convert_fusion.2
  893.1 28.4 %convert_reduce_fusion = (f32[1536]{0:T(1024)}, bf16[16,256,1536]{2,1,0:T(8,128)(2,1)}) fusion(f32[16,256,1536]{2,1,0:T(8,128)} %get-tuple-element.89, f32[1536]{0:T(1024)S(1)} %copy-done.116, bf16[1536,384]{1,0:T(8,128)(2,1)S(1)} %copy-done.112, f32[]{:T(128)} %bitcast.34, bf16[1,16,256,384]{3,2,1,0:T(8,128)(2,1)S(1)} %copy-done.28, f32[384]{0:T(512)S(1)} %copy-done.102), kind=kOutput, calls=%fused_computation.41 | convolution fusion | flops 4982831616 | bytes 42087940 | tf_op jit(solution)/shard_map/cfpd,kd->cfpk/dot_general | solution.py:202
  970.7 22.3 convert_bitcast_fusion.2
  992.9 23.5 %convert_reduce_fusion.2 = (f32[6,64]{1,0:T(8,128)}, bf16[1,16,256,6,64]{4,1,3,2,0:T(8,128)(2,1)}) fusion(bf16[16,256,6,64]{3,0,2,1:T(8,128)(2,1)} %copy.85, f32[256,6,16,16]{2,3,1,0:T(8,128)} %fusion.220, f32[256,6,16,16]{2,3,1,0:T(8,128)} %get-tuple-element.85, f32[256,6,16]{2,1,0:T(8,128)S(1)} %copy-done.119), kind=kOutput, calls=%fused_computation.45 | convolution fusion | flops 57826960 | bytes 9537024 | tf_op jit(solution)/shard_map/cphfg,cgphe->cfphe/dot_general | solution.py:231
  1083.9 24.4 %convert_reduce_fusion.4 = (f32[384]{0:T(512)}, f32[384]{0:T(512)}, f32[384]{0:T(512)}, f32[384]{0:T(512)}, bf16[1,16,256,384]{3,2,1,0:T(8,128)(2,1)S(1)}, /*ind...) fusion(f32[]{:T(128)} %bitcast.34, bf16[1,16,256,384]{3,2,1,0:T(8,128)(2,1)} %param.21, ...), kind=kOutput, calls=%fused_computation.101 | convolution fusion | flops 4877449216 | bytes 61044228 | tf_op jit(solution)/shard_map/cfpk,kd->cfpd/dot_general | solution.py:190
  1114.2 38.7 %fusion.221 = f32[8,6,256,2048]{3,2,1,0:T(8,128)} fusion(bf16[8,256,6,64]{1,3,2,0:T(8,128)(2,1)S(1)} %bitcast.323, bf16[8,2048,6,64]{1,3,2,0:T(8,128)(2,1)} %bitcast.318), kind=kOutput, calls=%fused_computation.266 | convolution fusion | flops 3221225472 | bytes 114819072 | tf_op jit(solution)/shard_map/csqhe,cskhe->cshqk/dot_general | solution.py:54
  1152.9 40.0 %fusion.55 = bf16[8,6,64,2048]{3,2,1,0:T(8,128)(2,1)} fusion(bf16[8,256,6,64]{1,3,2,0:T(8,128)(2,1)S(1)} %bitcast.324, f32[8,6,256]{2,1,0:T(8,128)S(1)} %copy-done.45, f32[8,6,256,2048]{3,2,1,0:T(8,128)} %get-tuple-element.82), kind=kOutput, calls=%fused_computation.68 | convolution fusion | flops 3303014400 | bytes 114868224 | tf_op jit(solution)/shard_map/cshqk,csqhe->cskhe/dot_general | solution.py:80
  1192.9 16.7 copy.108
  1209.6 126.3 %fusion.52 = bf16[8,6,64,2048]{3,2,1,0:T(8,128)(2,1)} fusion(f32[8,6,256,2048]{3,2,1,0:T(8,128)} %fusion.221, f32[8,6,256]{2,1,0:T(8,128)S(1)} %copy-done.45, f32[8,6,256,2048]{3,2,1,0:T(8,128)} %get-tuple-element.82, bf16[1,16,256,6,64]{2,4,3,1,0:T(8,128)(2,1)} %bitcast.327), kind=kOutput, calls=%fused_computation.67 | convolution fusion | flops 3454023680 | bytes 416940032 | tf_op jit(solution)/shard_map/cshqk,csqhe->cskhe/dot_general | solution.py:77
  1352.5 20.4 maximum_bitcast_fusion
  1375.0 41.3 %fusion.58 = bf16[8,6,64,2048]{3,2,1,0:T(8,128)(2,1)} fusion(bf16[8,256,6,64]{1,3,2,0:T(8,128)(2,1)S(1)} %bitcast.321, f32[8,6,256]{2,1,0:T(8,128)S(1)} %log_add_fusion, f32[8,6,256,2048]{3,2,1,0:T(8,128)} %get-tuple-element.80), kind=kOutput, calls=%fused_computation.69 | convolution fusion | flops 3303014400 | bytes 114868224 | tf_op jit(solution)/shard_map/cshqk,csqhe->cskhe/dot_general | solution.py:80
  1416.3 16.7 copy.110
  1433.0 39.5 %fusion.222 = f32[8,6,256,2048]{3,2,1,0:T(8,128)} fusion(bf16[8,256,6,64]{1,3,2,0:T(8,128)(2,1)S(1)} %bitcast.322, bf16[8,2048,6,64]{1,3,2,0:T(8,128)(2,1)} %bitcast.316), kind=kOutput, calls=%fused_computation.267 | convolution fusion | flops 3221225472 | bytes 114819072 | tf_op jit(solution)/shard_map/csqhe,cskhe->cshqk/dot_general | solution.py:54
  1472.5 131.2 %fusion.49 = bf16[8,6,64,2048]{3,2,1,0:T(8,128)(2,1)} fusion(f32[8,6,256,2048]{3,2,1,0:T(8,128)} %fusion.222, f32[8,6,256]{2,1,0:T(8,128)S(1)} %log_add_fusion, f32[8,6,256,2048]{3,2,1,0:T(8,128)} %get-tuple-element.80, bf16[1,16,256,6,64]{2,4,3,1,0:T(8,128)(2,1)} %bitcast.328), kind=kOutput, calls=%fused_computation.66 | convolution fusion | flops 3454023680 | bytes 416940032 | tf_op jit(solution)/shard_map/cshqk,csqhe->cskhe/dot_general | solution.py:77
  1603.7 16.8 copy.109
  1620.5 20.4 maximum_bitcast_fusion.1
  1652.8 128.5 %fusion.123 = bf16[8,6,64,256]{3,2,1,0:T(8,128)(2,1)S(1)} fusion(bf16[8,2048,6,64]{1,3,2,0:T(8,128)(2,1)} %bitcast.312, f32[8,6,256,2048]{3,2,1,0:T(8,128)} %fusion.221, f32[8,6,256]{2,1,0:T(8,128)S(1)} %copy-done.46, f32[8,6,256,2048]{3,2,1,0:T(8,128)} %get-tuple-element.82), kind=kOutput, calls=%fused_computation.159 | convolution fusion | flops 3448518656 | bytes 215531520 | tf_op jit(solution)/shard_map/cshqk,cskhe->csqhe/dot_general | solution.py:66
  1783.0 128.0 %fusion.120 = bf16[8,6,64,256]{3,2,1,0:T(8,128)(2,1)} fusion(bf16[8,2048,6,64]{1,3,2,0:T(8,128)(2,1)} %bitcast.314, f32[8,6,256,2048]{3,2,1,0:T(8,128)} %fusion.222, f32[8,6,256]{2,1,0:T(8,128)S(1)} %log_add_fusion, f32[8,6,256,2048]{3,2,1,0:T(8,128)} %get-tuple-element.80), kind=kOutput, calls=%fused_computation.158 | convolution fusion | flops 3448518656 | bytes 215531520 | tf_op jit(solution)/shard_map/cshqk,cskhe->csqhe/dot_general | solution.py:66
  2002.1 42.0 %all-reduce.1 = (f32[3456]{0:T(1024)}, f32[768]{0:T(1024)}, f32[384]{0:T(512)}, f32[768]{0:T(1024)}, f32[384]{0:T(512)}, /*index=5*/f32[1536]{0:T(1024)}, f32[384]{0:T(512)}) all-reduce(f32[3456]{0:T(1024)S(1)} %reshape.915, f32[768]{0:T(1024)S(1)} %get-tuple-element.100, ...), channel_id=1, replica_groups=mesh['clip'=4,'sp'=8] {'clip','sp'}, use_global_device_ids=true, to_apply=%region_33.34 | all-reduce | flops 7680 | bytes 61440 | tf_op jit(solution)/shard_map/psum | solution.py:339
  2044.1 215.2 %all-reduce.5.cloned.1.call-done = (f32[384,3456]{1,0:T(8,128)}, f32[384,1152]{1,0:T(8,128)}, f32[384,384]{1,0:T(8,128)}, f32[384,1152]{1,0:T(8,128)}, f32[384,3...) async-done(((f32[384,3456]{1,0:T(8,128)}, f32[384,1152]{1,0:T(8,128)}, f32[384,384]{1,0:T(8,128)}, f32[384,1152]{1,0:T(8,128)}, f32[384,384]{1,0:T(8,128)}, ...) | async-done | bytes 14745616 | tf_op jit(solution)/shard_map/psum | solution.py:339
  (373 shorter events, 442.9 us)
Async XLA Ops:
  7.2 240.9 %all-gather.3.cloned.1.call-start = ((), (), s32[]{:S(2)}) async-start(), calls=%async_computation.2 | async-start | bytes 28311552 | tf_op jit(solution)/shard_map/all_gather | solution.py:136
  11.5 15.8 copy-start.67
  11.5 15.8 copy-start.96
  14.4 13.0 copy-start.43
  25.3 443.0 %all-gather.5.cloned.1.call-start = ((), (), s32[]{:S(2)}) async-start(), calls=%async_computation.3 | async-start | bytes 28311552 | tf_op jit(solution)/shard_map/all_gather | solution.py:136
  26.1 1930.0 %reduce-scatter.3.cloned.1.call-start = ((), (), s32[]{:S(2)}) async-start(), calls=%async_computation.4 | async-start | bytes 28311552 | tf_op jit(solution)/shard_map/reduce_scatter | solution.py:287
  573.6 31.1 %copy-start.39 = (f32[8,6,256]{2,1,0:T(8,128)}, f32[8,6,256]{2,1,0:T(8,128)S(1)}, u32[]{:S(2)}) copy-start(f32[8,6,256]{2,1,0:T(8,128)S(1)} %get-tuple-element.79) | copy-start | bytes 147460
  604.7 37.9 %copy-start.47 = (f32[8,6,256]{2,1,0:T(8,128)}, f32[8,6,256]{2,1,0:T(8,128)S(1)}, u32[]{:S(2)}) copy-start(f32[8,6,256]{2,1,0:T(8,128)S(1)} %fusion.7) | copy-start | bytes 147460
  715.2 41.9 %copy-start.13 = (bf16[8,256,384]{2,1,0:T(8,128)(2,1)S(1)}, bf16[8,256,384]{2,1,0:T(8,128)(2,1)}, u32[]{:S(2)}) copy-start(bf16[8,256,384]{2,1,0:T(8,128)(2,1)} %copy.80) | copy-start | bytes 4718596
  715.2 41.9 %copy-start.37 = (bf16[384,384]{1,0:T(8,128)(2,1)S(1)}, bf16[384,384]{1,0:T(8,128)(2,1)}, u32[]{:S(2)}) copy-start(bf16[384,384]{1,0:T(8,128)(2,1)} %param.26) | copy-start | bytes 884740
  715.2 41.9 %copy-start.72 = (f32[384]{0:T(512)S(1)}, f32[384]{0:T(512)}, u32[]{:S(2)}) copy-start(f32[384]{0:T(512)} %param.27) | copy-start | bytes 4612
  715.2 41.9 %copy-start.80 = (f32[384]{0:T(512)S(1)}, f32[384]{0:T(512)}, u32[]{:S(2)}) copy-start(f32[384]{0:T(512)} %get-tuple-element.33) | copy-start | bytes 4612
  764.8 11.5 copy-start.7
  764.8 11.5 copy-start.51
  874.1 58.2 %copy-start.8 = (f32[1,16,256,384]{3,2,1,0:T(8,128)}, f32[1,16,256,384]{3,2,1,0:T(8,128)S(1)}, u32[]{:S(2)}) copy-start(f32[1,16,256,384]{3,2,1,0:T(8,128)S(1)} %get-tuple-element.56) | copy-start | bytes 18874372
  874.1 58.1 %copy-start.57 = (f32[16,256]{1,0:T(8,128)}, f32[16,256]{1,0:T(8,128)S(1)}, u32[]{:S(2)}) copy-start(f32[16,256]{1,0:T(8,128)S(1)} %broadcast_multiply_fusion.1) | copy-start | bytes 49156
  875.5 56.8 %copy-start.65 = (f32[16,256]{1,0:T(8,128)}, f32[16,256]{1,0:T(8,128)S(1)}, u32[]{:S(2)}) copy-start(f32[16,256]{1,0:T(8,128)S(1)} %fusion.167) | copy-start | bytes 49156
  876.3 16.8 copy-start.28
  876.3 16.8 copy-start.102
  876.3 16.8 copy-start.112
  958.1 12.6 copy-start.119
  1052.8 13.0 copy-start.52
  1052.8 13.0 copy-start.77
  1052.8 13.0 copy-start.115
  1083.9 24.5 %copy-start.38 = (bf16[384,384]{1,0:T(8,128)(2,1)S(1)}, bf16[384,384]{1,0:T(8,128)(2,1)}, u32[]{:S(2)}) copy-start(bf16[384,384]{1,0:T(8,128)(2,1)} %param.26) | copy-start | bytes 884740
  1114.2 38.7 %copy-start.45 = (f32[8,6,256]{2,1,0:T(8,128)S(1)}, f32[8,6,256]{2,1,0:T(8,128)}, u32[]{:S(2)}) copy-start(f32[8,6,256]{2,1,0:T(8,128)} %log_add_fusion.1) | copy-start | bytes 147460
  1373.0 583.1 %reduce-scatter.5.cloned.1.call-start = ((), (), s32[]{:S(2)}) async-start(), calls=%async_computation.5 | async-start | bytes 28311552 | tf_op jit(solution)/shard_map/reduce_scatter | solution.py:287
  1640.9 618.4 %all-reduce.5.cloned.1.call-start = ((), (), s32[]{:S(2)}) async-start(), calls=%async_computation.6 | async-start | bytes 29491200 | tf_op jit(solution)/shard_map/psum | solution.py:339
  1923.9 14.5 slice-start
  1927.2 11.2 slice-start.1
  1927.2 11.2 copy-start.23
  1927.2 17.4 slice-start.2
  (97 other events, 577.8 us)
Sparse Core Ops, SparseCore 0:
  25.5 222.5 all-gather.2
  250.2 218.0 all-gather.4
  1373.1 245.3 reduce-scatter.2
  1641.1 245.4 reduce-scatter.4
  1996.0 263.3 all-reduce.4
where the time goes:
time: 2290 us; the launch traced here: 2280 us
  matrix products  1110 us (48%)
  waiting for transfers between devices  609 us (27%)
  local copies, waits for them, and re-layouts  328 us (14%)
  other arithmetic  168 us (7%)
  blocking collectives  42 us (2%)
    all_gather x2, waiting for transfers between devices, body(): lax.all_gather(keyvals[:, first:first + FRAME_BLOCK], 'sp', axis=2, tiled...  393 us
    dot_general x2, matrix products, key_pass(): jnp.einsum('cshqk,csqhe->cskhe', grad_scores, queries, preferred_element_...  258 us
    dot_general x2, matrix products, query_pass(): jnp.einsum('cshqk,cskhe->csqhe', grad_scores, keys, preferred_element_typ...  257 us
    psum x1, waiting for transfers between devices, body(): lax.psum((grad_ada_weight, grad_ada_bias, grad_spatial_proj, grad_spatial...  215 us
    dot_general x2, matrix products, key_pass(): jnp.einsum('cshqk,csqhe->cskhe', soft_weights.astype(jnp.bfloat16), grads...  81.3 us
    dot_general x2, matrix products, attend(): jnp.einsum('csqhe,cskhe->cshqk', queries, keys, preferred_element_type=jn...  78.4 us
    dot_general x2, matrix products, probabilities(): jnp.einsum('csqhe,cskhe->cshqk', grads, values, preferred_element_type=jn...  78.2 us
    dot_general x2, matrix products, attend(): jnp.einsum('cshqk,cskhe->csqhe', soft_weights, values, preferred_element_...  77.1 us
  transfers between devices with their start and end apart: 5, of which 3 were waited for; matrix products, arithmetic and copies ran while one was open for 28% of the time, Pallas kernels for 0%

commit v1 on v0

--- a/solution.py
+++ b/solution.py
@@ -1,15 +1,18 @@
-from functools import partial
+from functools import partial, reduce
 import math
 
 import jax
 import jax.numpy as jnp
 from jax import lax
+from jax.experimental import pallas as pl
+from jax.experimental.pallas import tpu as pltpu
 from jax.sharding import PartitionSpec as P
 
 HEADS = 6
 HEAD_DIM = 64
 FRAME_BLOCK = 8
 TSTEPS = 1000
+GELU_RATE = math.sqrt(2.0 / math.pi)
 
 
 def modulate(field, shift, scale):
@@ -375,9 +378,480 @@
     )
 
 
+MXB = jnp.bfloat16
+F32 = jnp.float32
+TILE = 16
+VMEM_BYTES = 60 * 2**20
+
+
+def dot(left, right):
+    return jnp.dot(left, right, preferred_element_type=F32)
+
+
+def dot_nt(left, right):
+    return lax.dot_general(left, right, (((1,), (1,)), ((), ())), preferred_element_type=F32)
+
+
+def dot_tn(left, right):
+    return lax.dot_general(left, right, (((0,), (0,)), ((), ())), preferred_element_type=F32)
+
+
+def turned(array):
+    return array.astype(F32).T.astype(array.dtype)
+
+
+def normalise(field):
+    centred = field - jnp.mean(field, axis=-1, keepdims=True)
+    rate = lax.rsqrt(jnp.mean(centred * centred, axis=-1, keepdims=True) + 1e-06)
+    return centred * rate, rate
+
+
+def normalise_back(grad, normed, rate, scale):
+    inner = grad * (1.0 + scale)
+    mean = jnp.mean(inner, axis=-1, keepdims=True)
+    slope = jnp.mean(inner * normed, axis=-1, keepdims=True)
+    return rate * (inner - mean - normed * slope)
+
+
+def eight_rows(array):
+    return jnp.sum(array.reshape(array.shape[0] // 8, 8, array.shape[1]), axis=0)
+
+
+def low_lanes():
+    return lax.broadcasted_iota(jnp.int32, (1, 2 * HEAD_DIM), 1) < HEAD_DIM
+
+
+def halves(pair):
+    low = low_lanes()
+    zero = jnp.zeros_like(pair)
+    return jnp.where(low, pair, zero), jnp.where(low, zero, pair)
+
+
+def spatial_forward(
+    x_ref, modes_ref, proj_ref, bias_ref, q_ref, k_ref, v_ref, attn_ref, log_ref, turned_ref, rows, block, part
+):
+    tokens, width = x_ref.shape[1:]
+    pairs = width // (2 * HEAD_DIM)
+    shift = modes_ref[0:1, :]
+    scale = modes_ref[1:2, :]
+
+    def project(index, carry):
+        at = pl.ds(pl.multiple_of(index * rows, rows), rows)
+        normed, _ = normalise(x_ref[0, at, :].astype(F32))
+        hidden = (normed * (1.0 + scale) + shift).astype(MXB)
+        mixed = dot(hidden, proj_ref[...]) + bias_ref[...]
+        q_ref[0, at, :] = mixed[:, :width].astype(MXB)
+        k_ref[0, at, :] = mixed[:, width : 2 * width].astype(MXB)
+        value = mixed[:, 2 * width :].astype(MXB)
+        v_ref[0, at, :] = value
+        across = turned(value)
+        for head in range(2 * pairs):
+            turned_ref[head, :HEAD_DIM, at] = across[head * HEAD_DIM : (head + 1) * HEAD_DIM]
+        return carry
+
+    turned_ref[:, HEAD_DIM:, :] = jnp.ones((2 * pairs, turned_ref.shape[1] - HEAD_DIM, tokens), MXB)
+    lax.fori_loop(0, tokens // rows, project, 0)
+
+    def attend_block(index, carry):
+        pair = lax.rem(index, pairs)
+        at = pl.ds(pl.multiple_of(lax.div(index, pairs) * block, block), block)
+        lanes = pl.ds(pl.multiple_of(pair * 2 * HEAD_DIM, 2 * HEAD_DIM), 2 * HEAD_DIM)
+        scores = []
+        tops = []
+        for query in halves(q_ref[0, at, lanes] * MXB(HEAD_DIM**-0.5)):
+            each = [
+                dot_nt(k_ref[0, first : first + part, lanes], query) for first in range(0, tokens, part)
+            ]
+            top = [jnp.max(s.reshape(part // 8, 8, block), axis=0) for s in each]
+            scores.append(each)
+            tops.append(jnp.max(reduce(jnp.maximum, top), axis=0, keepdims=True))
+        mixed = []
+        for half in range(2):
+            total = jnp.zeros((turned_ref.shape[1], block), F32)
+            for number, s in enumerate(scores[half]):
+                weights = jnp.exp(s - tops[half]).astype(MXB)
+                values = turned_ref[2 * pair + half, :, number * part : (number + 1) * part]
+                total = total + dot(values, weights)
+            mass = total[HEAD_DIM : HEAD_DIM + 1]
+            log_ref[0, pair, half : half + 1, at] = tops[half] + jnp.log(mass)
+            mixed.append(total[:HEAD_DIM] / mass)
+        attn_ref[0, at, lanes] = jnp.concatenate(mixed, axis=0).T.astype(MXB)
+        return carry
+
+    lax.fori_loop(0, pairs * (tokens // block), attend_block, 0)
+
+
+def spatial_backward(
+    da_ref, attn_ref, q_ref, k_ref, v_ref, log_ref, x_ref, modes_ref, proj_turned_ref,
+    dx_ref, grad_proj_ref, sums_ref, bias_sums_ref,
+    mix_ref, delta_ref, dk_ref, dv_ref, rows, block, part,
+):
+    tokens, width = x_ref.shape[1:]
+    pairs = width // (2 * HEAD_DIM)
+    scale_factor = HEAD_DIM**-0.5
+
+    @pl.when(pl.program_id(0) == 0)
+    def _():
+        grad_proj_ref[...] = jnp.zeros_like(grad_proj_ref)
+        sums_ref[...] = jnp.zeros_like(sums_ref)
+        bias_sums_ref[...] = jnp.zeros_like(bias_sums_ref)
+
+    head_of = lax.broadcasted_iota(jnp.int32, (8, width), 1) // HEAD_DIM
+    picks = jnp.where(head_of == lax.broadcasted_iota(jnp.int32, (8, width), 0), 1.0, 0.0).astype(MXB)
+
+    def deltas(index, carry):
+        at = pl.ds(pl.multiple_of(index * rows, rows), rows)
+        product = da_ref[0, at, :].astype(F32) * attn_ref[0, at, :].astype(F32)
+        high = product.astype(MXB)
+        rest = (product - high.astype(F32)).astype(MXB)
+        summed = dot_nt(picks, high) + dot_nt(picks, rest)
+        for pair in range(pairs):
+            delta_ref[pair, 0:2, at] = summed[2 * pair : 2 * pair + 2]
+        return carry
+
+    lax.fori_loop(0, tokens // rows, deltas, 0)
+
+    for pair in range(pairs):
+        first_lane = 2 * HEAD_DIM * pair
+        lanes = slice(first_lane, first_lane + 2 * HEAD_DIM)
+        dk_ref[...] = jnp.zeros_like(dk_ref)
+        dv_ref[...] = jnp.zeros_like(dv_ref)
+        keys_across = turned(k_ref[0, :, lanes])
+
+        def queries_block(index, carry, pair=pair, lanes=lanes, keys_across=keys_across):
+            at = pl.ds(pl.multiple_of(index * block, block), block)
+            query = halves(q_ref[0, at, lanes] * MXB(scale_factor))
+            grad = halves(da_ref[0, at, lanes])
+            query_both = jnp.concatenate(query, axis=0)
+            grad_both = jnp.concatenate(grad, axis=0)
+            grad_query = [jnp.zeros((HEAD_DIM, block), F32), jnp.zeros((HEAD_DIM, block), F32)]
+            for first in range(0, tokens, part):
+                span = slice(first, first + part)
+                keys = k_ref[0, span, lanes]
+                values = v_ref[0, span, lanes]
+                weights = []
+                grad_scores = []
+                for half in range(2):
+                    scores = dot_nt(keys, query[half])
+                    exact = jnp.exp(scores - log_ref[0, pair, half : half + 1, at])
+                    grad_weights = dot_nt(values, grad[half])
+                    term = (exact * (grad_weights - delta_ref[pair, half : half + 1, at])).astype(MXB)
+                    weights.append(exact.astype(MXB))
+                    grad_scores.append(term)
+                    grad_query[half] = grad_query[half] + dot(
+                        keys_across[half * HEAD_DIM : (half + 1) * HEAD_DIM, span], term
+                    )
+                dv_ref[span, :] += dot(jnp.concatenate(weights, axis=1), grad_both)
+                dk_ref[span, :] += dot(jnp.concatenate(grad_scores, axis=1), query_both)
+            mix_ref[at, lanes] = (jnp.concatenate(grad_query, axis=0).T * scale_factor).astype(MXB)
+            return carry
+
+        lax.fori_loop(0, tokens // block, queries_block, 0)
+        mix_ref[:, width + first_lane : width + first_lane + 2 * HEAD_DIM] = dk_ref[...].astype(MXB)
+        mix_ref[:, 2 * width + first_lane : 2 * width + first_lane + 2 * HEAD_DIM] = dv_ref[...].astype(MXB)
+
+    shift = modes_ref[0:1, :]
+    scale = modes_ref[1:2, :]
+
+    def finish(index, carry):
+        at = pl.ds(pl.multiple_of(index * rows, rows), rows)
+        normed, rate = normalise(x_ref[0, at, :].astype(F32))
+        hidden = (normed * (1.0 + scale) + shift).astype(MXB)
+        grad_mix = mix_ref[at, :]
+        grad_proj_ref[...] += dot_tn(hidden, grad_mix)
+        bias_sums_ref[...] += eight_rows(grad_mix.astype(F32))
+        grad_hidden = dot(grad_mix, proj_turned_ref[...])
+        sums_ref[0] += eight_rows(grad_hidden)
+        sums_ref[1] += eight_rows(grad_hidden * normed)
+        dx_ref[0, at, :] = normalise_back(grad_hidden, normed, rate, scale).astype(MXB)
+        return carry
+
+    lax.fori_loop(0, tokens // rows, finish, 0)
+
+
+def middle(
+    x_ref, attn_ref, og_ref, weight_ref, modes_ref, mask_ref,
+    so_ref, so_turned_ref, so_bias_ref, t_ref, t_turned_ref, t_bias_ref, to_ref, to_turned_ref, to_bias_ref,
+    in_ref, in_turned_ref, in_bias_ref, out_ref, out_turned_ref, out_bias_ref,
+    block_ref, g1_ref, da_ref,
+    grad_so_ref, grad_t_ref, grad_to_ref, grad_in_ref, grad_out_ref, sums_ref, t_sums_ref, in_sums_ref,
+):
+    frames, tile, width = x_ref.shape
+    count = frames * tile
+    pairs = width // (2 * HEAD_DIM)
+    scale_factor = HEAD_DIM**-0.5
+
+    @pl.when(pl.program_id(0) == 0)
+    def _():
+        for ref in (grad_so_ref, grad_t_ref, grad_to_ref, grad_in_ref, grad_out_ref, sums_ref, t_sums_ref, in_sums_ref):
+            ref[...] = jnp.zeros_like(ref)
+
+    def mode(row):
+        return modes_ref[row : row + 1, :]
+
+    field = x_ref[...].reshape(count, width).astype(F32)
+    attn_one = attn_ref[...].reshape(count, width)
+    branch_one = dot(attn_one, so_ref[...]) + so_bias_ref[...]
+    field_one = field + mode(2) * branch_one
+    normed_two, rate_two = normalise(field_one)
+    hidden_two = (normed_two * (1.0 + mode(4)) + mode(3)).astype(MXB)
+    mixed = (dot(hidden_two, t_ref[...]) + t_bias_ref[...]).astype(MXB)
+    mask = mask_ref[...]
+    exact = []
+    rounded = []
+    queries = []
+    keys_across = []
+    attn_parts = []
+    for pair in range(pairs):
+        lanes = slice(2 * HEAD_DIM * pair, 2 * HEAD_DIM * (pair + 1))
+        query = halves(mixed[:, lanes] * MXB(scale_factor))
+        keys = mixed[:, width:][:, lanes]
+        values_across = turned(mixed[:, 2 * width :][:, lanes])
+        queries.append(query)
+        keys_across.append(turned(keys))
+        parts = []
+        for half in range(2):
+            scores = dot_nt(keys, query[half]) + mask
+            exponent = jnp.exp(scores - jnp.max(scores, axis=0, keepdims=True))
+            weights = exponent / jnp.sum(exponent, axis=0, keepdims=True)
+            exact.append(weights)
+            rounded.append(weights.astype(MXB))
+            parts.append(dot(values_across[half * HEAD_DIM : (half + 1) * HEAD_DIM], rounded[-1]))
+        attn_parts.append(jnp.concatenate(parts, axis=0).T.astype(MXB))
+    attn_two = jnp.concatenate(attn_parts, axis=1)
+    branch_two = dot(attn_two, to_ref[...]) + to_bias_ref[...]
+    field_two = field_one + mode(5) * branch_two
+    normed_three, rate_three = normalise(field_two)
+    hidden_three = (normed_three * (1.0 + mode(7)) + mode(6)).astype(MXB)
+    inner = dot(hidden_three, in_ref[...]) + in_bias_ref[...]
+    square = inner * inner
+    bend = jnp.tanh(inner * (GELU_RATE + GELU_RATE * 0.044715 * square))
+    half_up = 0.5 + 0.5 * bend
+    active = (inner * half_up).astype(MXB)
+    slope = half_up + inner * (0.5 - 0.5 * bend * bend) * (GELU_RATE + 3.0 * GELU_RATE * 0.044715 * square)
+    branch_three = dot(active, out_ref[...]) + out_bias_ref[...]
+    block_ref[...] = (field_two + mode(8) * branch_three).astype(MXB).reshape(frames, tile, width)
+
+    grad_field = og_ref[...].reshape(count, width).astype(F32) * weight_ref[...]
+    sums_ref[8] += eight_rows(grad_field * branch_three)
+    grad_branch = (mode(8) * grad_field).astype(MXB)
+    grad_out_ref[...] += dot_tn(grad_branch, active)
+    sums_ref[11] += eight_rows(grad_branch.astype(F32))
+    grad_inner = (dot(grad_branch, out_turned_ref[...]) * slope).astype(MXB)
+    grad_in_ref[...] += dot_tn(hidden_three, grad_inner)
+    in_sums_ref[...] += eight_rows(grad_inner.astype(F32))
+    grad_hidden = dot(grad_inner, in_turned_ref[...])
+    sums_ref[6] += eight_rows(grad_hidden)
+    sums_ref[7] += eight_rows(grad_hidden * normed_three)
+    grad_field = grad_field + normalise_back(grad_hidden, normed_three, rate_three, mode(7))
+
+    sums_ref[5] += eight_rows(grad_field * branch_two)
+    grad_branch = (mode(5) * grad_field).astype(MXB)
+    grad_to_ref[...] += dot_tn(attn_two, grad_branch)
+    sums_ref[10] += eight_rows(grad_branch.astype(F32))
+    grad_attn = dot(grad_branch, to_turned_ref[...]).astype(MXB)
+    grad_queries = []
+    grad_keys = []
+    grad_values = []
+    for pair in range(pairs):
+        lanes = slice(2 * HEAD_DIM * pair, 2 * HEAD_DIM * (pair + 1))
+        grad = halves(grad_attn[:, lanes])
+        values = mixed[:, 2 * width :][:, lanes]
+        grad_query = []
+        terms = []
+        for half in range(2):
+            weights = exact[2 * pair + half]
+            grad_weights = dot_nt(values, grad[half])
+            delta = jnp.sum(weights * grad_weights, axis=0, keepdims=True)
+            term = (weights * (grad_weights - delta)).astype(MXB)
+            terms.append(term)
+            grad_query.append(dot(keys_across[pair][half * HEAD_DIM : (half + 1) * HEAD_DIM], term))
+        both = jnp.concatenate(terms, axis=1)
+        grad_queries.append((jnp.concatenate(grad_query, axis=0).T * scale_factor).astype(MXB))
+        grad_keys.append(dot(both, jnp.concatenate(queries[pair], axis=0)).astype(MXB))
+        grad_values.append(
+            dot(
+                jnp.concatenate([rounded[2 * pair], rounded[2 * pair + 1]], axis=1),
+                jnp.concatenate(grad, axis=0),
+            ).astype(MXB)
+        )
+    grad_mix = jnp.concatenate(grad_queries + grad_keys + grad_values, axis=1)
+    grad_t_ref[...] += dot_tn(hidden_two, grad_mix)
+    t_sums_ref[...] += eight_rows(grad_mix.astype(F32))
+    grad_hidden = dot(grad_mix, t_turned_ref[...])
+    sums_ref[3] += eight_rows(grad_hidden)
+    sums_ref[4] += eight_rows(grad_hidden * normed_two)
+    grad_field = grad_field + normalise_back(grad_hidden, normed_two, rate_two, mode(4))
+
+    sums_ref[2] += eight_rows(grad_field * branch_one)
+    grad_branch = (mode(2) * grad_field).astype(MXB)
+    grad_so_ref[...] += dot_tn(attn_one, grad_branch)
+    sums_ref[9] += eight_rows(grad_branch.astype(F32))
+    g1_ref[...] = grad_field.reshape(frames, tile, width)
+    da_ref[...] = dot(grad_branch, so_turned_ref[...]).astype(MXB).reshape(frames, tile, width)
+
+
+def whole_spec(shape):
+    rank = len(shape)
+    return pl.BlockSpec(shape, lambda *_: (0,) * rank, pipeline_mode=pl.Buffered(1))
+
+
+def acc_spec(shape):
+    rank = len(shape)
+    return pl.BlockSpec(shape, lambda *_: (0,) * rank)
+
+
+def params():
+    return pltpu.CompilerParams(vmem_limit_bytes=VMEM_BYTES)
+
+
+def fast_body(
+    tokens, conditioning, timesteps, out_grad, ada_weight, ada_bias, spatial_proj, spatial_bias, spatial_out,
+    spatial_out_bias, temporal_proj, temporal_bias, temporal_out, temporal_out_bias, hidden_in, hidden_in_bias,
+    hidden_out, hidden_out_bias,
+):
+    _, frames, stripe, width = tokens.shape
+    hidden = hidden_in.shape[1]
+    pairs = width // (2 * HEAD_DIM)
+    cond_act = jax.nn.silu(conditioning.astype(F32)).astype(MXB)
+    modes = (jnp.dot(cond_act, ada_weight, preferred_element_type=F32) + ada_bias).reshape(9, width)
+
+    def to_frames(array):
+        return lax.all_to_all(array, "sp", split_axis=0, concat_axis=1, tiled=True)
+
+    def to_patches(array):
+        return lax.all_to_all(array, "sp", split_axis=1, concat_axis=0, tiled=True)
+
+    def widen(bias):
+        return jnp.concatenate([bias[:width], jnp.zeros((width,), F32), bias[width:]])[None, :]
+
+    x_patches = tokens[0]
+    x_frames = to_frames(x_patches)
+    mine, patches = x_frames.shape[:2]
+    frame_spec = pl.BlockSpec((1, patches, width), lambda f: (f, 0, 0))
+    log_spec = pl.BlockSpec((1, pairs, 2, patches), lambda f: (f, 0, 0, 0))
+    frame_shape = jax.ShapeDtypeStruct((mine, patches, width), MXB)
+    queries, keys, values, attn_frames, logs = pl.pallas_call(
+        partial(spatial_forward, rows=256, block=min(1024, patches), part=512),
+        grid=(mine,),
+        in_specs=[frame_spec, whole_spec((9, width)), whole_spec((width, 3 * width)), whole_spec((1, 3 * width))],
+        out_specs=[frame_spec] * 4 + [log_spec],
+        out_shape=[frame_shape] * 4 + [jax.ShapeDtypeStruct((mine, pairs, 2, patches), F32)],
+        scratch_shapes=[pltpu.VMEM((2 * pairs, HEAD_DIM + 16, patches), MXB)],
+        compiler_params=params(),
+    )(x_frames, modes, spatial_proj, widen(spatial_bias))
+    attn_patches = to_patches(attn_frames)
+
+    slope = jnp.tan((timesteps.astype(F32) / TSTEPS + 0.008) / 1.008 * (0.5 * math.pi))
+    loss_weight = jnp.minimum(1.0, 5.0 * slope * slope).reshape(1, 1)
+    count = frames * TILE
+    place = jnp.arange(count) % TILE
+    mask = jnp.where(place[:, None] == place[None, :], 0.0, -1e30).astype(F32)
+    tile_spec = pl.BlockSpec((frames, TILE, width), lambda i: (0, i, 0))
+    small = (
+        loss_weight * jnp.ones((1, width), F32), modes, mask,
+        spatial_out, spatial_out.T, spatial_out_bias[None, :],
+        temporal_proj, temporal_proj.T, widen(temporal_bias),
+        temporal_out, temporal_out.T, temporal_out_bias[None, :],
+        hidden_in, hidden_in.T, hidden_in_bias[None, :],
+        hidden_out, hidden_out.T, hidden_out_bias[None, :],
+    )
+    sums_shapes = [
+        (width, width), (width, 3 * width), (width, width), (width, hidden), (width, hidden),
+        (12, 8, width), (8, 3 * width), (8, hidden),
+    ]
+    out_shapes = [
+        jax.ShapeDtypeStruct((frames, stripe, width), MXB),
+        jax.ShapeDtypeStruct((frames, stripe, width), F32),
+        jax.ShapeDtypeStruct((frames, stripe, width), MXB),
+    ] + [jax.ShapeDtypeStruct(s, F32) for s in sums_shapes]
+    (
+        block_out, g1, da_patches, grad_so, grad_t, grad_to, grad_in, grad_out_turned, sums, t_sums, in_sums,
+    ) = pl.pallas_call(
+        middle,
+        grid=(stripe // TILE,),
+        in_specs=[tile_spec] * 3 + [whole_spec(a.shape) for a in small],
+        out_specs=[tile_spec] * 3 + [acc_spec(s) for s in sums_shapes],
+        out_shape=out_shapes,
+        compiler_params=params(),
+    )(x_patches, attn_patches, out_grad[0], *small)
+    da_frames = to_frames(da_patches)
+
+    sum_shapes = [(width, 3 * width), (2, 8, width), (8, 3 * width)]
+    dx_frames, grad_sp, sp_sums, sp_bias_sums = pl.pallas_call(
+        partial(spatial_backward, rows=256, block=min(1024, patches), part=512),
+        grid=(mine,),
+        in_specs=[frame_spec] * 5 + [log_spec, frame_spec, whole_spec((9, width)), whole_spec((3 * width, width))],
+        out_specs=[frame_spec] + [acc_spec(s) for s in sum_shapes],
+        out_shape=[frame_shape] + [jax.ShapeDtypeStruct(s, F32) for s in sum_shapes],
+        scratch_shapes=[
+            pltpu.VMEM((patches, 3 * width), MXB),
+            pltpu.VMEM((pairs, 2, patches), F32),
+            pltpu.VMEM((patches, 2 * HEAD_DIM), F32),
+            pltpu.VMEM((patches, 2 * HEAD_DIM), F32),
+        ],
+        compiler_params=params(),
+    )(da_frames, attn_frames, queries, keys, values, logs, x_frames, modes, spatial_proj.T)
+    input_grad = (g1 + to_patches(dx_frames).astype(F32)).astype(MXB)
+
+    clip_at = lax.axis_index("clip")
+    clips = lax.axis_size("clip")
+    vector = jnp.sum(sums, axis=1)
+    sp_vector = jnp.sum(sp_sums, axis=1)
+    grad_modes = jnp.concatenate([sp_vector, vector[2:9]], axis=0).reshape(1, 9 * width)
+    mine_only = (jnp.arange(clips) == clip_at)[:, None]
+    first_on_sp = (lax.axis_index("sp") == 0).astype(F32)
+    early = lax.psum((grad_so, grad_t, grad_to, grad_in, grad_out_turned), ("clip", "sp"))
+    sp_bias = jnp.sum(sp_bias_sums, axis=0)
+    t_bias = jnp.sum(t_sums, axis=0)
+    pieces = (
+        jnp.where(mine_only, grad_modes, 0.0),
+        jnp.where(mine_only, cond_act.astype(F32) * first_on_sp, 0.0),
+        sp_bias,
+        t_bias,
+        jnp.sum(in_sums, axis=0),
+        vector[9:12],
+    )
+    flat = jnp.concatenate([p.reshape(-1) for p in pieces])
+    flat, grad_sp = lax.psum((flat, grad_sp), ("clip", "sp"))
+    found = []
+    start = 0
+    for piece in pieces:
+        found.append(flat[start : start + piece.size].reshape(piece.shape))
+        start += piece.size
+    all_modes, all_cond, sp_bias, t_bias, in_bias, out_biases = found
+    grad_ada_weight = jnp.dot(all_cond.T, all_modes, precision=lax.Precision.HIGHEST)
+    grad_ada_bias = jnp.sum(all_modes, axis=0)
+    return (
+        block_out[None],
+        input_grad[None],
+        grad_ada_weight,
+        grad_ada_bias,
+        grad_sp,
+        jnp.concatenate([sp_bias[:width], sp_bias[2 * width :]]),
+        early[0],
+        out_biases[0],
+        early[1],
+        jnp.concatenate([t_bias[:width], t_bias[2 * width :]]),
+        early[2],
+        out_biases[1],
+        early[3],
+        in_bias,
+        early[4].T,
+        out_biases[2],
+    )
+
+
+def chosen(tokens, *others):
+    _, frames, stripe, _ = tokens.shape
+    if tokens.shape[0] == 1 and frames % lax.axis_size("sp") == 0 and stripe % TILE == 0:
+        return fast_body(tokens, *others)
+    return body(tokens, *others)
+
+
 def solution(mesh):
     return jax.shard_map(
-        body,
+        chosen,
         mesh=mesh,
         in_specs=(
             P("clip", None, "sp", None),

time: 2290 us -> 996 us (0.43)
  matrix products: 1110 us -> 6.69 us
  Pallas kernels: 0 us -> 432 us
  local copies, waits for them, and re-layouts: 328 us -> 55.9 us
  waiting for transfers between devices: 609 us -> 449 us
  other arithmetic: 168 us -> 9.96 us
  blocking collectives: 42 us -> 0 us
    dot_general x39 -> x2, matrix products: 1100 us -> 6.69 us  [the longest x1 6.22 us: fast_body(): jnp.dot(all_cond.T, all_modes, precision=lax.Precision.HIGHEST)]
    pallas_call x0 -> x3, Pallas kernels: none -> 432 us  [the longest x1 187 us: fast_body(): pl.pallas_call(partial(spatial_backward, rows=256, block=min(1024, patche...]
    all_gather x2 -> x0, waiting for transfers between devices: 393 us -> none  [body(): lax.all_gather(keyvals[:, first:first + FRAME_BLOCK], 'sp', axis=2, tiled...]
    all_to_all x0 -> x4, waiting for transfers between devices: none -> 201 us  [the longest x2 140 us: to_frames(): return lax.all_to_all(array, 'sp', split_axis=0, concat_axis=1, tiled=True)]
    slice x14 -> x7, local copies, waits for them, and re-layouts: 123 us -> 3.58 us  [the longest x3 2.16 us: fast_body(): found.append(flat[start:start + piece.size].reshape(piece.shape))]
    reduce_sum x16 -> x6, other arithmetic: 113 us -> 2.26 us  [the longest x1 0.79 us: fast_body(): sp_bias = jnp.sum(sp_bias_sums, axis=0)]
    reshape x11 -> x3, local copies, waits for them, and re-layouts: 69.1 us -> 0.64 us  [the longest x1 0.61 us: fast_body(): (jnp.dot(cond_act, ada_weight, preferred_element_type=F32) + ada_bias).re...]
    another operation x11 -> x1, local copies, waits for them, and re-layouts: 58.7 us -> 0.01 us
  transfers between devices with their start and end apart: 5 -> 5, of which waited for: 3 -> 4; matrix products, arithmetic and copies ran while one was open for 28% -> 4% of each run, Pallas kernels for 0% -> 0%
where the time goes in v1:
time: 996 us; the launch traced here: 989 us
  waiting for transfers between devices  449 us (45%)
  Pallas kernels  432 us (43%)
  local copies, waits for them, and re-layouts  55.9 us (6%)
  starting transfers between devices  20.7 us (2%)
  between operations  15.4 us (2%)
  other arithmetic  9.96 us (1%)
    psum x1, waiting for transfers between devices, fast_body(): flat, grad_sp = lax.psum((flat, grad_sp), ('clip', 'sp'))  248 us
    pallas_call x1, Pallas kernels, fast_body(): pl.pallas_call(partial(spatial_backward, rows=256, block=min(1024, patche...  187 us
    pallas_call x1, Pallas kernels, fast_body(): pl.pallas_call(middle, grid=(stripe // TILE,), in_specs=[tile_spec] * 3 +...  165 us
    all_to_all x2, waiting for transfers between devices, to_frames(): return lax.all_to_all(array, 'sp', split_axis=0, concat_axis=1, tiled=True)  140 us
    pallas_call x1, Pallas kernels, fast_body(): pl.pallas_call(partial(spatial_forward, rows=256, block=min(1024, patches...  80 us
    all_to_all x2, waiting for transfers between devices, to_patches(): return lax.all_to_all(array, 'sp', split_axis=1, concat_axis=0, tiled=True)  60.9 us
  transfers between devices with their start and end apart: 5, of which 4 were waited for; matrix products, arithmetic and copies ran while one was open for 4% of the time, Pallas kernels for 0%

profile of v1, /device:TPU:0, one launch (start us, length us, event | category | flops | bytes accessed | tf_op | source)
XLA Modules:
  0.0 989.1 jit_solution(15913907051188652127)
XLA Ops:
  7.2 6.6 all-to-all-start
  15.6 69.9 %all-to-all-done = bf16[16,256,384]{2,1,0:T(8,128)(2,1)} async-done(((bf16[16,256,384]{2,1,0:T(8,128)(2,1)}), bf16[16,256,384]{2,1,0:T(8,128)(2,1)}, u32[]{:S(2)}, u32[]{:S(2)}) %all-to-all-start) | async-done | bytes 3145760 | tf_op jit(solution)/shard_map/all_to_all | solution.py:720
  85.5 4.0 copy.58
  89.5 80.0 %shard_map.297 = (bf16[2,2048,384]{2,1,0:T(8,128)(2,1)}, bf16[2,2048,384]{2,1,0:T(8,128)(2,1)}, bf16[2,2048,384]{2,1,0:T(8,128)(2,1)}, bf16[2,2048,384]{2,1,0:T(8,128)(2,1)}, f32[2,3,2,2048]{3,2,1,0:T(2,128)}) custom-call(bf16[2,2048,384]{2,1,0:T(8,128)(2,1)} %bitcast.38, f32[9,384]{1,0:T(8,128)} %reshape.106.modes_ref, bf16[384,1152]{1,0:T(8,128)(2,1)} %proj_ref.1, ...), custom_call_target="tpu_custom_call" | custom-call | tf_op jit(solution)/shard_map/pallas_call | solution.py:734
  169.4 7.9 copy.59
  177.4 5.0 all-to-all-start.1
  183.7 1.4 copy.64
  185.2 1.5 copy.65
  186.7 1.3 copy.62
  188.0 0.9 copy.63
  188.9 0.9 copy.61
  192.1 0.8 compare_select_fusion.mask_ref
  193.0 60.9 %all-to-all-done.1 = bf16[2,2048,384]{2,0,1:T(2,128)(2,1)} async-done(((bf16[2,2048,384]{2,0,1:T(2,128)(2,1)}), bf16[2,2048,384]{2,0,1:T(2,128)(2,1)}, u32[]{:S(2)}, u32[]{:S(2)}) %all-to-all-start.1) | async-done | bytes 3145760 | tf_op jit(solution)/shard_map/all_to_all | solution.py:723
  253.9 4.1 copy.60
  258.6 165.1 %shard_map.298 = (bf16[16,256,384]{2,1,0:T(8,128)(2,1)}, f32[16,256,384]{2,1,0:T(8,128)}, bf16[16,256,384]{2,1,0:T(8,128)(2,1)}, f32[384,384]{1,0:T(8,128)}, f32...) custom-call(bf16[16,256,384]{2,1,0:T(8,128)(2,1)} %bitcast.41, ...), custom_call_target="tpu_custom_call" | custom-call | tf_op jit(solution)/shard_map/pallas_call | solution.py:770
  423.8 4.6 all-to-all-start.2
  428.5 1.4 copy.67
  430.1 69.8 %all-to-all-done.2 = bf16[16,256,384]{2,1,0:T(8,128)(2,1)} async-done(((bf16[16,256,384]{2,1,0:T(8,128)(2,1)}), bf16[16,256,384]{2,1,0:T(8,128)(2,1)}, u32[]{:S(2)}, u32[]{:S(2)}) %all-to-all-start.2) | async-done | bytes 3145760 | tf_op jit(solution)/shard_map/all_to_all | solution.py:720
  499.9 4.0 copy.66
  503.9 186.6 %shard_map.299 = (bf16[2,2048,384]{2,1,0:T(8,128)(2,1)}, f32[384,1152]{1,0:T(8,128)}, f32[2,8,384]{2,1,0:T(8,128)}, f32[8,1152]{1,0:T(8,128)}) custom-call(bf16[2,2048,384]{2,1,0:T(8,128)(2,1)} %bitcast.43, bf16[2,2048,384]{2,1,0:T(8,128)(2,1)} %get-tuple-element.36.attn_ref, bf16[2,2048,384]{2,1,0:T(8,128)(2,1)} %get-tuple-element.40.q_ref, ...), custom_call_target="tpu_custom_call" | custom-call | tf_op jit(solution)/shard_map/pallas_call | solution.py:781
  692.9 8.0 copy.68
  701.0 4.5 all-to-all-start.3
  705.5 248.2 %all-reduce.3.cloned.1.call-done = (f32[20352]{0:T(1024)}, f32[384,1152]{1,0:T(8,128)}, f32[384,384]{1,0:T(8,128)}, f32[384,1152]{1,0:T(8,128)}, f32[384,384]{1,...) async-done(((f32[20352]{0:T(1024)}, f32[384,1152]{1,0:T(8,128)}, f32[384,384]{1,0:T(8,128)}, f32[384,1152]{1,0:T(8,128)}, f32[384,384]{1,0:T(8,128)}, ...) | async-done | bytes 9518608 | tf_op jit(solution)/shard_map/psum | solution.py:816
  954.5 1.3 fusion.6
  955.8 3.0 copy.70
  959.5 1.4 fusion.5
  962.1 6.2 fusion.9
  968.3 2.5 copy.69
  970.9 5.5 fusion
  976.4 1.2 copy.85
  978.7 1.2 copy.87
  980.7 1.4 copy.89
  (98 shorter events, 12.5 us)
Async XLA Ops:
  7.2 7.3 copy-start
  7.2 6.6 copy-start.20
  7.2 6.6 copy-start.21
  7.2 7.3 copy-start.19
  7.2 7.7 copy-start.17
  7.2 78.2 %all-to-all-start = ((bf16[16,256,384]{2,1,0:T(8,128)(2,1)}), bf16[16,256,384]{2,1,0:T(8,128)(2,1)}, u32[]{:S(2)}, u32[]{:S(2)}) async-start(bf16[16,256,384]{2,1,0:T(8,128)(2,1)} %bitcast.40), calls=%async_computation | async-start | bytes 6291456 | tf_op jit(solution)/shard_map/all_to_all | solution.py:720
  177.4 6.3 copy-start.2
  177.4 7.8 copy-start.3
  177.4 76.5 %all-to-all-start.1 = ((bf16[2,2048,384]{2,0,1:T(2,128)(2,1)}), bf16[2,2048,384]{2,0,1:T(2,128)(2,1)}, u32[]{:S(2)}, u32[]{:S(2)}) async-start(bf16[2,2048,384]{2,0,1:T(2,128)(2,1)} %copy.59), calls=%async_computation.1 | async-start | bytes 6291456 | tf_op jit(solution)/shard_map/all_to_all | solution.py:723
  182.4 4.3 copy-start.5
  183.7 5.2 copy-start.9
  185.2 2.8 copy-start.10
  185.2 4.7 copy-start.18
  185.2 5.3 copy-start.22
  185.2 5.8 copy-start.23
  185.2 6.4 copy-start.24
  423.7 4.7 copy-start.4
  423.8 6.2 copy-start.13
  423.8 6.2 copy-start.16
  423.8 6.3 copy-start.15
  423.8 76.1 %all-to-all-start.2 = ((bf16[16,256,384]{2,1,0:T(8,128)(2,1)}), bf16[16,256,384]{2,1,0:T(8,128)(2,1)}, u32[]{:S(2)}, u32[]{:S(2)}) async-start(bf16[16,256,384]{2,1,0:T(8,128)(2,1)} %get-tuple-element.39), calls=%async_computation.2 | async-start | bytes 6291456 | tf_op jit(solution)/shard_map/all_to_all | solution.py:720
  428.4 525.2 %all-reduce.3.cloned.1.call-start = ((), (), s32[]{:S(2)}) async-start(), calls=%async_computation.4 | async-start | bytes 19038208 | tf_op jit(solution)/shard_map/psum | solution.py:816
  692.3 0.6 copy-start.14
  701.0 267.4 %all-to-all-start.3 = ((bf16[2,2048,384]{2,0,1:T(2,128)(2,1)}), bf16[2,2048,384]{2,0,1:T(2,128)(2,1)}, u32[]{:S(2)}, u32[]{:S(2)}) async-start(bf16[2,2048,384]{2,0,1:T(2,128)(2,1)} %copy.68), calls=%async_computation.3 | async-start | bytes 6291456 | tf_op jit(solution)/shard_map/all_to_all | solution.py:723
  970.9 5.5 copy-start.8
  976.3 1.4 copy-start.12
  976.3 2.3 copy-start.7
  977.8 2.1 copy-start.11
  977.8 2.9 copy-start.6
  978.7 3.4 copy-start.1
Sparse Core Ops, SparseCore 0:
  693.0 260.5 all-reduce.2

commit v2 on v1

--- a/solution.py
+++ b/solution.py
@@ -427,70 +427,217 @@
     return jnp.where(low, pair, zero), jnp.where(low, zero, pair)
 
 
+def others(count):
+    me = lax.axis_index("sp")
+    return me, [(step, lax.rem(me + step, count), lax.rem(me + count - step, count)) for step in range(1, count)]
+
+
+def send(source, target, send_sem, recv_sem, peer):
+    return pltpu.make_async_remote_copy(
+        src_ref=source, dst_ref=target, send_sem=send_sem, recv_sem=recv_sem,
+        device_id={"sp": peer}, device_id_type=pl.DeviceIdType.MESH,
+    )
+
+
+def greet(peers):
+    barrier = pltpu.get_barrier_semaphore()
+    for _, peer, _ in peers:
+        pl.semaphore_signal(barrier, inc=1, device_id={"sp": peer}, device_id_type=pl.DeviceIdType.MESH)
+
+
+def greeted(peers):
+    pl.semaphore_wait(pltpu.get_barrier_semaphore(), len(peers))
+
+
 def spatial_forward(
-    x_ref, modes_ref, proj_ref, bias_ref, q_ref, k_ref, v_ref, attn_ref, log_ref, turned_ref, rows, block, part
+    tokens_ref, modes_ref, proj_ref, bias_ref,
+    x_out, q_out, k_out, v_out, attn_out, patches_out, log_ref,
+    x_ref, q_ref, k_ref, v_ref, attn_ref, turned_ref,
+    x_send, x_recv, x_own, a_send, a_recv, a_own, save_sem,
+    rows, block, part, count,
+):
+    mine, tokens, width = x_ref.shape
+    stripe = tokens // count
+    pairs = width // (2 * HEAD_DIM)
+    near = block // stripe
+    blocks = tokens // block
+    me, peers = others(count)
+    shift = modes_ref[0:1, :]
+    scale = modes_ref[1:2, :]
+
+    def x_copy(frame, step, peer):
+        return send(
+            tokens_ref.at[peer * mine + frame],
+            x_ref.at[frame, pl.ds(pl.multiple_of(me * stripe, stripe), stripe), :],
+            x_send.at[frame, step], x_recv.at[frame, step], peer,
+        )
+
+    def x_keep(frame):
+        return pltpu.make_async_copy(
+            tokens_ref.at[me * mine + frame],
+            x_ref.at[frame, pl.ds(pl.multiple_of(me * stripe, stripe), stripe), :],
+            x_own.at[frame],
+        )
+
+    def saves(frame):
+        return [
+            pltpu.make_async_copy(held.at[frame], kept.at[frame], save_sem.at[place, frame])
+            for place, (held, kept) in enumerate(
+                ((x_ref, x_out), (q_ref, q_out), (k_ref, k_out), (v_ref, v_out), (attn_ref, attn_out))
+            )
+        ]
+
+    def a_copy(frame, pair, peer):
+        lanes = pl.ds(pl.multiple_of(pair * 2 * HEAD_DIM, 2 * HEAD_DIM), 2 * HEAD_DIM)
+        return send(
+            attn_ref.at[frame, pl.ds(pl.multiple_of(peer * stripe, stripe), stripe), lanes],
+            patches_out.at[me * mine + frame, :, lanes],
+            a_send.at[frame, pair, peer], a_recv.at[frame, pair, me], peer,
+        )
+
+    def a_landed(frame, pair, peer):
+        lanes = pl.ds(pl.multiple_of(pair * 2 * HEAD_DIM, 2 * HEAD_DIM), 2 * HEAD_DIM)
+        return send(
+            attn_ref.at[frame, pl.ds(pl.multiple_of(peer * stripe, stripe), stripe), lanes],
+            patches_out.at[peer * mine + frame, :, lanes],
+            a_send.at[frame, pair, peer], a_recv.at[frame, pair, peer], peer,
+        )
+
+    def a_keep(frame, pair):
+        lanes = pl.ds(pl.multiple_of(pair * 2 * HEAD_DIM, 2 * HEAD_DIM), 2 * HEAD_DIM)
+        return pltpu.make_async_copy(
+            attn_ref.at[frame, pl.ds(pl.multiple_of(me * stripe, stripe), stripe), lanes],
+            patches_out.at[me * mine + frame, :, lanes],
+            a_own.at[frame, pair],
+        )
+
+    greet(peers)
+    greeted(peers)
+    order = sorted(range(1, count), key=lambda step: -min(step, count - step))
+    for frame in range(mine):
+        for step in order:
+            x_copy(frame, step, lax.rem(me + step, count)).start()
+        x_keep(frame).start()
+    turned_ref[:, HEAD_DIM:, :] = jnp.ones((2 * pairs, turned_ref.shape[1] - HEAD_DIM, tokens), MXB)
+
+    def one_frame(frame, carry):
+        x_keep(frame).wait()
+        for step, _, source in peers:
+            x_copy(frame, step, source).wait_recv()
+        saves(frame)[0].start()
+
+        def project(index, carry):
+            at = pl.ds(pl.multiple_of(index * rows, rows), rows)
+            normed, _ = normalise(x_ref[frame, at, :].astype(F32))
+            hidden = (normed * (1.0 + scale) + shift).astype(MXB)
+            mixed = dot(hidden, proj_ref[...]) + bias_ref[...]
+            q_ref[frame, at, :] = mixed[:, :width].astype(MXB)
+            k_ref[frame, at, :] = mixed[:, width : 2 * width].astype(MXB)
+            value = mixed[:, 2 * width :].astype(MXB)
+            v_ref[frame, at, :] = value
+            across = turned(value)
+            for head in range(2 * pairs):
+                turned_ref[head, :HEAD_DIM, at] = across[head * HEAD_DIM : (head + 1) * HEAD_DIM]
+            return carry
+
+        lax.fori_loop(0, tokens // rows, project, 0)
+        for copy in saves(frame)[1:4]:
+            copy.start()
+
+        def attend_block(index, carry):
+            pair = lax.rem(index, pairs)
+            chunk = lax.rem(lax.div(index, pairs) + lax.div(me, near) + 1, blocks)
+            at = pl.ds(pl.multiple_of(chunk * block, block), block)
+            lanes = pl.ds(pl.multiple_of(pair * 2 * HEAD_DIM, 2 * HEAD_DIM), 2 * HEAD_DIM)
+            scores = []
+            tops = []
+            for query in halves(q_ref[frame, at, lanes] * MXB(HEAD_DIM**-0.5)):
+                each = [
+                    dot_nt(k_ref[frame, first : first + part, lanes], query)
+                    for first in range(0, tokens, part)
+                ]
+                top = [jnp.max(s.reshape(part // 8, 8, block), axis=0) for s in each]
+                scores.append(each)
+                tops.append(jnp.max(reduce(jnp.maximum, top), axis=0, keepdims=True))
+            mixed = []
+            for half in range(2):
+                total = jnp.zeros((turned_ref.shape[1], block), F32)
+                for number, s in enumerate(scores[half]):
+                    weights = jnp.exp(s - tops[half]).astype(MXB)
+                    values = turned_ref[2 * pair + half, :, number * part : (number + 1) * part]
+                    total = total + dot(values, weights)
+                mass = total[HEAD_DIM : HEAD_DIM + 1]
+                log_ref[frame, pair, half : half + 1, at] = tops[half] + jnp.log(mass)
+                mixed.append(total[:HEAD_DIM] / mass)
+            attn_ref[frame, at, lanes] = jnp.concatenate(mixed, axis=0).T.astype(MXB)
+            for place in range(near):
+                peer = chunk * near + place
+
+                @pl.when(peer != me)
+                def _():
+                    a_copy(frame, pair, peer).start()
+
+                @pl.when(peer == me)
+                def _():
+                    a_keep(frame, pair).start()
+
+            return carry
+
+        lax.fori_loop(0, pairs * blocks, attend_block, 0)
+        saves(frame)[4].start()
+        return carry
+
+    lax.fori_loop(0, mine, one_frame, 0)
+
+    for frame in range(mine):
+        for copy in saves(frame):
+            copy.wait()
+        for step, peer, _ in peers:
+            x_copy(frame, step, peer).wait_send()
+        for pair in range(pairs):
+            a_keep(frame, pair).wait()
+            for _, peer, _ in peers:
+                a_copy(frame, pair, peer).wait_send()
+                a_landed(frame, pair, peer).wait_recv()
+
+
+def spatial_backward(
+    da_ref, attn_ref, q_ref, k_ref, v_ref, log_ref, x_ref, modes_ref, proj_turned_ref,
+    patches_out, grad_proj_ref, sums_ref, bias_sums_ref,
+    dx_ref, mix_ref, delta_ref, dk_ref, dv_ref, send_sem, recv_sem, own_sem, rows, block, part, count,
 ):
     tokens, width = x_ref.shape[1:]
-    pairs = width // (2 * HEAD_DIM)
-    shift = modes_ref[0:1, :]
-    scale = modes_ref[1:2, :]
-
-    def project(index, carry):
-        at = pl.ds(pl.multiple_of(index * rows, rows), rows)
-        normed, _ = normalise(x_ref[0, at, :].astype(F32))
-        hidden = (normed * (1.0 + scale) + shift).astype(MXB)
-        mixed = dot(hidden, proj_ref[...]) + bias_ref[...]
-        q_ref[0, at, :] = mixed[:, :width].astype(MXB)
-        k_ref[0, at, :] = mixed[:, width : 2 * width].astype(MXB)
-        value = mixed[:, 2 * width :].astype(MXB)
-        v_ref[0, at, :] = value
-        across = turned(value)
-        for head in range(2 * pairs):
-            turned_ref[head, :HEAD_DIM, at] = across[head * HEAD_DIM : (head + 1) * HEAD_DIM]
-        return carry
-
-    turned_ref[:, HEAD_DIM:, :] = jnp.ones((2 * pairs, turned_ref.shape[1] - HEAD_DIM, tokens), MXB)
-    lax.fori_loop(0, tokens // rows, project, 0)
-
-    def attend_block(index, carry):
-        pair = lax.rem(index, pairs)
-        at = pl.ds(pl.multiple_of(lax.div(index, pairs) * block, block), block)
-        lanes = pl.ds(pl.multiple_of(pair * 2 * HEAD_DIM, 2 * HEAD_DIM), 2 * HEAD_DIM)
-        scores = []
-        tops = []
-        for query in halves(q_ref[0, at, lanes] * MXB(HEAD_DIM**-0.5)):
-            each = [
-                dot_nt(k_ref[0, first : first + part, lanes], query) for first in range(0, tokens, part)
-            ]
-            top = [jnp.max(s.reshape(part // 8, 8, block), axis=0) for s in each]
-            scores.append(each)
-            tops.append(jnp.max(reduce(jnp.maximum, top), axis=0, keepdims=True))
-        mixed = []
-        for half in range(2):
-            total = jnp.zeros((turned_ref.shape[1], block), F32)
-            for number, s in enumerate(scores[half]):
-                weights = jnp.exp(s - tops[half]).astype(MXB)
-                values = turned_ref[2 * pair + half, :, number * part : (number + 1) * part]
-                total = total + dot(values, weights)
-            mass = total[HEAD_DIM : HEAD_DIM + 1]
-            log_ref[0, pair, half : half + 1, at] = tops[half] + jnp.log(mass)
-            mixed.append(total[:HEAD_DIM] / mass)
-        attn_ref[0, at, lanes] = jnp.concatenate(mixed, axis=0).T.astype(MXB)
-        return carry
-
-    lax.fori_loop(0, pairs * (tokens // block), attend_block, 0)
-
-
-def spatial_backward(
-    da_ref, attn_ref, q_ref, k_ref, v_ref, log_ref, x_ref, modes_ref, proj_turned_ref,
-    dx_ref, grad_proj_ref, sums_ref, bias_sums_ref,
-    mix_ref, delta_ref, dk_ref, dv_ref, rows, block, part,
-):
-    tokens, width = x_ref.shape[1:]
+    mine = dx_ref.shape[0]
+    stripe = tokens // count
+    frame = pl.program_id(0)
+    me, peers = others(count)
+
+    def dx_copy(frame, peer):
+        return send(
+            dx_ref.at[frame, pl.ds(pl.multiple_of(peer * stripe, stripe), stripe), :],
+            patches_out.at[me * mine + frame], send_sem.at[frame, peer], recv_sem.at[frame, me], peer,
+        )
+
+    def dx_landed(frame, peer):
+        return send(
+            dx_ref.at[frame, pl.ds(pl.multiple_of(peer * stripe, stripe), stripe), :],
+            patches_out.at[peer * mine + frame], send_sem.at[frame, peer], recv_sem.at[frame, peer], peer,
+        )
+
+    def dx_keep(frame):
+        return pltpu.make_async_copy(
+            dx_ref.at[frame, pl.ds(pl.multiple_of(me * stripe, stripe), stripe), :],
+            patches_out.at[me * mine + frame], own_sem.at[frame],
+        )
+
+    @pl.when(frame == 0)
+    def _():
+        greet(peers)
+
     pairs = width // (2 * HEAD_DIM)
     scale_factor = HEAD_DIM**-0.5
 
-    @pl.when(pl.program_id(0) == 0)
+    @pl.when(frame == 0)
     def _():
         grad_proj_ref[...] = jnp.zeros_like(grad_proj_ref)
         sums_ref[...] = jnp.zeros_like(sums_ref)
@@ -553,8 +700,13 @@
     shift = modes_ref[0:1, :]
     scale = modes_ref[1:2, :]
 
+    @pl.when(frame == 0)
+    def _():
+        greeted(peers)
+
     def finish(index, carry):
-        at = pl.ds(pl.multiple_of(index * rows, rows), rows)
+        peer = lax.rem(me + count // 2 + index, count)
+        at = pl.ds(pl.multiple_of(peer * stripe, stripe), stripe)
         normed, rate = normalise(x_ref[0, at, :].astype(F32))
         hidden = (normed * (1.0 + scale) + shift).astype(MXB)
         grad_mix = mix_ref[at, :]
@@ -563,26 +715,69 @@
         grad_hidden = dot(grad_mix, proj_turned_ref[...])
         sums_ref[0] += eight_rows(grad_hidden)
         sums_ref[1] += eight_rows(grad_hidden * normed)
-        dx_ref[0, at, :] = normalise_back(grad_hidden, normed, rate, scale).astype(MXB)
+        dx_ref[frame, at, :] = normalise_back(grad_hidden, normed, rate, scale).astype(MXB)
+
+        @pl.when(peer != me)
+        def _():
+            dx_copy(frame, peer).start()
+
+        @pl.when(peer == me)
+        def _():
+            dx_keep(frame).start()
+
         return carry
 
-    lax.fori_loop(0, tokens // rows, finish, 0)
+    lax.fori_loop(0, count, finish, 0)
+
+    @pl.when(frame == mine - 1)
+    def _():
+        for each in range(mine):
+            dx_keep(each).wait()
+            for _, peer, _ in peers:
+                dx_copy(each, peer).wait_send()
+                dx_landed(each, peer).wait_recv()
 
 
 def middle(
     x_ref, attn_ref, og_ref, weight_ref, modes_ref, mask_ref,
     so_ref, so_turned_ref, so_bias_ref, t_ref, t_turned_ref, t_bias_ref, to_ref, to_turned_ref, to_bias_ref,
     in_ref, in_turned_ref, in_bias_ref, out_ref, out_turned_ref, out_bias_ref,
-    block_ref, g1_ref, da_ref,
+    block_ref, g1_ref, da_out,
     grad_so_ref, grad_t_ref, grad_to_ref, grad_in_ref, grad_out_ref, sums_ref, t_sums_ref, in_sums_ref,
+    da_ref, send_sem, recv_sem, own_sem, peer_count,
 ):
     frames, tile, width = x_ref.shape
     count = frames * tile
     pairs = width // (2 * HEAD_DIM)
     scale_factor = HEAD_DIM**-0.5
-
-    @pl.when(pl.program_id(0) == 0)
+    mine = frames // peer_count
+    steps = pl.num_programs(0)
+    stripe = da_out.shape[1] // peer_count
+    at_step = pl.program_id(0)
+    me, peers = others(peer_count)
+
+    def da_copy(at_step, step, peer):
+        first = pl.multiple_of(me * stripe + at_step * tile, tile)
+        slot = lax.rem(at_step, 2)
+        return send(
+            da_ref.at[slot, pl.ds(peer * mine, mine)], da_out.at[:, pl.ds(first, tile), :],
+            send_sem.at[slot, step], recv_sem.at[step], peer,
+        )
+
+    def da_keep(at_step):
+        first = pl.multiple_of(me * stripe + at_step * tile, tile)
+        slot = lax.rem(at_step, 2)
+        return pltpu.make_async_copy(
+            da_ref.at[slot, pl.ds(me * mine, mine)], da_out.at[:, pl.ds(first, tile), :], own_sem.at[slot]
+        )
+
+    def da_landed(step, source):
+        rows = da_out.at[:, pl.ds(pl.multiple_of(source * stripe, stripe), stripe), :]
+        return send(rows, rows, send_sem.at[0, step], recv_sem.at[step], source)
+
+    @pl.when(at_step == 0)
     def _():
+        greet(peers)
         for ref in (grad_so_ref, grad_t_ref, grad_to_ref, grad_in_ref, grad_out_ref, sums_ref, t_sums_ref, in_sums_ref):
             ref[...] = jnp.zeros_like(ref)
 
@@ -688,7 +883,35 @@
     grad_so_ref[...] += dot_tn(attn_one, grad_branch)
     sums_ref[9] += eight_rows(grad_branch.astype(F32))
     g1_ref[...] = grad_field.reshape(frames, tile, width)
-    da_ref[...] = dot(grad_branch, so_turned_ref[...]).astype(MXB).reshape(frames, tile, width)
+    grad_attn = dot(grad_branch, so_turned_ref[...]).astype(MXB).reshape(frames, tile, width)
+
+    @pl.when(at_step == 0)
+    def _():
+        greeted(peers)
+
+    def sent(at_step):
+        da_keep(at_step).wait()
+        for step, peer, _ in peers:
+            da_copy(at_step, step, peer).wait_send()
+
+    @pl.when(at_step >= 2)
+    def _():
+        sent(at_step - 2)
+
+    da_ref[lax.rem(at_step, 2)] = grad_attn
+    da_keep(at_step).start()
+    for step, peer, _ in peers:
+        da_copy(at_step, step, peer).start()
+
+    @pl.when(at_step == steps - 1)
+    def _():
+        @pl.when(steps > 1)
+        def _():
+            sent(steps - 2)
+
+        sent(steps - 1)
+        for step, _, source in peers:
+            da_landed(step, source).wait_recv()
 
 
 def whole_spec(shape):
@@ -701,8 +924,16 @@
     return pl.BlockSpec(shape, lambda *_: (0,) * rank)
 
 
-def params():
-    return pltpu.CompilerParams(vmem_limit_bytes=VMEM_BYTES)
+def params(number):
+    return pltpu.CompilerParams(vmem_limit_bytes=VMEM_BYTES, collective_id=number, has_side_effects=True)
+
+
+def any_spec():
+    return pl.BlockSpec(memory_space=pl.ANY)
+
+
+def cost(flops, moved):
+    return pl.CostEstimate(flops=flops, bytes_accessed=moved, transcendentals=0)
 
 
 def fast_body(
@@ -716,36 +947,32 @@
     cond_act = jax.nn.silu(conditioning.astype(F32)).astype(MXB)
     modes = (jnp.dot(cond_act, ada_weight, preferred_element_type=F32) + ada_bias).reshape(9, width)
 
-    def to_frames(array):
-        return lax.all_to_all(array, "sp", split_axis=0, concat_axis=1, tiled=True)
-
-    def to_patches(array):
-        return lax.all_to_all(array, "sp", split_axis=1, concat_axis=0, tiled=True)
-
     def widen(bias):
         return jnp.concatenate([bias[:width], jnp.zeros((width,), F32), bias[width:]])[None, :]
 
     x_patches = tokens[0]
-    x_frames = to_frames(x_patches)
-    mine, patches = x_frames.shape[:2]
-    frame_spec = pl.BlockSpec((1, patches, width), lambda f: (f, 0, 0))
-    log_spec = pl.BlockSpec((1, pairs, 2, patches), lambda f: (f, 0, 0, 0))
+    count = lax.axis_size("sp")
+    mine, patches = frames // count, stripe * count
+    block = min(1024, patches)
     frame_shape = jax.ShapeDtypeStruct((mine, patches, width), MXB)
-    queries, keys, values, attn_frames, logs = pl.pallas_call(
-        partial(spatial_forward, rows=256, block=min(1024, patches), part=512),
-        grid=(mine,),
-        in_specs=[frame_spec, whole_spec((9, width)), whole_spec((width, 3 * width)), whole_spec((1, 3 * width))],
-        out_specs=[frame_spec] * 4 + [log_spec],
-        out_shape=[frame_shape] * 4 + [jax.ShapeDtypeStruct((mine, pairs, 2, patches), F32)],
-        scratch_shapes=[pltpu.VMEM((2 * pairs, HEAD_DIM + 16, patches), MXB)],
-        compiler_params=params(),
-    )(x_frames, modes, spatial_proj, widen(spatial_bias))
-    attn_patches = to_patches(attn_frames)
+    patch_shape = jax.ShapeDtypeStruct((frames, stripe, width), MXB)
+    dma = pltpu.SemaphoreType.DMA
+    x_frames, queries, keys, values, attn_frames, attn_patches, logs = pl.pallas_call(
+        partial(spatial_forward, rows=256, block=block, part=512, count=count),
+        in_specs=[any_spec()] + [pl.BlockSpec(memory_space=pltpu.VMEM)] * 3,
+        out_specs=[any_spec()] * 6 + [pl.BlockSpec(memory_space=pltpu.VMEM)],
+        out_shape=[frame_shape] * 5 + [patch_shape, jax.ShapeDtypeStruct((mine, pairs, 2, patches), F32)],
+        scratch_shapes=[pltpu.VMEM((mine, patches, width), MXB)] * 5
+        + [pltpu.VMEM((2 * pairs, HEAD_DIM + 16, patches), MXB)]
+        + [dma((mine, count)), dma((mine, count)), dma((mine,))]
+        + [dma((mine, pairs, count)), dma((mine, pairs, count)), dma((mine, pairs)), dma((5, mine))],
+        compiler_params=params(0),
+        cost_estimate=cost(10**11, 10**7),
+    )(x_patches, modes, spatial_proj, widen(spatial_bias))
 
     slope = jnp.tan((timesteps.astype(F32) / TSTEPS + 0.008) / 1.008 * (0.5 * math.pi))
     loss_weight = jnp.minimum(1.0, 5.0 * slope * slope).reshape(1, 1)
-    count = frames * TILE
-    place = jnp.arange(count) % TILE
+    place = jnp.arange(frames * TILE) % TILE
     mask = jnp.where(place[:, None] == place[None, :], 0.0, -1e30).astype(F32)
     tile_spec = pl.BlockSpec((frames, TILE, width), lambda i: (0, i, 0))
     small = (
@@ -761,38 +988,45 @@
         (12, 8, width), (8, 3 * width), (8, hidden),
     ]
     out_shapes = [
-        jax.ShapeDtypeStruct((frames, stripe, width), MXB),
+        patch_shape,
         jax.ShapeDtypeStruct((frames, stripe, width), F32),
-        jax.ShapeDtypeStruct((frames, stripe, width), MXB),
+        frame_shape,
     ] + [jax.ShapeDtypeStruct(s, F32) for s in sums_shapes]
     (
-        block_out, g1, da_patches, grad_so, grad_t, grad_to, grad_in, grad_out_turned, sums, t_sums, in_sums,
+        block_out, g1, da_frames, grad_so, grad_t, grad_to, grad_in, grad_out_turned, sums, t_sums, in_sums,
     ) = pl.pallas_call(
-        middle,
+        partial(middle, peer_count=count),
         grid=(stripe // TILE,),
         in_specs=[tile_spec] * 3 + [whole_spec(a.shape) for a in small],
-        out_specs=[tile_spec] * 3 + [acc_spec(s) for s in sums_shapes],
+        out_specs=[tile_spec] * 2 + [any_spec()] + [acc_spec(s) for s in sums_shapes],
         out_shape=out_shapes,
-        compiler_params=params(),
+        scratch_shapes=[pltpu.VMEM((2, frames, TILE, width), MXB), dma((2, count)), dma((count,)), dma((2,))],
+        compiler_params=params(1),
+        cost_estimate=cost(10**11, 10**7),
     )(x_patches, attn_patches, out_grad[0], *small)
-    da_frames = to_frames(da_patches)
-
+    frame_spec = pl.BlockSpec((1, patches, width), lambda f: (f, 0, 0))
+    log_spec = pl.BlockSpec((1, pairs, 2, patches), lambda f: (f, 0, 0, 0))
     sum_shapes = [(width, 3 * width), (2, 8, width), (8, 3 * width)]
-    dx_frames, grad_sp, sp_sums, sp_bias_sums = pl.pallas_call(
-        partial(spatial_backward, rows=256, block=min(1024, patches), part=512),
+    dx_patches, grad_sp, sp_sums, sp_bias_sums = pl.pallas_call(
+        partial(spatial_backward, rows=256, block=block, part=512, count=count),
         grid=(mine,),
         in_specs=[frame_spec] * 5 + [log_spec, frame_spec, whole_spec((9, width)), whole_spec((3 * width, width))],
-        out_specs=[frame_spec] + [acc_spec(s) for s in sum_shapes],
-        out_shape=[frame_shape] + [jax.ShapeDtypeStruct(s, F32) for s in sum_shapes],
+        out_specs=[any_spec()] + [acc_spec(s) for s in sum_shapes],
+        out_shape=[patch_shape] + [jax.ShapeDtypeStruct(s, F32) for s in sum_shapes],
         scratch_shapes=[
+            pltpu.VMEM((mine, patches, width), MXB),
             pltpu.VMEM((patches, 3 * width), MXB),
             pltpu.VMEM((pairs, 2, patches), F32),
             pltpu.VMEM((patches, 2 * HEAD_DIM), F32),
             pltpu.VMEM((patches, 2 * HEAD_DIM), F32),
+            dma((mine, count)),
+            dma((mine, count)),
+            dma((mine,)),
         ],
-        compiler_params=params(),
+        compiler_params=params(2),
+        cost_estimate=cost(2 * 10**11, 10**7),
     )(da_frames, attn_frames, queries, keys, values, logs, x_frames, modes, spatial_proj.T)
-    input_grad = (g1 + to_patches(dx_frames).astype(F32)).astype(MXB)
+    input_grad = (g1 + dx_patches.astype(F32)).astype(MXB)
 
     clip_at = lax.axis_index("clip")
     clips = lax.axis_size("clip")
@@ -802,6 +1036,7 @@
     mine_only = (jnp.arange(clips) == clip_at)[:, None]
     first_on_sp = (lax.axis_index("sp") == 0).astype(F32)
     early = lax.psum((grad_so, grad_t, grad_to, grad_in, grad_out_turned), ("clip", "sp"))
+    early, grad_sp, sp_bias_sums = lax.optimization_barrier((early, grad_sp, sp_bias_sums))
     sp_bias = jnp.sum(sp_bias_sums, axis=0)
     t_bias = jnp.sum(t_sums, axis=0)
     pieces = (

time: 996 us -> 739 us (0.74)
  waiting for transfers between devices: 449 us -> 124 us
  Pallas kernels: 432 us -> 542 us
  local copies, waits for them, and re-layouts: 55.9 us -> 32 us
  starting transfers between devices: 20.7 us -> 0.08 us
    all_to_all x4 -> x0, waiting for transfers between devices: 201 us -> none  [the longest x2 140 us: to_frames(): return lax.all_to_all(array, 'sp', split_axis=0, concat_axis=1, tiled=True)]
    psum x1, waiting for transfers between devices: 248 us -> 124 us  [fast_body(): flat, grad_sp = lax.psum((flat, grad_sp), ('clip', 'sp'))]
    pallas_call x3, Pallas kernels: 432 us -> 542 us  [the longest x1 226 us: fast_body(): pl.pallas_call(partial(spatial_backward, rows=256, block=block, part=512,...]
    all_to_all x4 -> x0, starting transfers between devices: 20.7 us -> none  [the longest x2 11.2 us: to_frames(): return lax.all_to_all(array, 'sp', split_axis=0, concat_axis=1, tiled=True)]
    pallas_call x2 -> x0, local copies, waits for them, and re-layouts: 16 us -> none  [the longest x1 8.03 us: fast_body(): pl.pallas_call(partial(spatial_backward, rows=256, block=min(1024, patche...]
    all_to_all x3 -> x0, local copies, waits for them, and re-layouts: 12.1 us -> none  [the longest x2 7.95 us: to_frames(): return lax.all_to_all(array, 'sp', split_axis=0, concat_axis=1, tiled=True)]
    unnamed x67 -> x62, local copies, waits for them, and re-layouts: 16.9 us -> 22.9 us
  transfers between devices with their start and end apart: 5 -> 2, of which waited for: 4 -> 1; matrix products, arithmetic and copies ran while one was open for 4% -> 1% of each run, Pallas kernels for 0% -> 31%
where the time goes in v2:
time: 739 us; the launch traced here: 733 us
  Pallas kernels  542 us (73%)
  waiting for transfers between devices  124 us (17%)
  local copies, waits for them, and re-layouts  32 us (4%)
  between operations  15.3 us (2%)
  other arithmetic  11.7 us (2%)
    pallas_call x1, Pallas kernels, fast_body(): pl.pallas_call(partial(spatial_backward, rows=256, block=block, part=512,...  226 us
    pallas_call x1, Pallas kernels, fast_body(): pl.pallas_call(partial(middle, peer_count=count), grid=(stripe // TILE,),...  174 us
    pallas_call x1, Pallas kernels, fast_body(): pl.pallas_call(partial(spatial_forward, rows=256, block=block, part=512,...  142 us
    psum x1, waiting for transfers between devices, fast_body(): flat, grad_sp = lax.psum((flat, grad_sp), ('clip', 'sp'))  124 us
    unnamed x62, local copies, waits for them, and re-layouts  22.9 us
  transfers between devices with their start and end apart: 2, of which 1 were waited for; matrix products, arithmetic and copies ran while one was open for 1% of the time, Pallas kernels for 31%

profile of v2, /device:TPU:0, one launch (start us, length us, event | category | flops | bytes accessed | tf_op | source)
XLA Modules:
  0.0 732.6 jit_solution(5400607910142794466)
XLA Ops:
  7.3 1.7 copy-done
  8.9 1.2 convolution_reduce_fusion
  10.1 0.9 add.43
  11.6 0.8 fusion.7
  13.7 0.8 compare_select_fusion.mask_ref
  14.6 1.8 copy.41
  17.0 1.3 copy.42
  18.9 1.8 copy.43
  21.3 1.4 copy.44
  23.3 1.4 copy.45
  25.3 142.4 %shard_map.297 = (bf16[2,2048,384]{2,1,0:T(8,128)(2,1)}, bf16[2,2048,384]{2,1,0:T(8,128)(2,1)}, bf16[2,2048,384]{2,1,0:T(8,128)(2,1)}, bf16[2,2048,384]{2,1,0:T(...) custom-call(bf16[16,256,384]{2,1,0:T(8,128)(2,1)} %bitcast.27, ...), custom_call_target="tpu_custom_call" | custom-call | flops 99999997952 | bytes 10000000 | tf_op jit(solution)/shard_map/pallas_call | solution.py:960
  168.2 174.2 %shard_map.298 = (bf16[16,256,384]{2,1,0:T(8,128)(2,1)}, f32[16,256,384]{2,1,0:T(8,128)}, bf16[2,2048,384]{2,1,0:T(8,128)(2,1)}, f32[384,384]{1,0:T(8,128)}, f32...) custom-call(bf16[16,256,384]{2,1,0:T(8,128)(2,1)} %bitcast.28, ...), custom_call_target="tpu_custom_call" | custom-call | flops 99999997952 | bytes 10000000 | tf_op jit(solution)/shard_map/pallas_call | solution.py:997
  342.6 1.1 copy-done.10
  343.7 1.3 copy.46
  345.0 225.8 %shard_map.299 = (bf16[16,256,384]{2,1,0:T(8,128)(2,1)}, f32[384,1152]{1,0:T(8,128)}, f32[2,8,384]{2,1,0:T(8,128)}, f32[8,1152]{1,0:T(8,128)}) custom-call(bf16[2,2048,384]{2,1,0:T(8,128)(2,1)} %get-tuple-element.48.da_ref, bf16[2,2048,384]{2,1,0:T(8,128)(2,1)} %get-tuple-element.49.attn_ref, bf16[2,2048,384]{2,1,0:T(8,128)(2,1)} %get-tuple-element.50.q_ref, ...), custom_call_target="tpu_custom_call" | custom-call | flops 199999995904 | bytes 10000000 | tf_op jit(solution)/shard_map/pallas_call | solution.py:1010
  570.9 0.8 reduce_sum.54
  572.1 0.8 reduce_sum.56
  573.6 6.3 fusion
  579.9 1.9 copy.47
  581.8 123.8 %all-reduce.5.cloned.1.call-done = (f32[20352]{0:T(1024)}, f32[384,1152]{1,0:T(8,128)}) async-done(((f32[20352]{0:T(1024)}, f32[384,1152]{1,0:T(8,128)}), (f32[20352]{0:T(1024)}, f32[384,1152]{1,0:T(8,128)})) %all-reduce.5.cloned.1.call-update) | async-done | bytes 1850896 | tf_op jit(solution)/shard_map/psum | solution.py:1051
  705.6 1.3 fusion.6
  706.9 0.8 slice.91
  707.7 1.4 fusion.5
  709.2 0.6 reduce_sum.59
  709.8 6.2 fusion.9
  717.2 1.7 copy.68
  718.9 0.9 copy-done.6
  719.8 1.2 copy.69
  721.3 0.8 copy.70
  722.2 1.2 copy.71
  723.4 0.8 copy.72
  724.2 1.4 copy.73
  (82 shorter events, 7.4 us)
Async XLA Ops:
  7.2 1.8 copy-start
  7.2 9.2 %copy-start.19 = (f32[384]{0:T(512)S(1)}, f32[384]{0:T(512)}, u32[]{:S(2)}) copy-start(f32[384]{0:T(512)} %param.27) | copy-start | bytes 4612
  7.2 9.8 %copy-start.9 = (bf16[384,1152]{1,0:T(8,128)(2,1)S(1)}, bf16[384,1152]{1,0:T(8,128)(2,1)}, u32[]{:S(2)}) copy-start(bf16[384,1152]{1,0:T(8,128)(2,1)} %t_ref.1) | copy-start | bytes 2654212
  7.2 13.5 %copy-start.20 = (f32[384]{0:T(512)S(1)}, f32[384]{0:T(512)}, u32[]{:S(2)}) copy-start(f32[384]{0:T(512)} %param.31) | copy-start | bytes 4612
  7.2 564.8 %all-reduce.7.cloned.1.call-start = ((), (), s32[]{:S(2)}) async-start(), calls=%async_computation.1 | async-start | bytes 15335424 | tf_op jit(solution)/shard_map/psum | solution.py:1038
  10.1 11.2 %copy-start.7 = (bf16[384,1536]{1,0:T(8,128)(2,1)S(1)}, bf16[384,1536]{1,0:T(8,128)(2,1)}, u32[]{:S(2)}) copy-start(bf16[384,1536]{1,0:T(8,128)(2,1)} %in_ref.1) | copy-start | bytes 3538948
  10.1 12.6 %copy-start.17 = (f32[1536]{0:T(1024)S(1)}, f32[1536]{0:T(1024)}, u32[]{:S(2)}) copy-start(f32[1536]{0:T(1024)} %param.33) | copy-start | bytes 18436
  10.1 13.2 %copy-start.8 = (bf16[1536,384]{1,0:T(8,128)(2,1)S(1)}, bf16[1536,384]{1,0:T(8,128)(2,1)}, u32[]{:S(2)}) copy-start(bf16[1536,384]{1,0:T(8,128)(2,1)} %out_ref.1) | copy-start | bytes 3538948
  17.0 7.8 %copy-start.21 = (f32[384]{0:T(512)S(1)}, f32[384]{0:T(512)}, u32[]{:S(2)}) copy-start(f32[384]{0:T(512)} %param.35) | copy-start | bytes 4612
  342.5 1.2 copy-start.10
  342.5 363.1 %all-reduce.5.cloned.1.call-start = ((), (), s32[]{:S(2)}) async-start(), calls=%async_computation | async-start | bytes 3702784 | tf_op jit(solution)/shard_map/psum | solution.py:1051
  345.0 225.8 %copy-start.13 = (f32[12,8,384]{2,1,0:T(8,128)S(1)}, f32[12,8,384]{2,1,0:T(8,128)}, u32[]{:S(2)}) copy-start(f32[12,8,384]{2,1,0:T(8,128)} %get-tuple-element.57) | copy-start | bytes 442372
  345.0 226.8 %copy-start.18 = (bf16[1,384]{1,0:T(2,128)(2,1)S(1)}, bf16[1,384]{1,0:T(2,128)(2,1)}, u32[]{:S(2)}) copy-start(bf16[1,384]{1,0:T(2,128)(2,1)} %param.19) | copy-start | bytes 2308
  345.0 227.0 %copy-start.16 = (f32[8,1152]{1,0:T(8,128)S(1)}, f32[8,1152]{1,0:T(8,128)}, u32[]{:S(2)}) copy-start(f32[8,1152]{1,0:T(8,128)} %get-tuple-element.66) | copy-start | bytes 110596
  345.0 227.0 %copy-start.15 = (f32[8,1536]{1,0:T(8,128)S(1)}, f32[8,1536]{1,0:T(8,128)}, u32[]{:S(2)}) copy-start(f32[8,1536]{1,0:T(8,128)} %get-tuple-element.67) | copy-start | bytes 147460
  572.9 0.6 copy-start.14
  573.6 6.3 copy-start.4
  581.8 135.4 %copy-start.2 = (bf16[16,256,384]{2,1,0:T(8,128)(2,1)S(1)}, bf16[16,256,384]{2,1,0:T(8,128)(2,1)}, u32[]{:S(2)}) copy-start(bf16[16,256,384]{2,1,0:T(8,128)(2,1)} %get-tuple-element.46) | copy-start | bytes 9437188
  717.2 2.6 copy-start.6
  719.8 1.4 copy-start.12
  719.8 2.3 copy-start.5
  721.3 2.1 copy-start.11
  721.3 2.9 copy-start.3
  722.2 3.4 copy-start.1
Sparse Core Ops, SparseCore 0:
  342.6 204.9 all-reduce.6
  573.7 131.8 all-reduce.4

commit v3 on v2

--- a/solution.py
+++ b/solution.py
@@ -13,6 +13,15 @@
 FRAME_BLOCK = 8
 TSTEPS = 1000
 GELU_RATE = math.sqrt(2.0 / math.pi)
+SP_BIAS = 9
+T_BIAS = 12
+SO_BIAS = 15
+TO_BIAS = 16
+OUT_BIAS = 17
+IN_BIAS = 18
+WEIGHT = 22
+COND = 23
+ROWS = 24
 
 
 def modulate(field, shift, scale):
@@ -380,7 +389,8 @@
 
 MXB = jnp.bfloat16
 F32 = jnp.float32
-TILE = 16
+TILE = 32
+GROUP = 8
 VMEM_BYTES = 60 * 2**20
 
 
@@ -417,6 +427,10 @@
     return jnp.sum(array.reshape(array.shape[0] // 8, 8, array.shape[1]), axis=0)
 
 
+def wide(ref, first, rows):
+    return jnp.concatenate([ref[first + row : first + row + 1, :] for row in range(rows)], axis=1)
+
+
 def low_lanes():
     return lax.broadcasted_iota(jnp.int32, (1, 2 * HEAD_DIM), 1) < HEAD_DIM
 
@@ -427,22 +441,22 @@
     return jnp.where(low, pair, zero), jnp.where(low, zero, pair)
 
 
-def others(count):
-    me = lax.axis_index("sp")
+def others(count, axis="sp"):
+    me = lax.axis_index(axis)
     return me, [(step, lax.rem(me + step, count), lax.rem(me + count - step, count)) for step in range(1, count)]
 
 
-def send(source, target, send_sem, recv_sem, peer):
+def send(source, target, send_sem, recv_sem, peer, axis="sp"):
     return pltpu.make_async_remote_copy(
         src_ref=source, dst_ref=target, send_sem=send_sem, recv_sem=recv_sem,
-        device_id={"sp": peer}, device_id_type=pl.DeviceIdType.MESH,
-    )
-
-
-def greet(peers):
+        device_id={axis: peer}, device_id_type=pl.DeviceIdType.MESH,
+    )
+
+
+def greet(peers, axis="sp"):
     barrier = pltpu.get_barrier_semaphore()
     for _, peer, _ in peers:
-        pl.semaphore_signal(barrier, inc=1, device_id={"sp": peer}, device_id_type=pl.DeviceIdType.MESH)
+        pl.semaphore_signal(barrier, inc=1, device_id={axis: peer}, device_id_type=pl.DeviceIdType.MESH)
 
 
 def greeted(peers):
@@ -450,7 +464,7 @@
 
 
 def spatial_forward(
-    tokens_ref, modes_ref, proj_ref, bias_ref,
+    tokens_ref, modes_ref, proj_ref,
     x_out, q_out, k_out, v_out, attn_out, patches_out, log_ref,
     x_ref, q_ref, k_ref, v_ref, attn_ref, turned_ref,
     x_send, x_recv, x_own, a_send, a_recv, a_own, save_sem,
@@ -464,6 +478,7 @@
     me, peers = others(count)
     shift = modes_ref[0:1, :]
     scale = modes_ref[1:2, :]
+    bias = wide(modes_ref, SP_BIAS, 3)
 
     def x_copy(frame, step, peer):
         return send(
@@ -530,7 +545,7 @@
             at = pl.ds(pl.multiple_of(index * rows, rows), rows)
             normed, _ = normalise(x_ref[frame, at, :].astype(F32))
             hidden = (normed * (1.0 + scale) + shift).astype(MXB)
-            mixed = dot(hidden, proj_ref[...]) + bias_ref[...]
+            mixed = dot(hidden, proj_ref[...]) + bias
             q_ref[frame, at, :] = mixed[:, :width].astype(MXB)
             k_ref[frame, at, :] = mixed[:, width : 2 * width].astype(MXB)
             value = mixed[:, 2 * width :].astype(MXB)
@@ -602,15 +617,43 @@
 
 
 def spatial_backward(
-    da_ref, attn_ref, q_ref, k_ref, v_ref, log_ref, x_ref, modes_ref, proj_turned_ref,
-    patches_out, grad_proj_ref, sums_ref, bias_sums_ref,
-    dx_ref, mix_ref, delta_ref, dk_ref, dv_ref, send_sem, recv_sem, own_sem, rows, block, part, count,
+    da_ref, attn_ref, q_ref, k_ref, v_ref, log_ref, x_ref, modes_ref, proj_ref, mid_sums_ref, t_sums_ref, in_sums_ref,
+    patches_out, grad_proj_ref, ada_ref, total_ref,
+    dx_ref, mix_ref, delta_ref, dk_ref, dv_ref, sums_ref, bias_sums_ref,
+    clip_out_ref, clip_in_ref, unit_out_ref, unit_in_ref, piece_ref, all_ref, vec_ref, vec_in_ref, row_ref, row_in_ref,
+    send_sem, recv_sem, own_sem, g1_send, g1_recv, g2_send, g2_recv, g3_send, g3_recv, g4_send, g4_recv,
+    v1_send, v1_recv, v2_send, v2_recv, rows, block, part, count, clips,
 ):
     tokens, width = x_ref.shape[1:]
     mine = dx_ref.shape[0]
     stripe = tokens // count
     frame = pl.program_id(0)
     me, peers = others(count)
+    clip, clip_peers = others(clips, "clip")
+    span_rows = width // clips
+    unit = 16 * (-(-span_rows // (16 * count)))
+    owners = span_rows // unit
+
+    def g1_copy(peer, slot):
+        return send(
+            clip_out_ref.at[peer], clip_in_ref.at[slot], g1_send.at[peer], g1_recv.at[slot], peer, "clip"
+        )
+
+    def g2_copy(peer, slot):
+        return send(unit_out_ref.at[peer], unit_in_ref.at[slot], g2_send.at[peer], g2_recv.at[slot], peer)
+
+    def g3_copy(peer, slot):
+        part_rows = pl.ds(pl.multiple_of(slot * unit, unit), unit)
+        return send(piece_ref.at[part_rows, :], piece_ref.at[part_rows, :], g3_send.at[peer], g3_recv.at[slot], peer)
+
+    def g4_copy(peer, slot):
+        return send(piece_ref, all_ref.at[slot], g4_send.at[peer], g4_recv.at[slot], peer, "clip")
+
+    def v1_copy(peer, slot):
+        return send(vec_ref, vec_in_ref.at[slot], v1_send.at[peer], v1_recv.at[slot], peer)
+
+    def v2_copy(peer, slot):
+        return send(row_ref, row_in_ref.at[slot], v2_send.at[peer], v2_recv.at[slot], peer, "clip")
 
     def dx_copy(frame, peer):
         return send(
@@ -633,6 +676,7 @@
     @pl.when(frame == 0)
     def _():
         greet(peers)
+        greet(clip_peers, "clip")
 
     pairs = width // (2 * HEAD_DIM)
     scale_factor = HEAD_DIM**-0.5
@@ -702,17 +746,35 @@
 
     @pl.when(frame == 0)
     def _():
-        greeted(peers)
+        greeted(peers + clip_peers)
+
+    def hidden_of(at):
+        normed, rate = normalise(x_ref[0, at, :].astype(F32))
+        return normed, rate, (normed * (1.0 + scale) + shift).astype(MXB)
+
+    def weigh(index, carry):
+        at = pl.ds(pl.multiple_of(index * rows, rows), rows)
+        _, _, hidden = hidden_of(at)
+        grad_mix = mix_ref[at, :]
+        grad_proj_ref[...] += dot_tn(hidden, grad_mix)
+        bias_sums_ref[...] += eight_rows(grad_mix.astype(F32))
+        return carry
+
+    lax.fori_loop(0, tokens // rows, weigh, 0)
+    last = frame == mine - 1
+
+    @pl.when(last)
+    def _():
+        for each in range(clips):
+            clip_out_ref[each] = grad_proj_ref[each * span_rows : (each + 1) * span_rows, :].astype(MXB)
+        for _, peer, _ in clip_peers:
+            g1_copy(peer, clip).start()
 
     def finish(index, carry):
         peer = lax.rem(me + count // 2 + index, count)
         at = pl.ds(pl.multiple_of(peer * stripe, stripe), stripe)
-        normed, rate = normalise(x_ref[0, at, :].astype(F32))
-        hidden = (normed * (1.0 + scale) + shift).astype(MXB)
-        grad_mix = mix_ref[at, :]
-        grad_proj_ref[...] += dot_tn(hidden, grad_mix)
-        bias_sums_ref[...] += eight_rows(grad_mix.astype(F32))
-        grad_hidden = dot(grad_mix, proj_turned_ref[...])
+        normed, rate, _ = hidden_of(at)
+        grad_hidden = dot_nt(mix_ref[at, :], proj_ref[...])
         sums_ref[0] += eight_rows(grad_hidden)
         sums_ref[1] += eight_rows(grad_hidden * normed)
         dx_ref[frame, at, :] = normalise_back(grad_hidden, normed, rate, scale).astype(MXB)
@@ -727,10 +789,107 @@
 
         return carry
 
-    lax.fori_loop(0, count, finish, 0)
-
-    @pl.when(frame == mine - 1)
+    lax.fori_loop(0, count // 2, finish, 0)
+
+    @pl.when(last)
     def _():
+        total = grad_proj_ref[pl.ds(pl.multiple_of(clip * span_rows, span_rows), span_rows), :]
+        for _, _, source in clip_peers:
+            g1_copy(source, source).wait_recv()
+            total = total + clip_in_ref[source].astype(F32)
+        for owner in range(owners):
+            unit_out_ref[owner] = total[owner * unit : (owner + 1) * unit].astype(MXB)
+
+            @pl.when(owner != me)
+            def _():
+                g2_copy(owner, me).start()
+
+    lax.fori_loop(count // 2, count, finish, 0)
+
+    @pl.when(last)
+    def _():
+        def row_sum(array):
+            return jnp.sum(array, axis=0, keepdims=True)
+
+        def rows_of(array):
+            flat = row_sum(array)
+            return [flat[:, first : first + width] for first in range(0, flat.shape[1], width)]
+
+        lines = [row_sum(sums_ref[0]), row_sum(sums_ref[1])]
+        lines += [row_sum(mid_sums_ref[line]) for line in range(2, 9)]
+        lines += rows_of(bias_sums_ref[...]) + rows_of(t_sums_ref[...])
+        lines += [row_sum(mid_sums_ref[line]) for line in range(9, 12)]
+        lines += rows_of(in_sums_ref[...])
+        lines += [modes_ref[COND : COND + 1, :]] * (ROWS - len(lines))
+        vec_ref[...] = jnp.concatenate(lines, axis=0)
+        for _, peer, _ in peers:
+            v1_copy(peer, me).start()
+
+        @pl.when(me < owners)
+        def _():
+            total = unit_out_ref[me].astype(F32)
+            for _, _, source in peers:
+                g2_copy(me, source).wait_recv()
+                total = total + unit_in_ref[source].astype(F32)
+            piece_ref[pl.ds(pl.multiple_of(me * unit, unit), unit), :] = total.astype(MXB)
+            for _, peer, _ in peers:
+                g3_copy(peer, me).start()
+
+        total = vec_ref[...]
+        for _, _, source in peers:
+            v1_copy(source, source).wait_recv()
+            total = total + vec_in_ref[source]
+        at_row = lax.broadcasted_iota(jnp.int32, (ROWS, width), 0)
+        row_ref[...] = jnp.where(at_row < COND, total, vec_ref[...])
+        for _, peer, _ in clip_peers:
+            v2_copy(peer, clip).start()
+
+        for owner in range(owners):
+
+            @pl.when(owner != me)
+            def _():
+                g3_copy(owner, owner).wait_recv()
+
+        for _, peer, _ in clip_peers:
+            g4_copy(peer, clip).start()
+        grad_proj_ref[pl.ds(pl.multiple_of(clip * span_rows, span_rows), span_rows), :] = piece_ref[...].astype(F32)
+
+        row_in_ref[clip] = row_ref[...]
+        for _, _, source in clip_peers:
+            v2_copy(source, source).wait_recv()
+        total = row_in_ref[0]
+        for each in range(1, clips):
+            total = total + row_in_ref[each]
+        total_ref[...] = total
+        tall = [row_in_ref[each][ROWS - 8 :].T[:, 7:8] for each in range(clips)]
+        for block_at in range(9):
+            outer = tall[0] * row_in_ref[0, block_at : block_at + 1, :]
+            for each in range(1, clips):
+                outer = outer + tall[each] * row_in_ref[each, block_at : block_at + 1, :]
+            ada_ref[:, block_at * width : (block_at + 1) * width] = outer
+
+        for _, _, source in clip_peers:
+            g4_copy(source, source).wait_recv()
+            grad_proj_ref[pl.ds(pl.multiple_of(source * span_rows, span_rows), span_rows), :] = all_ref[source].astype(F32)
+
+        for _, peer, _ in clip_peers:
+            g1_copy(peer, clip).wait_send()
+            g4_copy(peer, clip).wait_send()
+            v2_copy(peer, clip).wait_send()
+        for _, peer, _ in peers:
+            v1_copy(peer, me).wait_send()
+
+        for owner in range(owners):
+
+            @pl.when(owner != me)
+            def _():
+                g2_copy(owner, me).wait_send()
+
+        @pl.when(me < owners)
+        def _():
+            for _, peer, _ in peers:
+                g3_copy(peer, me).wait_send()
+
         for each in range(mine):
             dx_keep(each).wait()
             for _, peer, _ in peers:
@@ -739,9 +898,7 @@
 
 
 def middle(
-    x_ref, attn_ref, og_ref, weight_ref, modes_ref, mask_ref,
-    so_ref, so_turned_ref, so_bias_ref, t_ref, t_turned_ref, t_bias_ref, to_ref, to_turned_ref, to_bias_ref,
-    in_ref, in_turned_ref, in_bias_ref, out_ref, out_turned_ref, out_bias_ref,
+    x_ref, attn_ref, og_ref, modes_ref, so_ref, t_ref, to_ref, in_ref, out_ref,
     block_ref, g1_ref, da_out,
     grad_so_ref, grad_t_ref, grad_to_ref, grad_in_ref, grad_out_ref, sums_ref, t_sums_ref, in_sums_ref,
     da_ref, send_sem, recv_sem, own_sem, peer_count,
@@ -784,58 +941,72 @@
     def mode(row):
         return modes_ref[row : row + 1, :]
 
-    field = x_ref[...].reshape(count, width).astype(F32)
-    attn_one = attn_ref[...].reshape(count, width)
-    branch_one = dot(attn_one, so_ref[...]) + so_bias_ref[...]
+    cell = frames * GROUP
+    groups = tile // GROUP
+
+    def gather(ref):
+        whole = ref[...].astype(F32)
+        return jnp.concatenate(
+            [whole[:, g * GROUP : (g + 1) * GROUP, :].reshape(cell, width) for g in range(groups)], axis=0
+        )
+
+    def scatter(value):
+        return jnp.concatenate(
+            [value[g * cell : (g + 1) * cell].reshape(frames, GROUP, width) for g in range(groups)], axis=1
+        )
+
+    field = gather(x_ref)
+    attn_one = gather(attn_ref).astype(MXB)
+    branch_one = dot(attn_one, so_ref[...]) + mode(SO_BIAS)
     field_one = field + mode(2) * branch_one
     normed_two, rate_two = normalise(field_one)
     hidden_two = (normed_two * (1.0 + mode(4)) + mode(3)).astype(MXB)
-    mixed = (dot(hidden_two, t_ref[...]) + t_bias_ref[...]).astype(MXB)
-    mask = mask_ref[...]
+    mixed = (dot(hidden_two, t_ref[...]) + wide(modes_ref, T_BIAS, 3)).astype(MXB)
+    row_at = lax.broadcasted_iota(jnp.int32, (cell, 2 * cell), 0)
+    lane_at = lax.broadcasted_iota(jnp.int32, (cell, 2 * cell), 1)
+    mask = jnp.where(lax.rem(row_at, GROUP) == lax.rem(lane_at, GROUP), 0.0, -1e30).astype(F32)
     exact = []
     rounded = []
     queries = []
-    keys_across = []
-    attn_parts = []
-    for pair in range(pairs):
-        lanes = slice(2 * HEAD_DIM * pair, 2 * HEAD_DIM * (pair + 1))
-        query = halves(mixed[:, lanes] * MXB(scale_factor))
-        keys = mixed[:, width:][:, lanes]
-        values_across = turned(mixed[:, 2 * width :][:, lanes])
-        queries.append(query)
-        keys_across.append(turned(keys))
-        parts = []
-        for half in range(2):
-            scores = dot_nt(keys, query[half]) + mask
+    attn_rows = []
+    for g in range(groups):
+        of_group = mixed[g * cell : (g + 1) * cell]
+        attn_parts = []
+        for pair in range(pairs):
+            lanes = slice(2 * HEAD_DIM * pair, 2 * HEAD_DIM * (pair + 1))
+            query = jnp.concatenate(halves(of_group[:, lanes] * MXB(scale_factor)), axis=0)
+            queries.append(query)
+            scores = dot_nt(of_group[:, width:][:, lanes], query) + mask
             exponent = jnp.exp(scores - jnp.max(scores, axis=0, keepdims=True))
-            weights = exponent / jnp.sum(exponent, axis=0, keepdims=True)
+            weights = exponent * (1.0 / jnp.sum(exponent, axis=0, keepdims=True))
             exact.append(weights)
             rounded.append(weights.astype(MXB))
-            parts.append(dot(values_across[half * HEAD_DIM : (half + 1) * HEAD_DIM], rounded[-1]))
-        attn_parts.append(jnp.concatenate(parts, axis=0).T.astype(MXB))
-    attn_two = jnp.concatenate(attn_parts, axis=1)
-    branch_two = dot(attn_two, to_ref[...]) + to_bias_ref[...]
+            both = dot_tn(of_group[:, 2 * width :][:, lanes], rounded[-1])
+            attn_parts.append(jnp.concatenate([both[:HEAD_DIM, :cell], both[HEAD_DIM:, cell:]], axis=0).T.astype(MXB))
+        attn_rows.append(jnp.concatenate(attn_parts, axis=1))
+    attn_two = jnp.concatenate(attn_rows, axis=0)
+    branch_two = dot(attn_two, to_ref[...]) + mode(TO_BIAS)
     field_two = field_one + mode(5) * branch_two
     normed_three, rate_three = normalise(field_two)
     hidden_three = (normed_three * (1.0 + mode(7)) + mode(6)).astype(MXB)
-    inner = dot(hidden_three, in_ref[...]) + in_bias_ref[...]
+    inner = dot(hidden_three, in_ref[...]) + wide(modes_ref, IN_BIAS, in_ref.shape[1] // width)
     square = inner * inner
     bend = jnp.tanh(inner * (GELU_RATE + GELU_RATE * 0.044715 * square))
     half_up = 0.5 + 0.5 * bend
     active = (inner * half_up).astype(MXB)
     slope = half_up + inner * (0.5 - 0.5 * bend * bend) * (GELU_RATE + 3.0 * GELU_RATE * 0.044715 * square)
-    branch_three = dot(active, out_ref[...]) + out_bias_ref[...]
-    block_ref[...] = (field_two + mode(8) * branch_three).astype(MXB).reshape(frames, tile, width)
-
-    grad_field = og_ref[...].reshape(count, width).astype(F32) * weight_ref[...]
+    branch_three = dot(active, out_ref[...]) + mode(OUT_BIAS)
+    block_ref[...] = scatter(field_two + mode(8) * branch_three).astype(MXB)
+
+    grad_field = gather(og_ref).astype(F32) * mode(WEIGHT)
     sums_ref[8] += eight_rows(grad_field * branch_three)
     grad_branch = (mode(8) * grad_field).astype(MXB)
     grad_out_ref[...] += dot_tn(grad_branch, active)
     sums_ref[11] += eight_rows(grad_branch.astype(F32))
-    grad_inner = (dot(grad_branch, out_turned_ref[...]) * slope).astype(MXB)
+    grad_inner = (dot_nt(grad_branch, out_ref[...]) * slope).astype(MXB)
     grad_in_ref[...] += dot_tn(hidden_three, grad_inner)
     in_sums_ref[...] += eight_rows(grad_inner.astype(F32))
-    grad_hidden = dot(grad_inner, in_turned_ref[...])
+    grad_hidden = dot_nt(grad_inner, in_ref[...])
     sums_ref[6] += eight_rows(grad_hidden)
     sums_ref[7] += eight_rows(grad_hidden * normed_three)
     grad_field = grad_field + normalise_back(grad_hidden, normed_three, rate_three, mode(7))
@@ -844,36 +1015,30 @@
     grad_branch = (mode(5) * grad_field).astype(MXB)
     grad_to_ref[...] += dot_tn(attn_two, grad_branch)
     sums_ref[10] += eight_rows(grad_branch.astype(F32))
-    grad_attn = dot(grad_branch, to_turned_ref[...]).astype(MXB)
-    grad_queries = []
-    grad_keys = []
-    grad_values = []
-    for pair in range(pairs):
-        lanes = slice(2 * HEAD_DIM * pair, 2 * HEAD_DIM * (pair + 1))
-        grad = halves(grad_attn[:, lanes])
-        values = mixed[:, 2 * width :][:, lanes]
-        grad_query = []
-        terms = []
-        for half in range(2):
-            weights = exact[2 * pair + half]
-            grad_weights = dot_nt(values, grad[half])
-            delta = jnp.sum(weights * grad_weights, axis=0, keepdims=True)
-            term = (weights * (grad_weights - delta)).astype(MXB)
-            terms.append(term)
-            grad_query.append(dot(keys_across[pair][half * HEAD_DIM : (half + 1) * HEAD_DIM], term))
-        both = jnp.concatenate(terms, axis=1)
-        grad_queries.append((jnp.concatenate(grad_query, axis=0).T * scale_factor).astype(MXB))
-        grad_keys.append(dot(both, jnp.concatenate(queries[pair], axis=0)).astype(MXB))
-        grad_values.append(
-            dot(
-                jnp.concatenate([rounded[2 * pair], rounded[2 * pair + 1]], axis=1),
-                jnp.concatenate(grad, axis=0),
-            ).astype(MXB)
-        )
-    grad_mix = jnp.concatenate(grad_queries + grad_keys + grad_values, axis=1)
+    grad_attn = dot_nt(grad_branch, to_ref[...]).astype(MXB)
+    mix_rows = []
+    for g in range(groups):
+        of_group = mixed[g * cell : (g + 1) * cell]
+        grad_queries = []
+        grad_keys = []
+        grad_values = []
+        for pair in range(pairs):
+            lanes = slice(2 * HEAD_DIM * pair, 2 * HEAD_DIM * (pair + 1))
+            grad = jnp.concatenate(halves(grad_attn[g * cell : (g + 1) * cell, lanes]), axis=0)
+            at = g * pairs + pair
+            grad_weights = dot_nt(of_group[:, 2 * width :][:, lanes], grad)
+            delta = jnp.sum(exact[at] * grad_weights, axis=0, keepdims=True)
+            term = (exact[at] * (grad_weights - delta)).astype(MXB)
+            both = dot_tn(of_group[:, width:][:, lanes], term)
+            grad_query = jnp.concatenate([both[:HEAD_DIM, :cell], both[HEAD_DIM:, cell:]], axis=0).T
+            grad_queries.append((grad_query * scale_factor).astype(MXB))
+            grad_keys.append(dot(term, queries[at]).astype(MXB))
+            grad_values.append(dot(rounded[at], grad).astype(MXB))
+        mix_rows.append(jnp.concatenate(grad_queries + grad_keys + grad_values, axis=1))
+    grad_mix = jnp.concatenate(mix_rows, axis=0)
     grad_t_ref[...] += dot_tn(hidden_two, grad_mix)
     t_sums_ref[...] += eight_rows(grad_mix.astype(F32))
-    grad_hidden = dot(grad_mix, t_turned_ref[...])
+    grad_hidden = dot_nt(grad_mix, t_ref[...])
     sums_ref[3] += eight_rows(grad_hidden)
     sums_ref[4] += eight_rows(grad_hidden * normed_two)
     grad_field = grad_field + normalise_back(grad_hidden, normed_two, rate_two, mode(4))
@@ -882,8 +1047,8 @@
     grad_branch = (mode(2) * grad_field).astype(MXB)
     grad_so_ref[...] += dot_tn(attn_one, grad_branch)
     sums_ref[9] += eight_rows(grad_branch.astype(F32))
-    g1_ref[...] = grad_field.reshape(frames, tile, width)
-    grad_attn = dot(grad_branch, so_turned_ref[...]).astype(MXB).reshape(frames, tile, width)
+    g1_ref[...] = scatter(grad_field)
+    grad_attn = scatter(dot_nt(grad_branch, so_ref[...])).astype(MXB)
 
     @pl.when(at_step == 0)
     def _():
@@ -945,10 +1110,20 @@
     hidden = hidden_in.shape[1]
     pairs = width // (2 * HEAD_DIM)
     cond_act = jax.nn.silu(conditioning.astype(F32)).astype(MXB)
-    modes = (jnp.dot(cond_act, ada_weight, preferred_element_type=F32) + ada_bias).reshape(9, width)
-
-    def widen(bias):
-        return jnp.concatenate([bias[:width], jnp.zeros((width,), F32), bias[width:]])[None, :]
+    modes = jnp.dot(cond_act, ada_weight, preferred_element_type=F32) + ada_bias
+    slope = jnp.tan((timesteps.astype(F32) / TSTEPS + 0.008) / 1.008 * (0.5 * math.pi))
+    loss_weight = jnp.minimum(1.0, 5.0 * slope * slope)
+    blank = jnp.zeros((width,), F32)
+    modes = jnp.concatenate(
+        [
+            modes.reshape(-1),
+            spatial_bias[:width], blank, spatial_bias[width:],
+            temporal_bias[:width], blank, temporal_bias[width:],
+            spatial_out_bias, temporal_out_bias, hidden_out_bias, hidden_in_bias,
+            jnp.broadcast_to(loss_weight, (width,)),
+            cond_act.astype(F32).reshape(-1),
+        ]
+    ).reshape(ROWS, width)
 
     x_patches = tokens[0]
     count = lax.axis_size("sp")
@@ -959,7 +1134,7 @@
     dma = pltpu.SemaphoreType.DMA
     x_frames, queries, keys, values, attn_frames, attn_patches, logs = pl.pallas_call(
         partial(spatial_forward, rows=256, block=block, part=512, count=count),
-        in_specs=[any_spec()] + [pl.BlockSpec(memory_space=pltpu.VMEM)] * 3,
+        in_specs=[any_spec()] + [pl.BlockSpec(memory_space=pltpu.VMEM)] * 2,
         out_specs=[any_spec()] * 6 + [pl.BlockSpec(memory_space=pltpu.VMEM)],
         out_shape=[frame_shape] * 5 + [patch_shape, jax.ShapeDtypeStruct((mine, pairs, 2, patches), F32)],
         scratch_shapes=[pltpu.VMEM((mine, patches, width), MXB)] * 5
@@ -968,21 +1143,10 @@
         + [dma((mine, pairs, count)), dma((mine, pairs, count)), dma((mine, pairs)), dma((5, mine))],
         compiler_params=params(0),
         cost_estimate=cost(10**11, 10**7),
-    )(x_patches, modes, spatial_proj, widen(spatial_bias))
-
-    slope = jnp.tan((timesteps.astype(F32) / TSTEPS + 0.008) / 1.008 * (0.5 * math.pi))
-    loss_weight = jnp.minimum(1.0, 5.0 * slope * slope).reshape(1, 1)
-    place = jnp.arange(frames * TILE) % TILE
-    mask = jnp.where(place[:, None] == place[None, :], 0.0, -1e30).astype(F32)
+    )(x_patches, modes, spatial_proj)
+
     tile_spec = pl.BlockSpec((frames, TILE, width), lambda i: (0, i, 0))
-    small = (
-        loss_weight * jnp.ones((1, width), F32), modes, mask,
-        spatial_out, spatial_out.T, spatial_out_bias[None, :],
-        temporal_proj, temporal_proj.T, widen(temporal_bias),
-        temporal_out, temporal_out.T, temporal_out_bias[None, :],
-        hidden_in, hidden_in.T, hidden_in_bias[None, :],
-        hidden_out, hidden_out.T, hidden_out_bias[None, :],
-    )
+    small = (modes, spatial_out, temporal_proj, temporal_out, hidden_in, hidden_out)
     sums_shapes = [
         (width, width), (width, 3 * width), (width, width), (width, hidden), (width, hidden),
         (12, 8, width), (8, 3 * width), (8, hidden),
@@ -1006,11 +1170,16 @@
     )(x_patches, attn_patches, out_grad[0], *small)
     frame_spec = pl.BlockSpec((1, patches, width), lambda f: (f, 0, 0))
     log_spec = pl.BlockSpec((1, pairs, 2, patches), lambda f: (f, 0, 0, 0))
-    sum_shapes = [(width, 3 * width), (2, 8, width), (8, 3 * width)]
-    dx_patches, grad_sp, sp_sums, sp_bias_sums = pl.pallas_call(
-        partial(spatial_backward, rows=256, block=block, part=512, count=count),
+    clips = lax.axis_size("clip")
+    span_rows = width // clips
+    unit = 16 * (-(-span_rows // (16 * count)))
+    sum_shapes = [(width, 3 * width), (width, 9 * width), (ROWS, width)]
+    dx_patches, grad_sp, grad_ada, total = pl.pallas_call(
+        partial(spatial_backward, rows=512, block=block, part=512, count=count, clips=clips),
         grid=(mine,),
-        in_specs=[frame_spec] * 5 + [log_spec, frame_spec, whole_spec((9, width)), whole_spec((3 * width, width))],
+        in_specs=[frame_spec] * 5
+        + [log_spec, frame_spec, whole_spec((ROWS, width)), whole_spec((width, 3 * width))]
+        + [whole_spec(a.shape) for a in (sums, t_sums, in_sums)],
         out_specs=[any_spec()] + [acc_spec(s) for s in sum_shapes],
         out_shape=[patch_shape] + [jax.ShapeDtypeStruct(s, F32) for s in sum_shapes],
         scratch_shapes=[
@@ -1019,61 +1188,54 @@
             pltpu.VMEM((pairs, 2, patches), F32),
             pltpu.VMEM((patches, 2 * HEAD_DIM), F32),
             pltpu.VMEM((patches, 2 * HEAD_DIM), F32),
+            pltpu.VMEM((2, 8, width), F32),
+            pltpu.VMEM((8, 3 * width), F32),
+            pltpu.VMEM((clips, span_rows, 3 * width), MXB),
+            pltpu.VMEM((clips, span_rows, 3 * width), MXB),
+            pltpu.VMEM((count, unit, 3 * width), MXB),
+            pltpu.VMEM((count, unit, 3 * width), MXB),
+            pltpu.VMEM((span_rows, 3 * width), MXB),
+            pltpu.VMEM((clips, span_rows, 3 * width), MXB),
+            pltpu.VMEM((ROWS, width), F32),
+            pltpu.VMEM((count, ROWS, width), F32),
+            pltpu.VMEM((ROWS, width), F32),
+            pltpu.VMEM((clips, ROWS, width), F32),
             dma((mine, count)),
             dma((mine, count)),
             dma((mine,)),
-        ],
+        ]
+        + [dma((clips,))] * 2
+        + [dma((count,))] * 4
+        + [dma((clips,))] * 2
+        + [dma((count,))] * 2
+        + [dma((clips,))] * 2,
         compiler_params=params(2),
         cost_estimate=cost(2 * 10**11, 10**7),
-    )(da_frames, attn_frames, queries, keys, values, logs, x_frames, modes, spatial_proj.T)
+    )(da_frames, attn_frames, queries, keys, values, logs, x_frames, modes, spatial_proj, sums, t_sums, in_sums)
     input_grad = (g1 + dx_patches.astype(F32)).astype(MXB)
-
-    clip_at = lax.axis_index("clip")
-    clips = lax.axis_size("clip")
-    vector = jnp.sum(sums, axis=1)
-    sp_vector = jnp.sum(sp_sums, axis=1)
-    grad_modes = jnp.concatenate([sp_vector, vector[2:9]], axis=0).reshape(1, 9 * width)
-    mine_only = (jnp.arange(clips) == clip_at)[:, None]
-    first_on_sp = (lax.axis_index("sp") == 0).astype(F32)
     early = lax.psum((grad_so, grad_t, grad_to, grad_in, grad_out_turned), ("clip", "sp"))
-    early, grad_sp, sp_bias_sums = lax.optimization_barrier((early, grad_sp, sp_bias_sums))
-    sp_bias = jnp.sum(sp_bias_sums, axis=0)
-    t_bias = jnp.sum(t_sums, axis=0)
-    pieces = (
-        jnp.where(mine_only, grad_modes, 0.0),
-        jnp.where(mine_only, cond_act.astype(F32) * first_on_sp, 0.0),
-        sp_bias,
-        t_bias,
-        jnp.sum(in_sums, axis=0),
-        vector[9:12],
-    )
-    flat = jnp.concatenate([p.reshape(-1) for p in pieces])
-    flat, grad_sp = lax.psum((flat, grad_sp), ("clip", "sp"))
-    found = []
-    start = 0
-    for piece in pieces:
-        found.append(flat[start : start + piece.size].reshape(piece.shape))
-        start += piece.size
-    all_modes, all_cond, sp_bias, t_bias, in_bias, out_biases = found
-    grad_ada_weight = jnp.dot(all_cond.T, all_modes, precision=lax.Precision.HIGHEST)
-    grad_ada_bias = jnp.sum(all_modes, axis=0)
+    flat = total.reshape(-1)
+
+    def lines(first, rows=1):
+        return flat[first * width : (first + rows) * width]
+
     return (
         block_out[None],
         input_grad[None],
-        grad_ada_weight,
-        grad_ada_bias,
+        grad_ada,
+        lines(0, 9),
         grad_sp,
-        jnp.concatenate([sp_bias[:width], sp_bias[2 * width :]]),
+        jnp.concatenate([lines(SP_BIAS), lines(SP_BIAS + 2)]),
         early[0],
-        out_biases[0],
+        lines(SO_BIAS),
         early[1],
-        jnp.concatenate([t_bias[:width], t_bias[2 * width :]]),
+        jnp.concatenate([lines(T_BIAS), lines(T_BIAS + 2)]),
         early[2],
-        out_biases[1],
+        lines(TO_BIAS),
         early[3],
-        in_bias,
+        lines(IN_BIAS, hidden // width),
         early[4].T,
-        out_biases[2],
+        lines(OUT_BIAS),
     )
 
 

time: 739 us -> 591 us (0.80)
  waiting for transfers between devices: 124 us -> 0.02 us
  Pallas kernels: 542 us -> 534 us
    psum x1 -> x0, waiting for transfers between devices: 124 us -> none  [fast_body(): flat, grad_sp = lax.psum((flat, grad_sp), ('clip', 'sp'))]
    pallas_call x1, Pallas kernels: 174 us -> 125 us  [fast_body(): pl.pallas_call(partial(middle, peer_count=count), grid=(stripe // TILE,),...]
    pallas_call x1, Pallas kernels: 226 us -> 268 us  [fast_body(): pl.pallas_call(partial(spatial_backward, rows=512, block=block, part=512,...]
    unnamed x62 -> x37, local copies, waits for them, and re-layouts: 22.9 us -> 21 us
  transfers between devices with their start and end apart: 2 -> 1, of which waited for: 1 -> 0; matrix products, arithmetic and copies ran while one was open for 1% -> 2% of each run, Pallas kernels for 31% -> 46%
where the time goes in v3:
time: 591 us; the launch traced here: 585 us
  Pallas kernels  534 us (90%)
  local copies, waits for them, and re-layouts  25.8 us (4%)
  between operations  15.3 us (3%)
  other arithmetic  8.2 us (1%)
    pallas_call x1, Pallas kernels, fast_body(): pl.pallas_call(partial(spatial_backward, rows=512, block=block, part=512,...  268 us
    pallas_call x1, Pallas kernels, fast_body(): pl.pallas_call(partial(spatial_forward, rows=256, block=block, part=512,...  141 us
    pallas_call x1, Pallas kernels, fast_body(): pl.pallas_call(partial(middle, peer_count=count), grid=(stripe // TILE,),...  125 us
    unnamed x37, local copies, waits for them, and re-layouts  21 us
  transfers between devices with their start and end apart: 1, of which 0 were waited for; matrix products, arithmetic and copies ran while one was open for 2% of the time, Pallas kernels for 46%

profile of v3, /device:TPU:0, one launch (start us, length us, event | category | flops | bytes accessed | tf_op | source)
XLA Modules:
  0.0 584.5 jit_solution(11707821893985504598)
XLA Ops:
  8.1 0.7 convert_reduce_fusion
  9.0 1.2 convolution_reduce_fusion
  10.1 0.7 add_dynamic-update-slice_fusion
  10.8 0.7 constant_dynamic-update-slice_fusion.11
  11.5 0.7 constant_dynamic-update-slice_fusion.9
  12.2 0.7 constant_dynamic-update-slice_fusion.8
  12.9 0.7 constant_dynamic-update-slice_fusion.6
  13.6 0.7 constant_dynamic-update-slice_fusion.5
  14.3 0.7 constant_dynamic-update-slice_fusion.4
  15.0 0.7 constant_dynamic-update-slice_fusion.3
  15.7 0.7 constant_dynamic-update-slice_fusion.2
  16.4 0.6 reshape.58.modes_ref
  17.0 141.0 %shard_map.297 = (bf16[2,2048,384]{2,1,0:T(8,128)(2,1)}, bf16[2,2048,384]{2,1,0:T(8,128)(2,1)}, bf16[2,2048,384]{2,1,0:T(8,128)(2,1)}, bf16[2,2048,384]{2,1,0:T(...) custom-call(bf16[16,256,384]{2,1,0:T(8,128)(2,1)} %bitcast.13, ...), custom_call_target="tpu_custom_call" | custom-call | flops 99999997952 | bytes 10000000 | tf_op jit(solution)/shard_map/pallas_call | solution.py:1135
  158.0 124.9 %shard_map.298 = (bf16[16,256,384]{2,1,0:T(8,128)(2,1)}, f32[16,256,384]{2,1,0:T(8,128)}, bf16[2,2048,384]{2,1,0:T(8,128)(2,1)}, f32[384,384]{1,0:T(8,128)}, f32...) custom-call(bf16[16,256,384]{2,1,0:T(8,128)(2,1)} %bitcast.14, ...), custom_call_target="tpu_custom_call" | custom-call | flops 99999997952 | bytes 10000000 | tf_op jit(solution)/shard_map/pallas_call | solution.py:1161
  283.0 268.1 %shard_map.299 = (bf16[16,256,384]{2,1,0:T(8,128)(2,1)}, f32[384,1152]{1,0:T(8,128)}, f32[384,3456]{1,0:T(8,128)}, f32[24,384]{1,0:T(8,128)}) custom-call(bf16[2,2048,384]{2,1,0:T(8,128)(2,1)} %get-tuple-element.41.da_ref, bf16[2,2048,384]{2,1,0:T(8,128)(2,1)} %get-tuple-element.42.attn_ref, bf16[2,2048,384]{2,1,0:T(8,128)(2,1)} %get-tuple-element.43.q_ref, ...), custom_call_target="tpu_custom_call" | custom-call | flops 199999995904 | bytes 10000000 | tf_op jit(solution)/shard_map/pallas_call | solution.py:1177
  551.1 0.7 slice.84
  551.8 0.7 slice.70
  552.5 0.6 slice.85
  553.1 0.6 slice.71
  553.7 1.5 slice_reduce_fusion
  555.3 0.6 pad_maximum_fusion
  555.9 6.1 %fusion = bf16[1,16,256,384]{3,2,1,0:T(8,128)(2,1)} fusion(f32[16,256,384]{2,1,0:T(8,128)} %get-tuple-element.40, bf16[16,256,384]{2,1,0:T(8,128)(2,1)} %get-tuple-element.51), kind=kLoop, calls=%fused_computation.1 | loop fusion | flops 4718592 | bytes 12582912 | tf_op jit(solution)/shard_map/broadcast_in_dim | solution.py:1224
  562.0 3.2 copy.34
  565.2 1.7 copy.61
  566.9 2.0 copy-done.2
  568.9 2.4 copy.62
  571.3 0.4 copy-done.6
  571.6 1.2 copy.63
  573.1 0.8 copy.64
  573.9 1.2 copy.65
  575.1 0.8 copy.66
  575.9 1.4 copy.67
  (24 shorter events, 0.5 us)
Async XLA Ops:
  7.2 1.8 copy-start
  7.2 554.8 %all-reduce.3.cloned.1.call-start = ((), (), s32[]{:S(2)}) async-start(), calls=%async_computation | async-start | bytes 15335424 | tf_op jit(solution)/shard_map/psum | solution.py:1216
  562.0 3.2 copy-start.3
  565.2 3.6 copy-start.2
  568.9 2.8 copy-start.6
  571.6 1.4 copy-start.8
  571.6 2.3 copy-start.5
  573.1 2.1 copy-start.7
  573.1 2.9 copy-start.4
  573.9 3.4 copy-start.1
Sparse Core Ops, SparseCore 0:
  283.1 198.0 all-reduce.2

commit v4 on v3

--- a/solution.py
+++ b/solution.py
@@ -466,26 +466,30 @@
 def spatial_forward(
     tokens_ref, modes_ref, proj_ref,
     x_out, q_out, k_out, v_out, attn_out, patches_out, log_ref,
-    x_ref, q_ref, k_ref, v_ref, attn_ref, turned_ref,
+    x_ref, q_ref, k_ref, v_ref, attn_ref, turned_ref, mixed_ref, top_ref,
     x_send, x_recv, x_own, a_send, a_recv, a_own, save_sem,
-    rows, block, part, count,
+    block, part, count,
 ):
     mine, tokens, width = x_ref.shape
     stripe = tokens // count
     pairs = width // (2 * HEAD_DIM)
     near = block // stripe
-    blocks = tokens // block
+    soon = patches_out.shape[1]
     me, peers = others(count)
     shift = modes_ref[0:1, :]
     scale = modes_ref[1:2, :]
     bias = wide(modes_ref, SP_BIAS, 3)
 
-    def x_copy(frame, step, peer):
+    def x_copy(frame, peer):
         return send(
             tokens_ref.at[peer * mine + frame],
             x_ref.at[frame, pl.ds(pl.multiple_of(me * stripe, stripe), stripe), :],
-            x_send.at[frame, step], x_recv.at[frame, step], peer,
-        )
+            x_send.at[frame, peer], x_recv.at[frame, me], peer,
+        )
+
+    def x_landed(frame, source):
+        rows = x_ref.at[frame, pl.ds(pl.multiple_of(source * stripe, stripe), stripe), :]
+        return send(rows, rows, x_send.at[frame, source], x_recv.at[frame, source], source)
 
     def x_keep(frame):
         return pltpu.make_async_copy(
@@ -505,7 +509,7 @@
     def a_copy(frame, pair, peer):
         lanes = pl.ds(pl.multiple_of(pair * 2 * HEAD_DIM, 2 * HEAD_DIM), 2 * HEAD_DIM)
         return send(
-            attn_ref.at[frame, pl.ds(pl.multiple_of(peer * stripe, stripe), stripe), lanes],
+            attn_ref.at[frame, pl.ds(pl.multiple_of(peer * stripe, stripe), soon), lanes],
             patches_out.at[me * mine + frame, :, lanes],
             a_send.at[frame, pair, peer], a_recv.at[frame, pair, me], peer,
         )
@@ -513,7 +517,7 @@
     def a_landed(frame, pair, peer):
         lanes = pl.ds(pl.multiple_of(pair * 2 * HEAD_DIM, 2 * HEAD_DIM), 2 * HEAD_DIM)
         return send(
-            attn_ref.at[frame, pl.ds(pl.multiple_of(peer * stripe, stripe), stripe), lanes],
+            attn_ref.at[frame, pl.ds(pl.multiple_of(peer * stripe, stripe), soon), lanes],
             patches_out.at[peer * mine + frame, :, lanes],
             a_send.at[frame, pair, peer], a_recv.at[frame, pair, peer], peer,
         )
@@ -521,72 +525,113 @@
     def a_keep(frame, pair):
         lanes = pl.ds(pl.multiple_of(pair * 2 * HEAD_DIM, 2 * HEAD_DIM), 2 * HEAD_DIM)
         return pltpu.make_async_copy(
-            attn_ref.at[frame, pl.ds(pl.multiple_of(me * stripe, stripe), stripe), lanes],
+            attn_ref.at[frame, pl.ds(pl.multiple_of(me * stripe, stripe), soon), lanes],
             patches_out.at[me * mine + frame, :, lanes],
             a_own.at[frame, pair],
         )
 
+    near_source = lax.div(me, near) * near
+    far_source = near - near_source
+
+    def x_sends(frame, first, stop, far):
+        for place in range(first, stop):
+            peer = (far_source if far else near_source) + lax.rem(me + place, near)
+            x_copy(frame, peer).start()
+
     greet(peers)
     greeted(peers)
-    order = sorted(range(1, count), key=lambda step: -min(step, count - step))
     for frame in range(mine):
-        for step in order:
-            x_copy(frame, step, lax.rem(me + step, count)).start()
         x_keep(frame).start()
-    turned_ref[:, HEAD_DIM:, :] = jnp.ones((2 * pairs, turned_ref.shape[1] - HEAD_DIM, tokens), MXB)
-
-    def one_frame(frame, carry):
-        x_keep(frame).wait()
-        for step, _, source in peers:
-            x_copy(frame, step, source).wait_recv()
-        saves(frame)[0].start()
-
-        def project(index, carry):
-            at = pl.ds(pl.multiple_of(index * rows, rows), rows)
-            normed, _ = normalise(x_ref[frame, at, :].astype(F32))
-            hidden = (normed * (1.0 + scale) + shift).astype(MXB)
-            mixed = dot(hidden, proj_ref[...]) + bias
-            q_ref[frame, at, :] = mixed[:, :width].astype(MXB)
-            k_ref[frame, at, :] = mixed[:, width : 2 * width].astype(MXB)
-            value = mixed[:, 2 * width :].astype(MXB)
-            v_ref[frame, at, :] = value
-            across = turned(value)
-            for head in range(2 * pairs):
-                turned_ref[head, :HEAD_DIM, at] = across[head * HEAD_DIM : (head + 1) * HEAD_DIM]
-            return carry
-
-        lax.fori_loop(0, tokens // rows, project, 0)
-        for copy in saves(frame)[1:4]:
-            copy.start()
-
-        def attend_block(index, carry):
-            pair = lax.rem(index, pairs)
-            chunk = lax.rem(lax.div(index, pairs) + lax.div(me, near) + 1, blocks)
-            at = pl.ds(pl.multiple_of(chunk * block, block), block)
-            lanes = pl.ds(pl.multiple_of(pair * 2 * HEAD_DIM, 2 * HEAD_DIM), 2 * HEAD_DIM)
-            scores = []
-            tops = []
-            for query in halves(q_ref[frame, at, lanes] * MXB(HEAD_DIM**-0.5)):
-                each = [
-                    dot_nt(k_ref[frame, first : first + part, lanes], query)
-                    for first in range(0, tokens, part)
-                ]
-                top = [jnp.max(s.reshape(part // 8, 8, block), axis=0) for s in each]
-                scores.append(each)
-                tops.append(jnp.max(reduce(jnp.maximum, top), axis=0, keepdims=True))
+    x_sends(0, 1, near, False)
+    x_sends(0, 0, near // 2, True)
+    for frame in range(1, mine):
+        x_sends(frame, 1, near, False)
+    x_sends(0, near // 2, near, True)
+    for frame in range(1, mine):
+        x_sends(frame, 0, near, True)
+    turned_ref[:, :, HEAD_DIM:, :] = jnp.ones(
+        (mine, 2 * pairs, turned_ref.shape[2] - HEAD_DIM, tokens), MXB
+    )
+    mixed_ref[...] = jnp.zeros_like(mixed_ref)
+    top_ref[...] = jnp.full_like(top_ref, -1e30)
+
+    def stage(index, carry):
+        pair = lax.rem(index, pairs)
+        group = lax.div(index, pairs)
+        early = group < mine
+        place = lax.rem(jnp.maximum(group - mine, 0), 3)
+        frame = jnp.where(early, group, lax.div(jnp.maximum(group - mine, 0), 3))
+
+        @pl.when((pair == 0) & (early | (place == 0)))
+        def _():
+            first_source = jnp.where(early, near_source, far_source)
+
+            def project(index, carry):
+                source = first_source + index
+                at = pl.ds(pl.multiple_of(source * stripe, stripe), stripe)
+
+                @pl.when(source == me)
+                def _():
+                    x_keep(frame).wait()
+
+                @pl.when(source != me)
+                def _():
+                    x_landed(frame, source).wait_recv()
+
+                normed, _ = normalise(x_ref[frame, at, :].astype(F32))
+                hidden = (normed * (1.0 + scale) + shift).astype(MXB)
+                mixed = dot(hidden, proj_ref[...]) + bias
+                q_ref[frame, at, :] = mixed[:, :width].astype(MXB)
+                k_ref[frame, at, :] = mixed[:, width : 2 * width].astype(MXB)
+                value = mixed[:, 2 * width :].astype(MXB)
+                v_ref[frame, at, :] = value
+                across = turned(value)
+                for head in range(2 * pairs):
+                    turned_ref[frame, head, :HEAD_DIM, at] = across[head * HEAD_DIM : (head + 1) * HEAD_DIM]
+                return carry
+
+            lax.fori_loop(0, near, project, 0)
+
+            @pl.when(group >= mine)
+            def _():
+                for copy in saves(frame)[:4]:
+                    copy.start()
+
+        query_source = jnp.where(early | (place == 2), near_source, far_source)
+        key_source = jnp.where(early | (place == 0), near_source, far_source)
+        at = pl.ds(pl.multiple_of(query_source * stripe, block), block)
+        lanes = pl.ds(pl.multiple_of(pair * 2 * HEAD_DIM, 2 * HEAD_DIM), 2 * HEAD_DIM)
+        spans = [pl.ds(pl.multiple_of(key_source * stripe + first, part), part) for first in range(0, block, part)]
+        scores = []
+        tops = []
+        decays = []
+        for side, query in enumerate(halves(q_ref[frame, at, lanes] * MXB(HEAD_DIM**-0.5))):
+            each = [dot_nt(k_ref[frame, span, lanes], query) for span in spans]
+            top = [jnp.max(s.reshape(part // 8, 8, block), axis=0) for s in each]
+            before = top_ref[frame, pair, side : side + 1, at]
+            now = jnp.maximum(before, jnp.max(reduce(jnp.maximum, top), axis=0, keepdims=True))
+            top_ref[frame, pair, side : side + 1, at] = now
+            scores.append(each)
+            tops.append(now)
+            decays.append(jnp.exp(before - now))
+        for side in range(2):
+            total = mixed_ref[frame, 2 * pair + side, :, at] * decays[side]
+            for span, s in zip(spans, scores[side]):
+                weights = jnp.exp(s - tops[side]).astype(MXB)
+                total = total + dot(turned_ref[frame, 2 * pair + side, :, span], weights)
+            mixed_ref[frame, 2 * pair + side, :, at] = total
+
+        @pl.when((group >= mine) & (place >= 1))
+        def _():
             mixed = []
-            for half in range(2):
-                total = jnp.zeros((turned_ref.shape[1], block), F32)
-                for number, s in enumerate(scores[half]):
-                    weights = jnp.exp(s - tops[half]).astype(MXB)
-                    values = turned_ref[2 * pair + half, :, number * part : (number + 1) * part]
-                    total = total + dot(values, weights)
+            for side in range(2):
+                total = mixed_ref[frame, 2 * pair + side, :, at]
                 mass = total[HEAD_DIM : HEAD_DIM + 1]
-                log_ref[frame, pair, half : half + 1, at] = tops[half] + jnp.log(mass)
+                log_ref[frame, pair, side : side + 1, at] = tops[side] + jnp.log(mass)
                 mixed.append(total[:HEAD_DIM] / mass)
             attn_ref[frame, at, lanes] = jnp.concatenate(mixed, axis=0).T.astype(MXB)
-            for place in range(near):
-                peer = chunk * near + place
+            for other in range(near):
+                peer = query_source + other
 
                 @pl.when(peer != me)
                 def _():
@@ -596,19 +641,19 @@
                 def _():
                     a_keep(frame, pair).start()
 
-            return carry
-
-        lax.fori_loop(0, pairs * blocks, attend_block, 0)
-        saves(frame)[4].start()
+        @pl.when((group >= mine) & (place == 2) & (pair == pairs - 1))
+        def _():
+            saves(frame)[4].start()
+
         return carry
 
-    lax.fori_loop(0, mine, one_frame, 0)
+    lax.fori_loop(0, 4 * mine * pairs, stage, 0)
 
     for frame in range(mine):
         for copy in saves(frame):
             copy.wait()
-        for step, peer, _ in peers:
-            x_copy(frame, step, peer).wait_send()
+        for _, peer, _ in peers:
+            x_copy(frame, peer).wait_send()
         for pair in range(pairs):
             a_keep(frame, pair).wait()
             for _, peer, _ in peers:
@@ -618,11 +663,11 @@
 
 def spatial_backward(
     da_ref, attn_ref, q_ref, k_ref, v_ref, log_ref, x_ref, modes_ref, proj_ref, mid_sums_ref, t_sums_ref, in_sums_ref,
-    patches_out, grad_proj_ref, ada_ref, total_ref,
-    dx_ref, mix_ref, delta_ref, dk_ref, dv_ref, sums_ref, bias_sums_ref,
+    patches_out, proj_out, row_out,
+    grad_proj_ref, dx_ref, mix_ref, delta_ref, dq_ref, dk_ref, dv_ref, across_ref, sums_ref, bias_sums_ref,
     clip_out_ref, clip_in_ref, unit_out_ref, unit_in_ref, piece_ref, all_ref, vec_ref, vec_in_ref, row_ref, row_in_ref,
     send_sem, recv_sem, own_sem, g1_send, g1_recv, g2_send, g2_recv, g3_send, g3_recv, g4_send, g4_recv,
-    v1_send, v1_recv, v2_send, v2_recv, rows, block, part, count, clips,
+    v1_send, v1_recv, v2_send, v2_recv, rows, part, count, clips,
 ):
     tokens, width = x_ref.shape[1:]
     mine = dx_ref.shape[0]
@@ -702,94 +747,114 @@
 
     lax.fori_loop(0, tokens // rows, deltas, 0)
 
-    for pair in range(pairs):
-        first_lane = 2 * HEAD_DIM * pair
-        lanes = slice(first_lane, first_lane + 2 * HEAD_DIM)
-        dk_ref[...] = jnp.zeros_like(dk_ref)
-        dv_ref[...] = jnp.zeros_like(dv_ref)
-        keys_across = turned(k_ref[0, :, lanes])
-
-        def queries_block(index, carry, pair=pair, lanes=lanes, keys_across=keys_across):
-            at = pl.ds(pl.multiple_of(index * block, block), block)
+    def turn_keys(pair, carry):
+        lanes = pl.ds(pl.multiple_of(pair * 2 * HEAD_DIM, 2 * HEAD_DIM), 2 * HEAD_DIM)
+        across_ref[pair] = turned(k_ref[0, :, lanes])
+        dq_ref[pair] = jnp.zeros(dq_ref.shape[1:], F32)
+        dk_ref[:, lanes] = jnp.zeros((tokens, 2 * HEAD_DIM), F32)
+        dv_ref[:, lanes] = jnp.zeros((tokens, 2 * HEAD_DIM), F32)
+        return carry
+
+    lax.fori_loop(0, pairs, turn_keys, 0)
+
+    @pl.when(frame == 0)
+    def _():
+        greeted(peers + clip_peers)
+
+    half = tokens // 2
+    near = half // stripe
+    near_first = lax.div(me, near) * half
+    far_first = half - near_first
+    last = frame == mine - 1
+    shift = modes_ref[0:1, :]
+    scale = modes_ref[1:2, :]
+
+    def hidden_of(at):
+        normed, rate = normalise(x_ref[0, at, :].astype(F32))
+        return normed, rate, (normed * (1.0 + scale) + shift).astype(MXB)
+
+    def phase_pass(phase, carry):
+        def step_pass(index, carry):
+            pair = lax.rem(index, pairs)
+            step = lax.div(index, pairs) + 3 * phase
+            lanes = pl.ds(pl.multiple_of(pair * 2 * HEAD_DIM, 2 * HEAD_DIM), 2 * HEAD_DIM)
+            query_first = jnp.where(step >= 2, near_first, far_first)
+            key_first = jnp.where(lax.rem(step, 2) == 1, near_first, far_first)
+            at = pl.ds(pl.multiple_of(query_first, half), half)
             query = halves(q_ref[0, at, lanes] * MXB(scale_factor))
             grad = halves(da_ref[0, at, lanes])
             query_both = jnp.concatenate(query, axis=0)
             grad_both = jnp.concatenate(grad, axis=0)
-            grad_query = [jnp.zeros((HEAD_DIM, block), F32), jnp.zeros((HEAD_DIM, block), F32)]
-            for first in range(0, tokens, part):
-                span = slice(first, first + part)
+            grad_query = [jnp.zeros((HEAD_DIM, half), F32), jnp.zeros((HEAD_DIM, half), F32)]
+            for first in range(0, half, part):
+                span = pl.ds(pl.multiple_of(key_first + first, part), part)
                 keys = k_ref[0, span, lanes]
                 values = v_ref[0, span, lanes]
                 weights = []
                 grad_scores = []
-                for half in range(2):
-                    scores = dot_nt(keys, query[half])
-                    exact = jnp.exp(scores - log_ref[0, pair, half : half + 1, at])
-                    grad_weights = dot_nt(values, grad[half])
-                    term = (exact * (grad_weights - delta_ref[pair, half : half + 1, at])).astype(MXB)
+                for side in range(2):
+                    scores = dot_nt(keys, query[side])
+                    exact = jnp.exp(scores - log_ref[0, pair, side : side + 1, at])
+                    grad_weights = dot_nt(values, grad[side])
+                    term = (exact * (grad_weights - delta_ref[pair, side : side + 1, at])).astype(MXB)
                     weights.append(exact.astype(MXB))
                     grad_scores.append(term)
-                    grad_query[half] = grad_query[half] + dot(
-                        keys_across[half * HEAD_DIM : (half + 1) * HEAD_DIM, span], term
-                    )
-                dv_ref[span, :] += dot(jnp.concatenate(weights, axis=1), grad_both)
-                dk_ref[span, :] += dot(jnp.concatenate(grad_scores, axis=1), query_both)
-            mix_ref[at, lanes] = (jnp.concatenate(grad_query, axis=0).T * scale_factor).astype(MXB)
+                    across = across_ref[pair, side * HEAD_DIM : (side + 1) * HEAD_DIM, span]
+                    grad_query[side] = grad_query[side] + dot(across, term)
+                dv_ref[span, lanes] += dot(jnp.concatenate(weights, axis=1), grad_both)
+                dk_ref[span, lanes] += dot(jnp.concatenate(grad_scores, axis=1), query_both)
+            for side in range(2):
+                dq_ref[pair, side * HEAD_DIM : (side + 1) * HEAD_DIM, at] += grad_query[side]
             return carry
 
-        lax.fori_loop(0, tokens // block, queries_block, 0)
-        mix_ref[:, width + first_lane : width + first_lane + 2 * HEAD_DIM] = dk_ref[...].astype(MXB)
-        mix_ref[:, 2 * width + first_lane : 2 * width + first_lane + 2 * HEAD_DIM] = dv_ref[...].astype(MXB)
-
-    shift = modes_ref[0:1, :]
-    scale = modes_ref[1:2, :]
-
-    @pl.when(frame == 0)
-    def _():
-        greeted(peers + clip_peers)
-
-    def hidden_of(at):
-        normed, rate = normalise(x_ref[0, at, :].astype(F32))
-        return normed, rate, (normed * (1.0 + scale) + shift).astype(MXB)
-
-    def weigh(index, carry):
-        at = pl.ds(pl.multiple_of(index * rows, rows), rows)
-        _, _, hidden = hidden_of(at)
-        grad_mix = mix_ref[at, :]
-        grad_proj_ref[...] += dot_tn(hidden, grad_mix)
-        bias_sums_ref[...] += eight_rows(grad_mix.astype(F32))
+        lax.fori_loop(0, jnp.where(phase == 0, 3 * pairs, pairs), step_pass, 0)
+        first_row = jnp.where(phase == 0, far_first, near_first)
+
+        def weigh(index, carry):
+            at = pl.ds(pl.multiple_of(first_row + index * rows, rows), rows)
+            for pair in range(pairs):
+                lanes = slice(2 * HEAD_DIM * pair, 2 * HEAD_DIM * (pair + 1))
+                mix_ref[at, lanes] = (dq_ref[pair, :, at].T * scale_factor).astype(MXB)
+            mix_ref[at, width : 2 * width] = dk_ref[at, :].astype(MXB)
+            mix_ref[at, 2 * width :] = dv_ref[at, :].astype(MXB)
+            _, _, hidden = hidden_of(at)
+            grad_mix = mix_ref[at, :]
+            grad_proj_ref[...] += dot_tn(hidden, grad_mix)
+            bias_sums_ref[...] += eight_rows(grad_mix.astype(F32))
+            return carry
+
+        lax.fori_loop(0, half // rows, weigh, 0)
+
+        @pl.when(last & (phase == 1))
+        def _():
+            for each in range(clips):
+                clip_out_ref[each] = grad_proj_ref[each * span_rows : (each + 1) * span_rows, :].astype(MXB)
+            for _, peer, _ in clip_peers:
+                g1_copy(peer, clip).start()
+
+        def finish(index, carry):
+            peer = lax.div(first_row, stripe) + index
+            at = pl.ds(pl.multiple_of(first_row + index * stripe, stripe), stripe)
+            normed, rate, _ = hidden_of(at)
+            grad_hidden = dot_nt(mix_ref[at, :], proj_ref[...])
+            sums_ref[0] += eight_rows(grad_hidden)
+            sums_ref[1] += eight_rows(grad_hidden * normed)
+            dx_ref[frame, at, :] = normalise_back(grad_hidden, normed, rate, scale).astype(MXB)
+
+            @pl.when(peer != me)
+            def _():
+                dx_copy(frame, peer).start()
+
+            @pl.when(peer == me)
+            def _():
+                dx_keep(frame).start()
+
+            return carry
+
+        lax.fori_loop(0, near, finish, 0)
         return carry
 
-    lax.fori_loop(0, tokens // rows, weigh, 0)
-    last = frame == mine - 1
-
-    @pl.when(last)
-    def _():
-        for each in range(clips):
-            clip_out_ref[each] = grad_proj_ref[each * span_rows : (each + 1) * span_rows, :].astype(MXB)
-        for _, peer, _ in clip_peers:
-            g1_copy(peer, clip).start()
-
-    def finish(index, carry):
-        peer = lax.rem(me + count // 2 + index, count)
-        at = pl.ds(pl.multiple_of(peer * stripe, stripe), stripe)
-        normed, rate, _ = hidden_of(at)
-        grad_hidden = dot_nt(mix_ref[at, :], proj_ref[...])
-        sums_ref[0] += eight_rows(grad_hidden)
-        sums_ref[1] += eight_rows(grad_hidden * normed)
-        dx_ref[frame, at, :] = normalise_back(grad_hidden, normed, rate, scale).astype(MXB)
-
-        @pl.when(peer != me)
-        def _():
-            dx_copy(frame, peer).start()
-
-        @pl.when(peer == me)
-        def _():
-            dx_keep(frame).start()
-
-        return carry
-
-    lax.fori_loop(0, count // 2, finish, 0)
+    lax.fori_loop(0, 2, phase_pass, 0)
 
     @pl.when(last)
     def _():
@@ -804,10 +869,6 @@
             def _():
                 g2_copy(owner, me).start()
 
-    lax.fori_loop(count // 2, count, finish, 0)
-
-    @pl.when(last)
-    def _():
         def row_sum(array):
             return jnp.sum(array, axis=0, keepdims=True)
 
@@ -852,25 +913,14 @@
 
         for _, peer, _ in clip_peers:
             g4_copy(peer, clip).start()
-        grad_proj_ref[pl.ds(pl.multiple_of(clip * span_rows, span_rows), span_rows), :] = piece_ref[...].astype(F32)
-
+        proj_out[pl.ds(pl.multiple_of(clip * span_rows, span_rows), span_rows), :] = piece_ref[...]
         row_in_ref[clip] = row_ref[...]
         for _, _, source in clip_peers:
             v2_copy(source, source).wait_recv()
-        total = row_in_ref[0]
-        for each in range(1, clips):
-            total = total + row_in_ref[each]
-        total_ref[...] = total
-        tall = [row_in_ref[each][ROWS - 8 :].T[:, 7:8] for each in range(clips)]
-        for block_at in range(9):
-            outer = tall[0] * row_in_ref[0, block_at : block_at + 1, :]
-            for each in range(1, clips):
-                outer = outer + tall[each] * row_in_ref[each, block_at : block_at + 1, :]
-            ada_ref[:, block_at * width : (block_at + 1) * width] = outer
-
+        row_out[...] = row_in_ref[...]
         for _, _, source in clip_peers:
             g4_copy(source, source).wait_recv()
-            grad_proj_ref[pl.ds(pl.multiple_of(source * span_rows, span_rows), span_rows), :] = all_ref[source].astype(F32)
+            proj_out[pl.ds(pl.multiple_of(source * span_rows, span_rows), span_rows), :] = all_ref[source]
 
         for _, peer, _ in clip_peers:
             g1_copy(peer, clip).wait_send()
@@ -898,10 +948,11 @@
 
 
 def middle(
-    x_ref, attn_ref, og_ref, modes_ref, so_ref, t_ref, to_ref, in_ref, out_ref,
+    x_ref, soon_ref, og_ref, attn_hbm, modes_ref, so_ref, t_ref, to_ref, in_ref, out_ref,
     block_ref, g1_ref, da_out,
-    grad_so_ref, grad_t_ref, grad_to_ref, grad_in_ref, grad_out_ref, sums_ref, t_sums_ref, in_sums_ref,
-    da_ref, send_sem, recv_sem, own_sem, peer_count,
+    so_out, t_out, to_out, in_out, out_out, sums_ref, t_sums_ref, in_sums_ref,
+    grad_so_ref, grad_t_ref, grad_to_ref, grad_in_ref, grad_out_ref,
+    da_ref, attn_ref, late_ref, send_sem, recv_sem, own_sem, late_send, late_recv, late_own, peer_count,
 ):
     frames, tile, width = x_ref.shape
     count = frames * tile
@@ -932,14 +983,52 @@
         rows = da_out.at[:, pl.ds(pl.multiple_of(source * stripe, stripe), stripe), :]
         return send(rows, rows, send_sem.at[0, step], recv_sem.at[step], source)
 
+    soon_steps = (stripe - late_ref.shape[1]) // tile
+    late = late_ref.shape[1]
+
+    def late_copy(frame, step, peer):
+        rows = pl.ds(pl.multiple_of(peer * stripe + stripe - late, tile), late)
+        return send(
+            attn_hbm.at[frame, rows, :], late_ref.at[me * mine + frame],
+            late_send.at[frame, step], late_recv.at[frame, step], peer,
+        )
+
+    def late_landed(frame, step, source):
+        rows = late_ref.at[source * mine + frame]
+        return send(rows, rows, late_send.at[frame, step], late_recv.at[frame, step], source)
+
+    def late_keep(frame):
+        rows = pl.ds(pl.multiple_of(me * stripe + stripe - late, tile), late)
+        return pltpu.make_async_copy(attn_hbm.at[frame, rows, :], late_ref.at[me * mine + frame], late_own.at[frame])
+
     @pl.when(at_step == 0)
     def _():
         greet(peers)
+        greeted(peers)
+        for frame in range(mine):
+            late_keep(frame).start()
+            for step, peer, _ in peers:
+                late_copy(frame, step, peer).start()
         for ref in (grad_so_ref, grad_t_ref, grad_to_ref, grad_in_ref, grad_out_ref, sums_ref, t_sums_ref, in_sums_ref):
             ref[...] = jnp.zeros_like(ref)
 
     def mode(row):
         return modes_ref[row : row + 1, :]
+
+    @pl.when(at_step < soon_steps)
+    def _():
+        attn_ref[...] = soon_ref[...]
+
+    @pl.when(at_step == soon_steps)
+    def _():
+        for frame in range(mine):
+            late_keep(frame).wait()
+            for step, _, source in peers:
+                late_landed(frame, step, source).wait_recv()
+
+    @pl.when(at_step >= soon_steps)
+    def _():
+        attn_ref[...] = late_ref[:, pl.ds(pl.multiple_of((at_step - soon_steps) * tile, tile), tile), :]
 
     cell = frames * GROUP
     groups = tile // GROUP
@@ -1050,10 +1139,6 @@
     g1_ref[...] = scatter(grad_field)
     grad_attn = scatter(dot_nt(grad_branch, so_ref[...])).astype(MXB)
 
-    @pl.when(at_step == 0)
-    def _():
-        greeted(peers)
-
     def sent(at_step):
         da_keep(at_step).wait()
         for step, peer, _ in peers:
@@ -1075,8 +1160,15 @@
             sent(steps - 2)
 
         sent(steps - 1)
-        for step, _, source in peers:
+        for step, peer, source in peers:
             da_landed(step, source).wait_recv()
+            for frame in range(mine):
+                late_copy(frame, step, peer).wait_send()
+        so_out[...] = grad_so_ref[...].astype(MXB)
+        t_out[...] = grad_t_ref[...].astype(MXB)
+        to_out[...] = grad_to_ref[...].astype(MXB)
+        in_out[...] = grad_in_ref[...].astype(MXB)
+        out_out[...] = grad_out_ref[...].astype(MXB)
 
 
 def whole_spec(shape):
@@ -1114,31 +1206,41 @@
     slope = jnp.tan((timesteps.astype(F32) / TSTEPS + 0.008) / 1.008 * (0.5 * math.pi))
     loss_weight = jnp.minimum(1.0, 5.0 * slope * slope)
     blank = jnp.zeros((width,), F32)
-    modes = jnp.concatenate(
-        [
-            modes.reshape(-1),
-            spatial_bias[:width], blank, spatial_bias[width:],
-            temporal_bias[:width], blank, temporal_bias[width:],
-            spatial_out_bias, temporal_out_bias, hidden_out_bias, hidden_in_bias,
-            jnp.broadcast_to(loss_weight, (width,)),
-            cond_act.astype(F32).reshape(-1),
-        ]
-    ).reshape(ROWS, width)
+    pieces = (
+        modes.reshape(-1),
+        spatial_bias[:width], blank, spatial_bias[width:],
+        temporal_bias[:width], blank, temporal_bias[width:],
+        spatial_out_bias, temporal_out_bias, hidden_out_bias, hidden_in_bias,
+        jnp.broadcast_to(loss_weight, (width,)),
+        cond_act.astype(F32).reshape(-1),
+    )
+    packed = jnp.zeros((ROWS * width,), F32)
+    start = 0
+    for piece in pieces:
+        packed = packed + jnp.pad(piece, (start, ROWS * width - start - piece.size))
+        start += piece.size
+    modes = packed.reshape(ROWS, width)
 
     x_patches = tokens[0]
     count = lax.axis_size("sp")
     mine, patches = frames // count, stripe * count
-    block = min(1024, patches)
+    block = patches // 2
+    soon = max(stripe // (2 * TILE), 1) * TILE
     frame_shape = jax.ShapeDtypeStruct((mine, patches, width), MXB)
     patch_shape = jax.ShapeDtypeStruct((frames, stripe, width), MXB)
     dma = pltpu.SemaphoreType.DMA
     x_frames, queries, keys, values, attn_frames, attn_patches, logs = pl.pallas_call(
-        partial(spatial_forward, rows=256, block=block, part=512, count=count),
+        partial(spatial_forward, block=block, part=512, count=count),
         in_specs=[any_spec()] + [pl.BlockSpec(memory_space=pltpu.VMEM)] * 2,
         out_specs=[any_spec()] * 6 + [pl.BlockSpec(memory_space=pltpu.VMEM)],
-        out_shape=[frame_shape] * 5 + [patch_shape, jax.ShapeDtypeStruct((mine, pairs, 2, patches), F32)],
+        out_shape=[frame_shape] * 5
+        + [
+            jax.ShapeDtypeStruct((frames, soon, width), MXB),
+            jax.ShapeDtypeStruct((mine, pairs, 2, patches), F32),
+        ],
         scratch_shapes=[pltpu.VMEM((mine, patches, width), MXB)] * 5
-        + [pltpu.VMEM((2 * pairs, HEAD_DIM + 16, patches), MXB)]
+        + [pltpu.VMEM((mine, 2 * pairs, HEAD_DIM + 16, patches), MXB)]
+        + [pltpu.VMEM((mine, 2 * pairs, HEAD_DIM + 16, patches), F32), pltpu.VMEM((mine, pairs, 2, patches), F32)]
         + [dma((mine, count)), dma((mine, count)), dma((mine,))]
         + [dma((mine, pairs, count)), dma((mine, pairs, count)), dma((mine, pairs)), dma((5, mine))],
         compiler_params=params(0),
@@ -1146,6 +1248,7 @@
     )(x_patches, modes, spatial_proj)
 
     tile_spec = pl.BlockSpec((frames, TILE, width), lambda i: (0, i, 0))
+    soon_spec = pl.BlockSpec((frames, TILE, width), lambda i: (0, jnp.minimum(i, soon // TILE - 1), 0))
     small = (modes, spatial_out, temporal_proj, temporal_out, hidden_in, hidden_out)
     sums_shapes = [
         (width, width), (width, 3 * width), (width, width), (width, hidden), (width, hidden),
@@ -1155,39 +1258,49 @@
         patch_shape,
         jax.ShapeDtypeStruct((frames, stripe, width), F32),
         frame_shape,
-    ] + [jax.ShapeDtypeStruct(s, F32) for s in sums_shapes]
+    ] + [jax.ShapeDtypeStruct(s, MXB if at < 5 else F32) for at, s in enumerate(sums_shapes)]
     (
         block_out, g1, da_frames, grad_so, grad_t, grad_to, grad_in, grad_out_turned, sums, t_sums, in_sums,
     ) = pl.pallas_call(
         partial(middle, peer_count=count),
         grid=(stripe // TILE,),
-        in_specs=[tile_spec] * 3 + [whole_spec(a.shape) for a in small],
+        in_specs=[tile_spec, soon_spec, tile_spec, any_spec()] + [whole_spec(a.shape) for a in small],
         out_specs=[tile_spec] * 2 + [any_spec()] + [acc_spec(s) for s in sums_shapes],
         out_shape=out_shapes,
-        scratch_shapes=[pltpu.VMEM((2, frames, TILE, width), MXB), dma((2, count)), dma((count,)), dma((2,))],
+        scratch_shapes=[pltpu.VMEM(s, F32) for s in sums_shapes[:5]]
+        + [pltpu.VMEM((2, frames, TILE, width), MXB), pltpu.VMEM((frames, TILE, width), MXB)]
+        + [pltpu.VMEM((frames, stripe - soon, width), MXB)]
+        + [dma((2, count)), dma((count,)), dma((2,))]
+        + [dma((mine, count)), dma((mine, count)), dma((mine,))],
         compiler_params=params(1),
         cost_estimate=cost(10**11, 10**7),
-    )(x_patches, attn_patches, out_grad[0], *small)
+    )(x_patches, attn_patches, out_grad[0], attn_frames, *small)
     frame_spec = pl.BlockSpec((1, patches, width), lambda f: (f, 0, 0))
     log_spec = pl.BlockSpec((1, pairs, 2, patches), lambda f: (f, 0, 0, 0))
     clips = lax.axis_size("clip")
     span_rows = width // clips
     unit = 16 * (-(-span_rows // (16 * count)))
-    sum_shapes = [(width, 3 * width), (width, 9 * width), (ROWS, width)]
-    dx_patches, grad_sp, grad_ada, total = pl.pallas_call(
-        partial(spatial_backward, rows=512, block=block, part=512, count=count, clips=clips),
+    dx_patches, grad_sp, lines_of = pl.pallas_call(
+        partial(spatial_backward, rows=512, part=512, count=count, clips=clips),
         grid=(mine,),
         in_specs=[frame_spec] * 5
         + [log_spec, frame_spec, whole_spec((ROWS, width)), whole_spec((width, 3 * width))]
         + [whole_spec(a.shape) for a in (sums, t_sums, in_sums)],
-        out_specs=[any_spec()] + [acc_spec(s) for s in sum_shapes],
-        out_shape=[patch_shape] + [jax.ShapeDtypeStruct(s, F32) for s in sum_shapes],
+        out_specs=[any_spec(), acc_spec((width, 3 * width)), acc_spec((clips, ROWS, width))],
+        out_shape=[
+            patch_shape,
+            jax.ShapeDtypeStruct((width, 3 * width), MXB),
+            jax.ShapeDtypeStruct((clips, ROWS, width), F32),
+        ],
         scratch_shapes=[
+            pltpu.VMEM((width, 3 * width), F32),
             pltpu.VMEM((mine, patches, width), MXB),
             pltpu.VMEM((patches, 3 * width), MXB),
             pltpu.VMEM((pairs, 2, patches), F32),
-            pltpu.VMEM((patches, 2 * HEAD_DIM), F32),
-            pltpu.VMEM((patches, 2 * HEAD_DIM), F32),
+            pltpu.VMEM((pairs, 2 * HEAD_DIM, patches), F32),
+            pltpu.VMEM((patches, width), F32),
+            pltpu.VMEM((patches, width), F32),
+            pltpu.VMEM((pairs, 2 * HEAD_DIM, patches), MXB),
             pltpu.VMEM((2, 8, width), F32),
             pltpu.VMEM((8, 3 * width), F32),
             pltpu.VMEM((clips, span_rows, 3 * width), MXB),
@@ -1214,7 +1327,11 @@
     )(da_frames, attn_frames, queries, keys, values, logs, x_frames, modes, spatial_proj, sums, t_sums, in_sums)
     input_grad = (g1 + dx_patches.astype(F32)).astype(MXB)
     early = lax.psum((grad_so, grad_t, grad_to, grad_in, grad_out_turned), ("clip", "sp"))
-    flat = total.reshape(-1)
+    early = tuple(g.astype(F32) for g in early)
+    flat = jnp.sum(lines_of, axis=0).reshape(-1)
+    conds = lines_of[:, COND]
+    grads = lines_of[:, :9].reshape(clips, 9 * width)
+    grad_ada = sum(conds[at][:, None] * grads[at][None, :] for at in range(clips))
 
     def lines(first, rows=1):
         return flat[first * width : (first + rows) * width]
@@ -1224,7 +1341,7 @@
         input_grad[None],
         grad_ada,
         lines(0, 9),
-        grad_sp,
+        grad_sp.astype(F32),
         jnp.concatenate([lines(SP_BIAS), lines(SP_BIAS + 2)]),
         early[0],
         lines(SO_BIAS),

time: 591 us -> 528 us (0.89)
  Pallas kernels: 534 us -> 478 us
  local copies, waits for them, and re-layouts: 25.8 us -> 10.6 us
  other arithmetic: 8.2 us -> 22.9 us
    pallas_call x2, Pallas kernels: 409 us -> 346 us  [the longest x1 220 us: fast_body(): pl.pallas_call(partial(spatial_backward, rows=512, part=512, count=count,...]
    unnamed x37 -> x14, local copies, waits for them, and re-layouts: 21 us -> 5.82 us
    convert_element_type x0 -> x5, other arithmetic: none -> 9.21 us  [the longest x4 6.73 us: fast_body(): early = tuple((g.astype(F32) for g in early))]
    pallas_call x1, Pallas kernels: 125 us -> 132 us  [fast_body(): pl.pallas_call(partial(middle, peer_count=count), grid=(stripe // TILE,),...]
  transfers between devices with their start and end apart: 1 -> 1, of which waited for: 0 -> 0; matrix products, arithmetic and copies ran while one was open for 2% -> 3% of each run, Pallas kernels for 46% -> 42%
where the time goes in v4:
time: 528 us; the launch traced here: 527 us
  Pallas kernels  478 us (91%)
  other arithmetic  22.9 us (4%)
  between operations  15 us (3%)
  local copies, waits for them, and re-layouts  10.6 us (2%)
    pallas_call x1, Pallas kernels, fast_body(): pl.pallas_call(partial(spatial_backward, rows=512, part=512, count=count,...  220 us
    pallas_call x1, Pallas kernels, fast_body(): pl.pallas_call(partial(middle, peer_count=count), grid=(stripe // TILE,),...  132 us
    pallas_call x1, Pallas kernels, fast_body(): pl.pallas_call(partial(spatial_forward, block=block, part=512, count=coun...  126 us
  transfers between devices with their start and end apart: 1, of which 0 were waited for; matrix products, arithmetic and copies ran while one was open for 3% of the time, Pallas kernels for 42%

profile of v4, /device:TPU:0, one launch (start us, length us, event | category | flops | bytes accessed | tf_op | source)
XLA Modules:
  0.0 527.4 jit_solution(15380727477799181917)
XLA Ops:
  7.2 0.0 copy-start
  7.2 0.0 all-reduce.16.cloned.1.call-start
  8.1 0.7 convert_reduce_fusion
  8.8 0.1 copy-done
  9.0 1.2 convolution_reduce_fusion
  10.1 0.8 fusion.4
  10.9 0.7 add.96
  11.6 0.7 convert_add_fusion
  12.4 0.6 reshape.76.modes_ref
  13.0 126.2 %shard_map.297 = (bf16[2,2048,384]{2,1,0:T(8,128)(2,1)}, bf16[2,2048,384]{2,1,0:T(8,128)(2,1)}, bf16[2,2048,384]{2,1,0:T(8,128)(2,1)}, bf16[2,2048,384]{2,1,0:T(...) custom-call(bf16[16,256,384]{2,1,0:T(8,128)(2,1)} %bitcast.13, ...), custom_call_target="tpu_custom_call" | custom-call | flops 99999997952 | bytes 10000000 | tf_op jit(solution)/shard_map/pallas_call | solution.py:1232
  139.2 131.7 %shard_map.298 = (bf16[16,256,384]{2,1,0:T(8,128)(2,1)}, f32[16,256,384]{2,1,0:T(8,128)}, bf16[2,2048,384]{2,1,0:T(8,128)(2,1)}, bf16[384,384]{1,0:T(8,128)(2,1)...) custom-call(bf16[16,256,384]{2,1,0:T(8,128)(2,1)} %bitcast.14, ...), custom_call_target="tpu_custom_call" | custom-call | flops 99999997952 | bytes 10000000 | tf_op jit(solution)/shard_map/pallas_call | solution.py:1264
  270.9 0.0 all-reduce.16.cloned.1.call-update
  271.0 219.7 %shard_map.299 = (bf16[16,256,384]{2,1,0:T(8,128)(2,1)}, bf16[384,1152]{1,0:T(8,128)(2,1)}, f32[4,24,384]{2,1,0:T(8,128)}) custom-call(bf16[2,2048,384]{2,1,0:T(8,128)(2,1)} %get-tuple-element.41.da_ref, bf16[2,2048,384]{2,1,0:T(8,128)(2,1)} %get-tuple-element.38.attn_hbm.attn_ref, bf16[2,2048,384]{2,1,0:T(8,128)(2,1)} %get-tuple-element.42.q_ref, ...), custom_call_target="tpu_custom_call" | custom-call | flops 199999995904 | bytes 10000000 | tf_op jit(solution)/shard_map/pallas_call | solution.py:1283
  490.7 0.0 copy-start.3
  490.7 1.1 reduce_sum.9
  491.8 0.8 fusion.3
  492.6 0.6 slice_reduce_fusion
  493.2 0.6 slice.135
  493.8 0.6 slice.121
  494.4 2.5 convert_element_type.63
  496.9 0.6 pad_maximum_fusion.1
  497.5 0.6 pad_maximum_fusion
  498.1 0.8 slice_reduce_fusion.10
  498.9 5.2 fusion
  504.1 4.0 multiply_add_fusion
  508.1 1.9 convert_element_type.64
  510.0 1.8 convert_element_type.66
  511.8 2.8 copy.35
  514.6 1.3 convert_element_type.65
  515.9 1.7 convert_element_type.67
  517.6 1.7 copy.43
  519.3 1.2 copy-done.1
  (17 shorter events, 0.0 us)
Async XLA Ops:
  7.2 1.8 copy-start
  7.2 500.9 %all-reduce.16.cloned.1.call-start = ((), (), s32[]{:S(2)}) async-start(), calls=%async_computation | async-start | bytes 7667712 | tf_op jit(solution)/shard_map/psum | solution.py:1329
  490.7 8.2 %copy-start.3 = (bf16[16,256,384]{2,1,0:T(8,128)(2,1)S(1)}, bf16[16,256,384]{2,1,0:T(8,128)(2,1)}, u32[]{:S(2)}) copy-start(bf16[16,256,384]{2,1,0:T(8,128)(2,1)} %get-tuple-element.50) | copy-start | bytes 9437188
  508.1 6.5 %copy-start.5 = (bf16[384,1152]{1,0:T(8,128)(2,1)S(1)}, bf16[384,1152]{1,0:T(8,128)(2,1)}, u32[]{:S(2)}) copy-start(bf16[384,1152]{1,0:T(8,128)(2,1)} %get-tuple-element.103) | copy-start | bytes 2654212
  511.8 4.1 copy-start.4
  514.6 3.0 copy-start.2
  517.6 2.9 copy-start.1
Sparse Core Ops, SparseCore 0:
  271.1 192.5 all-reduce.15

commit v5 on v4

--- a/solution.py
+++ b/solution.py
@@ -663,11 +663,13 @@
 
 def spatial_backward(
     da_ref, attn_ref, q_ref, k_ref, v_ref, log_ref, x_ref, modes_ref, proj_ref, mid_sums_ref, t_sums_ref, in_sums_ref,
-    patches_out, proj_out, row_out,
+    stack_hbm, patches_out, stack_out, proj_out, row_out,
     grad_proj_ref, dx_ref, mix_ref, delta_ref, dq_ref, dk_ref, dv_ref, across_ref, sums_ref, bias_sums_ref,
     clip_out_ref, clip_in_ref, unit_out_ref, unit_in_ref, piece_ref, all_ref, vec_ref, vec_in_ref, row_ref, row_in_ref,
+    early_in_ref, early_out_ref, early_unit_ref, early_piece_ref,
     send_sem, recv_sem, own_sem, g1_send, g1_recv, g2_send, g2_recv, g3_send, g3_recv, g4_send, g4_recv,
-    v1_send, v1_recv, v2_send, v2_recv, rows, part, count, clips,
+    v1_send, v1_recv, v2_send, v2_recv, e1_send, e1_recv, e2_send, e2_recv, e3_send, e3_recv, e4_send, e4_recv, e_own,
+    rows, part, count, clips,
 ):
     tokens, width = x_ref.shape[1:]
     mine = dx_ref.shape[0]
@@ -694,6 +696,98 @@
     def g4_copy(peer, slot):
         return send(piece_ref, all_ref.at[slot], g4_send.at[peer], g4_recv.at[slot], peer, "clip")
 
+    def clip_rows(each):
+        return pl.ds(pl.multiple_of(each * span_rows, span_rows), span_rows)
+
+    def unit_rows(each):
+        return pl.ds(pl.multiple_of(each * unit, unit), unit)
+
+    def e1_copy(peer, slot):
+        return send(
+            stack_hbm.at[:, clip_rows(peer), :], early_in_ref.at[slot], e1_send.at[peer], e1_recv.at[slot], peer, "clip"
+        )
+
+    def e1_keep():
+        return pltpu.make_async_copy(stack_hbm.at[:, clip_rows(clip), :], early_in_ref.at[clip], e_own.at[0])
+
+    def e2_copy(peer, slot):
+        return send(early_out_ref.at[peer], early_unit_ref.at[slot], e2_send.at[peer], e2_recv.at[slot], peer)
+
+    def e3_copy(peer, slot):
+        here = early_piece_ref.at[:, unit_rows(slot), :]
+        return send(here, here, e3_send.at[peer], e3_recv.at[slot], peer)
+
+    def e4_copy(peer, slot):
+        return send(
+            early_piece_ref, stack_out.at[:, clip_rows(slot), :], e4_send.at[peer], e4_recv.at[slot], peer, "clip"
+        )
+
+    def e4_keep():
+        return pltpu.make_async_copy(early_piece_ref, stack_out.at[:, clip_rows(clip), :], e_own.at[1])
+
+    def early_one():
+        e1_keep().start()
+        for _, peer, _ in clip_peers:
+            e1_copy(peer, clip).start()
+
+    def early_two():
+        e1_keep().wait()
+        for _, _, source in clip_peers:
+            e1_copy(source, source).wait_recv()
+
+        def add_up(owner, carry):
+            total = early_in_ref[0, :, unit_rows(owner), :].astype(F32)
+            for each in range(1, clips):
+                total = total + early_in_ref[each, :, unit_rows(owner), :].astype(F32)
+            early_out_ref[owner] = total.astype(MXB)
+
+            @pl.when(owner != me)
+            def _():
+                e2_copy(owner, me).start()
+
+            return carry
+
+        lax.fori_loop(0, owners, add_up, 0)
+
+    def early_three():
+        @pl.when(me < owners)
+        def _():
+            total = early_out_ref[me].astype(F32)
+            for _, _, source in peers:
+                e2_copy(me, source).wait_recv()
+                total = total + early_unit_ref[source].astype(F32)
+            early_piece_ref[:, unit_rows(me), :] = total.astype(MXB)
+            for _, peer, _ in peers:
+                e3_copy(peer, me).start()
+
+    def early_four():
+        for owner in range(owners):
+
+            @pl.when(owner != me)
+            def _():
+                e3_copy(owner, owner).wait_recv()
+
+        e4_keep().start()
+        for _, peer, _ in clip_peers:
+            e4_copy(peer, clip).start()
+
+    def early_end():
+        e4_keep().wait()
+        for _, peer, source in clip_peers:
+            e4_copy(source, source).wait_recv()
+            e1_copy(peer, clip).wait_send()
+            e4_copy(peer, clip).wait_send()
+        for owner in range(owners):
+
+            @pl.when(owner != me)
+            def _():
+                e2_copy(owner, me).wait_send()
+
+        @pl.when(me < owners)
+        def _():
+            for _, peer, _ in peers:
+                e3_copy(peer, me).wait_send()
+
     def v1_copy(peer, slot):
         return send(vec_ref, vec_in_ref.at[slot], v1_send.at[peer], v1_recv.at[slot], peer)
 
@@ -760,6 +854,7 @@
     @pl.when(frame == 0)
     def _():
         greeted(peers + clip_peers)
+        early_one()
 
     half = tokens // 2
     near = half // stripe
@@ -777,6 +872,15 @@
         def step_pass(index, carry):
             pair = lax.rem(index, pairs)
             step = lax.div(index, pairs) + 3 * phase
+
+            @pl.when((frame == 0) & (phase == 0) & (index == 2 * pairs))
+            def _():
+                early_two()
+
+            @pl.when(last & (phase == 0) & (index == 2 * pairs))
+            def _():
+                early_four()
+
             lanes = pl.ds(pl.multiple_of(pair * 2 * HEAD_DIM, 2 * HEAD_DIM), 2 * HEAD_DIM)
             query_first = jnp.where(step >= 2, near_first, far_first)
             key_first = jnp.where(lax.rem(step, 2) == 1, near_first, far_first)
@@ -852,6 +956,12 @@
             return carry
 
         lax.fori_loop(0, near, finish, 0)
+        stage = 2 * frame + phase
+
+        @pl.when(stage == 1)
+        def _():
+            early_three()
+
         return carry
 
     lax.fori_loop(0, 2, phase_pass, 0)
@@ -940,6 +1050,7 @@
             for _, peer, _ in peers:
                 g3_copy(peer, me).wait_send()
 
+        early_end()
         for each in range(mine):
             dx_keep(each).wait()
             for _, peer, _ in peers:
@@ -950,7 +1061,7 @@
 def middle(
     x_ref, soon_ref, og_ref, attn_hbm, modes_ref, so_ref, t_ref, to_ref, in_ref, out_ref,
     block_ref, g1_ref, da_out,
-    so_out, t_out, to_out, in_out, out_out, sums_ref, t_sums_ref, in_sums_ref,
+    stack_out, sums_ref, t_sums_ref, in_sums_ref,
     grad_so_ref, grad_t_ref, grad_to_ref, grad_in_ref, grad_out_ref,
     da_ref, attn_ref, late_ref, send_sem, recv_sem, own_sem, late_send, late_recv, late_own, peer_count,
 ):
@@ -1164,11 +1275,12 @@
             da_landed(step, source).wait_recv()
             for frame in range(mine):
                 late_copy(frame, step, peer).wait_send()
-        so_out[...] = grad_so_ref[...].astype(MXB)
-        t_out[...] = grad_t_ref[...].astype(MXB)
-        to_out[...] = grad_to_ref[...].astype(MXB)
-        in_out[...] = grad_in_ref[...].astype(MXB)
-        out_out[...] = grad_out_ref[...].astype(MXB)
+        place = 0
+        for ref in (grad_so_ref, grad_t_ref, grad_to_ref, grad_in_ref, grad_out_ref):
+            for first in range(0, ref.shape[1], width):
+                square = ref[:, first : first + width]
+                stack_out[place] = (square.T if ref is grad_out_ref else square).astype(MXB)
+                place += 1
 
 
 def whole_spec(shape):
@@ -1250,24 +1362,24 @@
     tile_spec = pl.BlockSpec((frames, TILE, width), lambda i: (0, i, 0))
     soon_spec = pl.BlockSpec((frames, TILE, width), lambda i: (0, jnp.minimum(i, soon // TILE - 1), 0))
     small = (modes, spatial_out, temporal_proj, temporal_out, hidden_in, hidden_out)
-    sums_shapes = [
-        (width, width), (width, 3 * width), (width, width), (width, hidden), (width, hidden),
-        (12, 8, width), (8, 3 * width), (8, hidden),
-    ]
+    folds = hidden // width
+    squares = 5 + 2 * folds
+    held_shapes = [(width, width), (width, 3 * width), (width, width), (width, hidden), (width, hidden)]
+    sums_shapes = [(squares, width, width), (12, 8, width), (8, 3 * width), (8, hidden)]
     out_shapes = [
         patch_shape,
         jax.ShapeDtypeStruct((frames, stripe, width), F32),
         frame_shape,
-    ] + [jax.ShapeDtypeStruct(s, MXB if at < 5 else F32) for at, s in enumerate(sums_shapes)]
+    ] + [jax.ShapeDtypeStruct(s, MXB if at < 1 else F32) for at, s in enumerate(sums_shapes)]
     (
-        block_out, g1, da_frames, grad_so, grad_t, grad_to, grad_in, grad_out_turned, sums, t_sums, in_sums,
+        block_out, g1, da_frames, stack, sums, t_sums, in_sums,
     ) = pl.pallas_call(
         partial(middle, peer_count=count),
         grid=(stripe // TILE,),
         in_specs=[tile_spec, soon_spec, tile_spec, any_spec()] + [whole_spec(a.shape) for a in small],
         out_specs=[tile_spec] * 2 + [any_spec()] + [acc_spec(s) for s in sums_shapes],
         out_shape=out_shapes,
-        scratch_shapes=[pltpu.VMEM(s, F32) for s in sums_shapes[:5]]
+        scratch_shapes=[pltpu.VMEM(s, F32) for s in held_shapes]
         + [pltpu.VMEM((2, frames, TILE, width), MXB), pltpu.VMEM((frames, TILE, width), MXB)]
         + [pltpu.VMEM((frames, stripe - soon, width), MXB)]
         + [dma((2, count)), dma((count,)), dma((2,))]
@@ -1280,15 +1392,17 @@
     clips = lax.axis_size("clip")
     span_rows = width // clips
     unit = 16 * (-(-span_rows // (16 * count)))
-    dx_patches, grad_sp, lines_of = pl.pallas_call(
+    dx_patches, early, grad_sp, lines_of = pl.pallas_call(
         partial(spatial_backward, rows=512, part=512, count=count, clips=clips),
         grid=(mine,),
         in_specs=[frame_spec] * 5
         + [log_spec, frame_spec, whole_spec((ROWS, width)), whole_spec((width, 3 * width))]
-        + [whole_spec(a.shape) for a in (sums, t_sums, in_sums)],
-        out_specs=[any_spec(), acc_spec((width, 3 * width)), acc_spec((clips, ROWS, width))],
+        + [whole_spec(a.shape) for a in (sums, t_sums, in_sums)]
+        + [any_spec()],
+        out_specs=[any_spec(), any_spec(), acc_spec((width, 3 * width)), acc_spec((clips, ROWS, width))],
         out_shape=[
             patch_shape,
+            jax.ShapeDtypeStruct((squares, width, width), MXB),
             jax.ShapeDtypeStruct((width, 3 * width), MXB),
             jax.ShapeDtypeStruct((clips, ROWS, width), F32),
         ],
@@ -1313,6 +1427,10 @@
             pltpu.VMEM((count, ROWS, width), F32),
             pltpu.VMEM((ROWS, width), F32),
             pltpu.VMEM((clips, ROWS, width), F32),
+            pltpu.VMEM((clips, squares, span_rows, width), MXB),
+            pltpu.VMEM((count, squares, unit, width), MXB),
+            pltpu.VMEM((count, squares, unit, width), MXB),
+            pltpu.VMEM((squares, span_rows, width), MXB),
             dma((mine, count)),
             dma((mine, count)),
             dma((mine,)),
@@ -1321,13 +1439,19 @@
         + [dma((count,))] * 4
         + [dma((clips,))] * 2
         + [dma((count,))] * 2
-        + [dma((clips,))] * 2,
+        + [dma((clips,))] * 2
+        + [dma((clips,))] * 2
+        + [dma((count,))] * 4
+        + [dma((clips,))] * 2
+        + [dma((2,))],
         compiler_params=params(2),
         cost_estimate=cost(2 * 10**11, 10**7),
-    )(da_frames, attn_frames, queries, keys, values, logs, x_frames, modes, spatial_proj, sums, t_sums, in_sums)
+    )(da_frames, attn_frames, queries, keys, values, logs, x_frames, modes, spatial_proj, sums, t_sums, in_sums, stack)
     input_grad = (g1 + dx_patches.astype(F32)).astype(MXB)
-    early = lax.psum((grad_so, grad_t, grad_to, grad_in, grad_out_turned), ("clip", "sp"))
-    early = tuple(g.astype(F32) for g in early)
+
+    def columns(first, number):
+        return jnp.concatenate([early[first + at].astype(F32) for at in range(number)], axis=1)
+
     flat = jnp.sum(lines_of, axis=0).reshape(-1)
     conds = lines_of[:, COND]
     grads = lines_of[:, :9].reshape(clips, 9 * width)
@@ -1343,22 +1467,25 @@
         lines(0, 9),
         grad_sp.astype(F32),
         jnp.concatenate([lines(SP_BIAS), lines(SP_BIAS + 2)]),
-        early[0],
+        columns(0, 1),
         lines(SO_BIAS),
-        early[1],
+        columns(1, 3),
         jnp.concatenate([lines(T_BIAS), lines(T_BIAS + 2)]),
-        early[2],
+        columns(4, 1),
         lines(TO_BIAS),
-        early[3],
+        columns(5, folds),
         lines(IN_BIAS, hidden // width),
-        early[4].T,
+        early[5 + folds :].astype(F32).reshape(hidden, width),
         lines(OUT_BIAS),
     )
 
 
 def chosen(tokens, *others):
-    _, frames, stripe, _ = tokens.shape
-    if tokens.shape[0] == 1 and frames % lax.axis_size("sp") == 0 and stripe % TILE == 0:
+    clips_here, frames, stripe, width = tokens.shape
+    count, clips = lax.axis_size("sp"), lax.axis_size("clip")
+    fits = clips_here == 1 and count % 2 == 0 and frames % count == 0 and frames >= 2 * count
+    fits = fits and stripe % (2 * TILE) == 0 and width % (16 * clips) == 0 and width <= 16 * clips * count
+    if fits:
         return fast_body(tokens, *others)
     return body(tokens, *others)
 

time: 528 us -> 510 us (0.966)
  between operations: 15 us -> 1.66 us
  transfers between devices with their start and end apart: 1 -> 0, of which waited for: 0 -> 0; matrix products, arithmetic and copies ran while one was open for 3% -> 0% of each run, Pallas kernels for 42% -> 0%
where the time goes in v5:
time: 510 us; the launch traced here: 509 us
  Pallas kernels  475 us (93%)
  other arithmetic  22.5 us (4%)
  local copies, waits for them, and re-layouts  8.9 us (2%)
    pallas_call x1, Pallas kernels, fast_body(): pl.pallas_call(partial(spatial_backward, rows=512, part=512, count=count,...  217 us
    pallas_call x1, Pallas kernels, fast_body(): pl.pallas_call(partial(middle, peer_count=count), grid=(stripe // TILE,),...  132 us
    pallas_call x1, Pallas kernels, fast_body(): pl.pallas_call(partial(spatial_forward, block=block, part=512, count=coun...  126 us

profile of v5, /device:TPU:0, one launch (start us, length us, event | category | flops | bytes accessed | tf_op | source)
XLA Modules:
  0.0 509.0 jit_solution(16802122103072018387)
XLA Ops:
  0.6 0.0 copy-start
  1.6 0.8 fusion.4
  2.3 0.1 copy-done
  2.4 1.2 convolution_reduce_fusion
  3.6 0.7 add.86
  4.3 0.7 convert_reduce_fusion
  5.0 0.8 convert_add_fusion
  5.8 0.6 reshape.100.modes_ref
  6.4 126.2 %shard_map.297 = (bf16[2,2048,384]{2,1,0:T(8,128)(2,1)}, bf16[2,2048,384]{2,1,0:T(8,128)(2,1)}, bf16[2,2048,384]{2,1,0:T(8,128)(2,1)}, bf16[2,2048,384]{2,1,0:T(...) custom-call(bf16[16,256,384]{2,1,0:T(8,128)(2,1)} %bitcast.34, ...), custom_call_target="tpu_custom_call" | custom-call | flops 99999997952 | bytes 10000000 | tf_op jit(solution)/shard_map/pallas_call | solution.py:1344
  132.6 131.9 %shard_map.298 = (bf16[16,256,384]{2,1,0:T(8,128)(2,1)}, f32[16,256,384]{2,1,0:T(8,128)}, bf16[2,2048,384]{2,1,0:T(8,128)(2,1)}, bf16[13,384,384]{2,1,0:T(8,128)...) custom-call(bf16[16,256,384]{2,1,0:T(8,128)(2,1)} %bitcast.35, ...), custom_call_target="tpu_custom_call" | custom-call | flops 99999997952 | bytes 10000000 | tf_op jit(solution)/shard_map/pallas_call | solution.py:1376
  264.6 216.6 %shard_map.299 = (bf16[16,256,384]{2,1,0:T(8,128)(2,1)}, bf16[13,384,384]{2,1,0:T(8,128)(2,1)}, bf16[384,1152]{1,0:T(8,128)(2,1)}, f32[4,24,384]{2,1,0:T(8,128)}) custom-call(bf16[2,2048,384]{2,1,0:T(8,128)(2,1)} %get-tuple-element.38.da_ref, bf16[2,2048,384]{2,1,0:T(8,128)(2,1)} %get-tuple-element.35.attn_hbm.attn_ref, ...), custom_call_target="tpu_custom_call" | custom-call | flops 199999995904 | bytes 10000000 | tf_op jit(solution)/shard_map/pallas_call | solution.py:1395
  481.2 0.0 copy-start.3
  481.2 6.2 %fusion = bf16[1,16,256,384]{3,2,1,0:T(8,128)(2,1)} fusion(f32[16,256,384]{2,1,0:T(8,128)} %get-tuple-element.37, bf16[16,256,384]{2,1,0:T(8,128)(2,1)} %get-tuple-element.48), kind=kLoop, calls=%fused_computation.2 | loop fusion | flops 4718592 | bytes 12582912 | tf_op jit(solution)/shard_map/broadcast_in_dim | solution.py:1465
  487.4 0.0 copy-start.2
  487.4 0.0 copy-done.3
  487.5 4.0 multiply_add_fusion
  491.5 0.6 slice.151
  492.1 0.0 copy-done.2
  492.1 1.3 convert_element_type.91
  493.4 0.6 slice_reduce_fusion
  494.0 0.6 pad_maximum_fusion
  494.6 3.0 slice_bitcast_fusion.3
  497.6 1.3 maximum_convert_fusion.1
  498.9 0.6 pad_maximum_fusion.1
  499.5 1.7 maximum_convert_fusion
  501.2 0.6 slice.174
  501.8 1.4 slice.175
  503.2 1.7 bitcast_convert_fusion
  504.9 0.0 copy-start.1
  504.9 4.1 copy.36
  509.0 0.0 copy-done.1
  (11 shorter events, 0.1 us)
Async XLA Ops:
  0.6 1.8 copy-start
  481.2 6.2 %copy-start.3 = (f32[4,24,384]{2,1,0:T(8,128)S(1)}, f32[4,24,384]{2,1,0:T(8,128)}, u32[]{:S(2)}) copy-start(f32[4,24,384]{2,1,0:T(8,128)} %get-tuple-element.49) | copy-start | bytes 442372
  487.4 4.7 copy-start.2
  504.9 4.1 copy-start.1
